TPU v7x, 32 devices: a whole 2x2x4 slice. The times are simulated.
32 devices in a mesh: row: 4 (over x, core), col: 2 (over y), exp: 4 (over z).
Axes of the slice: x: 2, y: 2, z: 4, core: 2. Of those that a mesh axis runs over, the one named last changes fastest.
Arguments:
- layer_input: bfloat16 [5120, 2048], P(('row', 'exp'), 'col'), may hold values from -6 to 6
- lengths: int32 [4, 3], P('exp'), may hold values from 1 to 1024, 1280 in all within a row
- routes: int32 [2, 2560, 6], P('col', ('row', 'exp')), may hold values from 0 to 15, all different within a row; in each aligned block of 160 rows (0 to 159, 160 to 319, ..., all dimensions but the last counted through in order) at most 90 rows name the same one
- norm1_gain: float32 [2048], replicated, may hold values from 0.5 to 1.5
- w_query: bfloat16 [2048, 3072], P('col', 'row'), may hold values from -0.125 to 0.125
- w_latent: bfloat16 [2, 1024, 576], P('col', 'row'), may hold values from -0.125 to 0.125
- latent_gain: float32 [512], replicated, may hold values from 0.5 to 1.5
- w_kv: bfloat16 [512, 4096], P(None, ('row', 'col')), may hold values from -0.25 to 0.25
- w_out: bfloat16 [2048, 2048], P('row', 'col'), may hold values from -2 to 2
- norm2_gain: float32 [2048], replicated, may hold values from 0.5 to 1.5
- shared_gate: bfloat16 [2048, 2816], P('col', 'row'), may hold values from -0.125 to 0.125
- shared_up: bfloat16 [2048, 2816], P('col', 'row'), may hold values from -0.125 to 0.125
- shared_down: bfloat16 [2816, 2048], P('row', 'col'), may hold values from -0.21875 to 0.21875
- router: bfloat16 [2048, 16], replicated, may hold values from -0.0625 to 0.0625
- expert_gate: bfloat16 [16, 2048, 1408], P(('row', 'exp'), None, 'col'), may hold values from -0.125 to 0.125
- expert_up: bfloat16 [16, 2048, 1408], P(('row', 'exp'), None, 'col'), may hold values from -0.125 to 0.125
- expert_down: bfloat16 [16, 2048, 1408], P(('row', 'exp'), None, 'col'), may hold values from -0.4375 to 0.4375
- cotangent: bfloat16 [5120, 2048], P(('row', 'exp'), 'col'), may hold values from -6 to 6
Outputs:
- layer_output: bfloat16 [5120, 2048], P(('row', 'exp'), 'col')
- input_grad: float32 [5120, 2048], P(('row', 'exp'), 'col')
- norm1_gain_grad: float32 [2048], replicated
- w_query_grad: float32 [2048, 3072], P('col', 'row')
- w_latent_grad: float32 [2, 1024, 576], P('col', 'row')
- latent_gain_grad: float32 [512], replicated
- w_kv_grad: float32 [512, 4096], P(None, ('row', 'col'))
- w_out_grad: float32 [2048, 2048], P('row', 'col')
- norm2_gain_grad: float32 [2048], replicated
- shared_gate_grad: float32 [2048, 2816], P('col', 'row')
- shared_up_grad: float32 [2048, 2816], P('col', 'row')
- shared_down_grad: float32 [2816, 2048], P('row', 'col')
- router_grad: float32 [2048, 16], replicated
- expert_gate_grad: float32 [16, 2048, 1408], P(('row', 'exp'), None, 'col')
- expert_up_grad: float32 [16, 2048, 1408], P(('row', 'exp'), None, 'col')
- expert_down_grad: float32 [16, 2048, 1408], P(('row', 'exp'), None, 'col')
Inputs may be any that keep to these rules, and one draw needn't show every extreme that they name: `routes`: each row of a token names 6 different experts. In the rows of one device (aligned blocks of 160 rows of the second dimension, for each first index) no expert is named more than 90 times, a bound that some block reaches. `lengths`: each row sums to 1280, and its largest entry is exactly 1024.
All inputs are finite; a program needn't handle non-finite values.
Results may differ from a plain program's by a relative error of at most 0.02.
Values may be sent and summed in bfloat16 or wider, within the bound.
A program may use at most 320 MiB of HBM per device.

v0:
```python
import math

import jax
import jax.numpy as jnp
from jax import lax
from jax.sharding import PartitionSpec as P

QK_NOPE = 128
ROPE = 64
KV_RANK = 512
V_DIM = 128


epsilon = 1e-06
theta_base = 10000.0


def as_sent(x):
    return jax.tree.map(lambda a: a.astype(jnp.bfloat16) if a.dtype == jnp.float32 else a, x)


def col_total(value):
    return lax.psum(value, "col")


def gather_rows(value):
    return lax.all_gather(value, "row", axis=0, tiled=True)


def sum_cols(value):
    return lax.psum_scatter(value, "col", scatter_dimension=1, tiled=True)


def gather_cols(value):
    return jax.tree.map(
        lambda part, own: part.astype(own.dtype),
        lax.all_gather(as_sent(value), "col", axis=1, tiled=True),
        value,
    )


def sum_rows(value):
    return lax.psum_scatter(value, "row", scatter_dimension=0, tiled=True)


def latent_total(value):
    return lax.psum(value, ("row", "col"))


def to_tokens(value):
    return lax.all_to_all(value, "col", split_axis=0, concat_axis=1, tiled=True)


def to_features(value):
    return lax.all_to_all(
        value.astype(jnp.bfloat16), "col", split_axis=1, concat_axis=0, tiled=True
    ).astype(value.dtype)


def expert_swap(value):
    return lax.all_to_all(value, ("row", "exp"), split_axis=0, concat_axis=0, tiled=True)


def expert_rows(value):
    return lax.all_gather(value, "col", axis=0, tiled=True)


def expert_sums(value):
    return lax.psum_scatter(
        value.astype(jnp.bfloat16), "col", scatter_dimension=0, tiled=True
    ).astype(jnp.float32)


def dot_nt(left, right):
    return lax.dot_general(
        left, right, (((1,), (1,)), ((), ())), preferred_element_type=jnp.float32
    )


def dot_tn(left, right):
    return lax.dot_general(
        left, right, (((0,), (0,)), ((), ())), preferred_element_type=jnp.float32
    )


def rotate(value, cosine, sine):
    half = value.shape[-1] // 2
    first, second = (value[..., :half], value[..., half:])
    return jnp.concatenate(
        [first * cosine - second * sine, first * sine + second * cosine], axis=-1
    )


def unrotate(value, cosine, sine):
    half = value.shape[-1] // 2
    first, second = (value[..., :half], value[..., half:])
    return jnp.concatenate(
        [first * cosine + second * sine, second * cosine - first * sine], axis=-1
    )


def sequence_layout(lengths_row, group):
    ends = jnp.cumsum(lengths_row)
    starts = ends - lengths_row
    index = jnp.arange(group, dtype=jnp.int32)
    seq_ids = jnp.sum((index[:, None] >= ends[None, :]).astype(jnp.int32), axis=1)
    member = seq_ids[:, None] == jnp.arange(lengths_row.shape[0], dtype=jnp.int32)[None, :]
    begins = jnp.sum(jnp.where(member, starts[None, :], 0), axis=1)
    return (seq_ids, index - begins)


def rotary_tables(places):
    half = ROPE // 2
    freqs = jnp.power(theta_base, -jnp.arange(half, dtype=jnp.float32) * (2.0 / ROPE))
    angle = places.astype(jnp.float32)[..., None] * freqs
    return (jnp.cos(angle), jnp.sin(angle))


def norm_rows(value, gain, width):
    square = col_total(jnp.sum(value * value, axis=1))
    factor = lax.rsqrt(square / width + epsilon)
    return (value * factor[:, None] * gain, factor)


def norm_back(value, factor, gain, grad, width):
    weighted = grad * gain
    inner = col_total(jnp.sum(weighted * value, axis=1))
    d_value = (
        factor[:, None] * weighted - value * (factor * factor * factor * inner / width)[:, None]
    )
    d_gain = jnp.sum(grad * value * factor[:, None], axis=0)
    return (d_value, d_gain)


def masked_scores(query_block, keys, seq_ids, first, scale):
    size = query_block.shape[0]
    group = keys.shape[0]
    scored = (
        jnp.einsum("qhd,khd->hqk", query_block, keys, preferred_element_type=jnp.float32) * scale
    )
    query_index = first + jnp.arange(size, dtype=jnp.int32)
    key_index = jnp.arange(group, dtype=jnp.int32)
    allowed = (seq_ids[first : first + size][:, None] == seq_ids[None, :]) & (
        key_index[None, :] <= query_index[:, None]
    )
    return jnp.where(allowed[None, :, :], scored, -1e30)


def expert_forward(inputs, gate_weight, up_weight, down_weight):
    gate_pre = jnp.dot(inputs, gate_weight, preferred_element_type=jnp.float32)
    up_pre = jnp.dot(inputs, up_weight, preferred_element_type=jnp.float32)
    expert_hidden = (jax.nn.silu(gate_pre) * up_pre).astype(jnp.bfloat16)
    return (dot_nt(expert_hidden, down_weight), gate_pre, up_pre, expert_hidden)


def expert_backward(
    inputs, gate_pre, up_pre, expert_hidden, d_result, gate_weight, up_weight, down_weight
):
    d_hidden = jnp.dot(d_result, down_weight, preferred_element_type=jnp.float32)
    grad_down = dot_tn(d_result, expert_hidden)
    sigmoid_gate = jax.nn.sigmoid(gate_pre)
    d_up = (d_hidden * gate_pre * sigmoid_gate).astype(jnp.bfloat16)
    d_gate = (d_hidden * up_pre * sigmoid_gate * (1.0 + gate_pre * (1.0 - sigmoid_gate))).astype(
        jnp.bfloat16
    )
    grad_gate = dot_tn(inputs, d_gate)
    grad_up = dot_tn(inputs, d_up)
    d_inputs = dot_nt(d_gate, gate_weight) + dot_nt(d_up, up_weight)
    return (d_inputs, grad_gate, grad_up, grad_down)


def per_device(
    layer_input,
    lengths,
    routes,
    norm1_gain,
    w_query,
    w_latent,
    latent_gain,
    w_kv,
    w_out,
    norm2_gain,
    shared_gate,
    shared_up,
    shared_down,
    router,
    expert_gate,
    expert_up,
    expert_down,
    cotangent,
):
    row_id = lax.axis_index("row")
    col_id = lax.axis_index("col")
    experts = lax.axis_size("row") * lax.axis_size("exp")
    tok_dev = routes.shape[1]
    topk_count = routes.shape[2]
    capacity = max(2, 3 * tok_dev * topk_count // (2 * experts))
    half_width = layer_input.shape[1]
    width = half_width * lax.axis_size("col")
    group = layer_input.shape[0] * lax.axis_size("row")
    heads_here = w_kv.shape[1] // (QK_NOPE + V_DIM)
    head_dim = QK_NOPE + ROPE
    scale = 1.0 / math.sqrt(head_dim)
    query_rows = group // 2
    seq_ids, places = sequence_layout(lengths[0], group)
    cosine, sine = rotary_tables(places)
    input_wide = layer_input.astype(jnp.float32)
    gain_one = lax.dynamic_slice_in_dim(norm1_gain, col_id * half_width, half_width)
    normed_one, factor_one = norm_rows(input_wide, gain_one, width)
    gathered = gather_rows(normed_one.astype(jnp.bfloat16))
    query_pre = sum_cols(jnp.dot(gathered, w_query, preferred_element_type=jnp.float32)).reshape(
        group, heads_here, head_dim
    )
    queries = jnp.concatenate(
        [
            query_pre[..., :QK_NOPE],
            rotate(query_pre[..., QK_NOPE:], cosine[:, None, :], sine[:, None, :]),
        ],
        axis=2,
    ).astype(jnp.bfloat16)
    slab = w_latent.shape[1]
    sub_cols = lax.dynamic_slice_in_dim(gathered, row_id * slab, slab, 1)
    latent = latent_total(jnp.dot(sub_cols, w_latent[0], preferred_element_type=jnp.float32))
    compressed_raw = latent[:, :KV_RANK]
    kv_factor = lax.rsqrt(jnp.mean(compressed_raw * compressed_raw, axis=1) + epsilon)
    compressed = (compressed_raw * kv_factor[:, None] * latent_gain).astype(jnp.bfloat16)
    rotary_key = rotate(latent[:, KV_RANK:], cosine, sine).astype(jnp.bfloat16)
    key_value = (
        jnp.dot(compressed, w_kv, preferred_element_type=jnp.float32)
        .astype(jnp.bfloat16)
        .reshape(group, heads_here, QK_NOPE + V_DIM)
    )
    keys = jnp.concatenate(
        [
            key_value[..., :QK_NOPE],
            jnp.broadcast_to(rotary_key[:, None, :], (group, heads_here, ROPE)),
        ],
        axis=2,
    )
    values = key_value[..., QK_NOPE:]
    block_outputs = []
    block_totals = []
    for first in range(0, group, query_rows):
        scores = masked_scores(queries[first : first + query_rows], keys, seq_ids, first, scale)
        highest = jnp.max(scores, axis=2, keepdims=True)
        log_total = highest + jnp.log(jnp.sum(jnp.exp(scores - highest), axis=2, keepdims=True))
        probs_low = jnp.exp(scores - log_total).astype(jnp.bfloat16)
        block_outputs.append(
            jnp.einsum(
                "hqk,khd->qhd", probs_low, values, preferred_element_type=jnp.float32
            ).astype(jnp.bfloat16)
        )
        block_totals.append(log_total)
    attended = jnp.concatenate(block_outputs, axis=0).reshape(group, heads_here * V_DIM)
    attended_all = gather_cols(attended)
    hidden_state = input_wide + sum_rows(
        jnp.dot(attended_all, w_out, preferred_element_type=jnp.float32)
    )
    gain_two = lax.dynamic_slice_in_dim(norm2_gain, col_id * half_width, half_width)
    normed_two, factor_two = norm_rows(hidden_state, gain_two, width)
    second_low = normed_two.astype(jnp.bfloat16)
    second_rows = gather_rows(second_low)
    shared_gate_pre, shared_up_pre = sum_cols(
        (
            jnp.dot(second_rows, shared_gate, preferred_element_type=jnp.float32),
            jnp.dot(second_rows, shared_up, preferred_element_type=jnp.float32),
        )
    )
    shared_hidden = (jax.nn.silu(shared_gate_pre) * shared_up_pre).astype(jnp.bfloat16)
    shared_all = gather_cols(shared_hidden)
    shared_result = sum_rows(jnp.dot(shared_all, shared_down, preferred_element_type=jnp.float32))
    token_rows = to_tokens(second_low)
    model_width = token_rows.shape[1]
    router_probs = jax.nn.softmax(
        jnp.dot(token_rows, router, preferred_element_type=jnp.float32), axis=1
    )
    chosen = routes[0]
    picks = chosen[:, :, None] == jnp.arange(experts, dtype=jnp.int32)[None, None, :]
    selected = jnp.sum(jnp.where(picks, router_probs[:, None, :], 0.0), axis=2)
    selected_total = jnp.sum(selected, axis=1, keepdims=True)
    gates = selected / selected_total
    flat_ids = chosen.reshape(-1)
    pair_count = flat_ids.shape[0]
    onehot_int = (flat_ids[:, None] == jnp.arange(experts, dtype=jnp.int32)[None, :]).astype(
        jnp.int32
    )
    earlier = jnp.cumsum(onehot_int, axis=0) - onehot_int
    slot_index = flat_ids * capacity + jnp.sum(earlier * onehot_int, axis=1)
    pair_of_slot = (
        jnp.zeros((experts * capacity,), jnp.int32)
        .at[slot_index]
        .set(jnp.arange(pair_count, dtype=jnp.int32))
    )
    slot_used = jnp.zeros((experts * capacity,), jnp.bool_).at[slot_index].set(True)
    send = jnp.where(
        slot_used[:, None],
        jnp.take(token_rows, pair_of_slot // topk_count, axis=0),
        jnp.zeros((), jnp.bfloat16),
    ).reshape(experts, capacity, model_width)
    received = expert_swap(send)
    inputs = expert_rows(received).reshape(-1, model_width)
    partial_result, gate_pre, up_pre, expert_hidden = expert_forward(
        inputs, expert_gate[0], expert_up[0], expert_down[0]
    )
    returned = expert_sums(partial_result.reshape(-1, capacity, model_width)).astype(jnp.bfloat16)
    back = expert_swap(returned)
    picked = (
        jnp.take(back.reshape(-1, model_width), slot_index, axis=0)
        .astype(jnp.float32)
        .reshape(tok_dev, topk_count, model_width)
    )
    routed = jnp.sum(gates[:, :, None] * picked, axis=1)
    output = (hidden_state + shared_result + to_features(routed)).astype(jnp.bfloat16)
    grad_out = cotangent.astype(jnp.float32)
    grad_tokens = to_tokens(cotangent).astype(jnp.float32)
    d_gates = jnp.einsum("tkd,td->tk", picked, grad_tokens, precision=lax.Precision.HIGHEST)
    d_picked = (
        (gates[:, :, None] * grad_tokens[:, None, :])
        .reshape(pair_count, model_width)
        .astype(jnp.bfloat16)
    )
    d_back = jnp.where(
        slot_used[:, None], jnp.take(d_picked, pair_of_slot, axis=0), jnp.zeros((), jnp.bfloat16)
    ).reshape(experts, capacity, model_width)
    d_returned = expert_swap(d_back)
    d_result_rows = expert_rows(d_returned).reshape(-1, model_width)
    d_inputs, grad_gate, grad_up, grad_down = expert_backward(
        inputs,
        gate_pre,
        up_pre,
        expert_hidden,
        d_result_rows,
        expert_gate[0],
        expert_up[0],
        expert_down[0],
    )
    d_received = expert_sums(d_inputs.reshape(-1, capacity, model_width)).astype(jnp.bfloat16)
    d_send = expert_swap(d_received)
    d_tokens = jnp.sum(
        jnp.take(d_send.reshape(-1, model_width), slot_index, axis=0)
        .astype(jnp.float32)
        .reshape(tok_dev, topk_count, model_width),
        axis=1,
    )
    d_selected = (d_gates - jnp.sum(d_gates * gates, axis=1, keepdims=True)) / selected_total
    d_router_probs = jnp.sum(jnp.where(picks, d_selected[:, :, None], 0.0), axis=1)
    d_logits = router_probs * (
        d_router_probs - jnp.sum(router_probs * d_router_probs, axis=1, keepdims=True)
    )
    grad_router = lax.dot_general(
        token_rows.astype(jnp.float32),
        d_logits,
        (((0,), (0,)), ((), ())),
        precision=lax.Precision.HIGHEST,
        preferred_element_type=jnp.float32,
    )
    d_tokens = d_tokens + lax.dot_general(
        d_logits,
        router.astype(jnp.float32),
        (((1,), (1,)), ((), ())),
        precision=lax.Precision.HIGHEST,
        preferred_element_type=jnp.float32,
    )
    d_second = to_features(d_tokens)
    grad_rows = gather_rows(cotangent)
    grad_shared_down = dot_tn(shared_all, grad_rows)
    d_shared_hidden = sum_cols(dot_nt(grad_rows, shared_down))
    sigmoid_shared = jax.nn.sigmoid(shared_gate_pre)
    d_shared_up = (d_shared_hidden * shared_gate_pre * sigmoid_shared).astype(jnp.bfloat16)
    d_shared_gate = (
        d_shared_hidden
        * shared_up_pre
        * sigmoid_shared
        * (1.0 + shared_gate_pre * (1.0 - sigmoid_shared))
    ).astype(jnp.bfloat16)
    d_gate_all, d_up_all = gather_cols((d_shared_gate, d_shared_up))
    grad_shared_gate = dot_tn(second_rows, d_gate_all)
    grad_shared_up = dot_tn(second_rows, d_up_all)
    d_second = d_second + sum_rows(dot_nt(d_gate_all, shared_gate) + dot_nt(d_up_all, shared_up))
    d_norm_two, grad_gain_two = norm_back(hidden_state, factor_two, gain_two, d_second, width)
    d_hidden = grad_out + d_norm_two
    d_branch_rows = gather_rows(d_hidden.astype(jnp.bfloat16))
    grad_w_out = dot_tn(attended_all, d_branch_rows)
    d_attended = (
        sum_cols(dot_nt(d_branch_rows, w_out))
        .astype(jnp.bfloat16)
        .reshape(group, heads_here, V_DIM)
    )
    d_query_blocks = []
    d_keys = jnp.zeros((group, heads_here, head_dim), jnp.float32)
    d_values = jnp.zeros((group, heads_here, V_DIM), jnp.float32)
    for number, first in enumerate(range(0, group, query_rows)):
        query_block = queries[first : first + query_rows]
        d_block = d_attended[first : first + query_rows]
        scores = masked_scores(query_block, keys, seq_ids, first, scale)
        probs = jnp.exp(scores - block_totals[number])
        d_probs = jnp.einsum("qhd,khd->hqk", d_block, values, preferred_element_type=jnp.float32)
        delta = jnp.sum(probs * d_probs, axis=2, keepdims=True)
        d_scores = (probs * (d_probs - delta)).astype(jnp.bfloat16)
        d_query_blocks.append(
            jnp.einsum("hqk,khd->qhd", d_scores, keys, preferred_element_type=jnp.float32) * scale
        )
        d_keys = (
            d_keys
            + jnp.einsum("hqk,qhd->khd", d_scores, query_block, preferred_element_type=jnp.float32)
            * scale
        )
        d_values = d_values + jnp.einsum(
            "hqk,qhd->khd", probs.astype(jnp.bfloat16), d_block, preferred_element_type=jnp.float32
        )
    d_query = jnp.concatenate(d_query_blocks, axis=0)
    d_query_pre = (
        jnp.concatenate(
            [
                d_query[..., :QK_NOPE],
                unrotate(d_query[..., QK_NOPE:], cosine[:, None, :], sine[:, None, :]),
            ],
            axis=2,
        )
        .astype(jnp.bfloat16)
        .reshape(group, heads_here * head_dim)
    )
    d_key_value = (
        jnp.concatenate([d_keys[..., :QK_NOPE], d_values], axis=2)
        .astype(jnp.bfloat16)
        .reshape(group, heads_here * (QK_NOPE + V_DIM))
    )
    grad_w_kv = dot_tn(compressed, d_key_value)
    d_latent_sum = latent_total(
        jnp.concatenate([dot_nt(d_key_value, w_kv), jnp.sum(d_keys[..., QK_NOPE:], axis=1)], axis=1)
    )
    d_compressed = d_latent_sum[:, :KV_RANK]
    weighted = d_compressed * latent_gain
    grad_latent_gain = jnp.sum(d_compressed * compressed_raw * kv_factor[:, None], axis=0)
    inner = jnp.sum(weighted * compressed_raw, axis=1)
    d_raw = (
        kv_factor[:, None] * weighted
        - compressed_raw * (kv_factor * kv_factor * kv_factor * inner / KV_RANK)[:, None]
    )
    d_latent = jnp.concatenate(
        [d_raw, unrotate(d_latent_sum[:, KV_RANK:], cosine, sine)], axis=1
    ).astype(jnp.bfloat16)
    grad_w_latent = dot_tn(sub_cols, d_latent)
    d_query_all = gather_cols(d_query_pre)
    grad_w_query = dot_tn(gathered, d_query_all)
    d_gathered = dot_nt(d_query_all, w_query)
    start_col = row_id * slab
    piece = lax.dynamic_slice_in_dim(d_gathered, start_col, slab, 1) + dot_nt(d_latent, w_latent[0])
    d_gathered = lax.dynamic_update_slice_in_dim(d_gathered, piece, start_col, 1)
    d_first = sum_rows(d_gathered)
    d_norm_one, grad_gain_one = norm_back(input_wide, factor_one, gain_one, d_first, width)
    input_grad = d_hidden + d_norm_one
    gain_one_full = lax.dynamic_update_slice_in_dim(
        jnp.zeros((width,), jnp.float32), grad_gain_one, col_id * half_width, 0
    )
    gain_two_full = lax.dynamic_update_slice_in_dim(
        jnp.zeros((width,), jnp.float32), grad_gain_two, col_id * half_width, 0
    )
    gain_one_all, gain_two_all, router_all = lax.psum(
        (gain_one_full, gain_two_full, grad_router), ("row", "col", "exp")
    )
    summed = (
        lax.psum(grad_w_query.astype(jnp.bfloat16), "exp").astype(jnp.float32),
        lax.psum(grad_w_latent.astype(jnp.bfloat16), "exp").astype(jnp.float32),
        lax.psum(grad_latent_gain.astype(jnp.bfloat16), "exp").astype(jnp.float32),
        lax.psum(grad_w_kv.astype(jnp.bfloat16), "exp").astype(jnp.float32),
        lax.psum(grad_w_out.astype(jnp.bfloat16), "exp").astype(jnp.float32),
        lax.psum(grad_shared_gate.astype(jnp.bfloat16), "exp").astype(jnp.float32),
        lax.psum(grad_shared_up.astype(jnp.bfloat16), "exp").astype(jnp.float32),
        lax.psum(grad_shared_down.astype(jnp.bfloat16), "exp").astype(jnp.float32),
    )
    return (
        output,
        input_grad,
        gain_one_all,
        summed[0],
        summed[1][None],
        summed[2],
        summed[3],
        summed[4],
        gain_two_all,
        summed[5],
        summed[6],
        summed[7],
        router_all,
        grad_gate[None],
        grad_up[None],
        grad_down[None],
    )


def solution(mesh):
    placed = (
        P(("row", "exp"), "col"),
        P("exp", None),
        P("col", ("row", "exp"), None),
        P(),
        P("col", "row"),
        P("col", "row", None),
        P(),
        P(None, ("row", "col")),
        P("row", "col"),
        P(),
        P("col", "row"),
        P("col", "row"),
        P("row", "col"),
        P(),
        P(("row", "exp"), None, "col"),
        P(("row", "exp"), None, "col"),
        P(("row", "exp"), None, "col"),
        P(("row", "exp"), "col"),
    )
    return jax.shard_map(
        per_device,
        mesh=mesh,
        in_specs=placed,
        out_specs=(
            P(("row", "exp"), "col"),
            P(("row", "exp"), "col"),
            P(),
            P("col", "row"),
            P("col", "row", None),
            P(),
            P(None, ("row", "col")),
            P("row", "col"),
            P(),
            P("col", "row"),
            P("col", "row"),
            P("row", "col"),
            P(),
            P(("row", "exp"), None, "col"),
            P(("row", "exp"), None, "col"),
            P(("row", "exp"), None, "col"),
        ),
        check_vma=False,
    )
```

profile of v0, /device:TPU:0, one launch (start us, length us, event | category | flops | bytes accessed | tf_op | source)
XLA Modules:
  0.0 2614.2 jit_solution(7120270421612438400)
XLA Ops:
  18.1 27.4 %all-gather.12.cloned.1.call-done = bf16[1280,1024]{1,0:T(8,128)(2,1)} async-done(((bf16[320,1024]{1,0:T(8,128)(2,1)}), bf16[1280,1024]{1,0:T(8,128)(2,1)}) %all-gather.12.cloned.1.call-update) | async-done | bytes 2621456 | tf_op jit(solution)/shard_map/all_gather | solution.py:27
  59.0 58.2 %all-reduce.8.cloned.1.call-done = f32[1280,576]{0,1:T(8,128)} async-done(((f32[1280,576]{0,1:T(8,128)}), f32[1280,576]{0,1:T(8,128)}) %all-reduce.8.cloned.1.call-update) | async-done | bytes 2949136 | tf_op jit(solution)/shard_map/psum | solution.py:47
  126.1 45.9 %reduce-scatter.12.cloned.1.call-done = f32[1280,384]{1,0:T(8,128)} async-done(((f32[1280,768]{1,0:T(8,128)}), f32[1280,384]{1,0:T(8,128)}) %reduce-scatter.12.cloned.1.call-update) | async-done | bytes 1966096 | tf_op jit(solution)/shard_map/reduce_scatter | solution.py:31
  190.5 24.0 all-gather.14.cloned.1.call-done
  314.1 143.9 %all_to_all.81 = bf16[16,90,2048]{2,1,0:T(8,128)(2,1)S(1)} all-to-all(bf16[16,90,2048]{2,1,0:T(8,128)(2,1)S(1)} %select_select_fusion.1), channel_id=1, replica_groups=mesh['row'=4,'col'=2,'exp'=4] {'row','exp'}, dimensions={0} | all-to-all | bytes 11796480 | tf_op jit(solution)/shard_map/all_to_all | solution.py:61
  464.0 141.5 %all-gather.20.cloned.1.call-done = bf16[32,90,2048]{2,0,1:T(8,128)(2,1)} async-done(((bf16[16,90,2048]{2,0,1:T(8,128)(2,1)}), bf16[32,90,2048]{2,0,1:T(8,128)(2,1)}) %all-gather.20.cloned.1.call-update) | async-done | bytes 11796496 | tf_op jit(solution)/shard_map/all_gather | solution.py:65
  711.4 129.5 %reduce-scatter.22.cloned.1.call-done = bf16[16,90,2048]{2,1,0:T(8,128)(2,1)} async-done(((bf16[32,90,2048]{2,1,0:T(8,128)(2,1)}), bf16[16,90,2048]{2,1,0:T(8,128)(2,1)}) %reduce-scatter.22.cloned.1.call-update) | async-done | bytes 5898256 | tf_op jit(solution)/shard_map/reduce_scatter | solution.py:69
  877.1 109.0 %all-to-all-done.2 = bf16[16,90,2048]{2,1,0:T(8,128)(2,1)} async-done(((bf16[16,90,2048]{2,1,0:T(8,128)(2,1)}), bf16[16,90,2048]{2,1,0:T(8,128)(2,1)}, u32[]{:S(2)}, u32[]{:S(2)}) %all-to-all-start.2) | async-done | bytes 5898272 | tf_op jit(solution)/shard_map/all_to_all | solution.py:61
  1063.8 137.9 %all-to-all-done.5 = bf16[16,90,2048]{2,1,0:T(8,128)(2,1)} async-done(((bf16[16,90,2048]{2,1,0:T(8,128)(2,1)}), bf16[16,90,2048]{2,1,0:T(8,128)(2,1)}, u32[]{:S(2)}, u32[]{:S(2)}) %all-to-all-start.5) | async-done | bytes 5898272 | tf_op jit(solution)/shard_map/all_to_all | solution.py:61
  1230.7 121.2 %all-gather.22.cloned.1.call-done = bf16[32,90,2048]{2,0,1:T(8,128)(2,1)} async-done(((bf16[16,90,2048]{2,0,1:T(8,128)(2,1)}), bf16[32,90,2048]{2,0,1:T(8,128)(2,1)}) %all-gather.22.cloned.1.call-update) | async-done | bytes 11796496 | tf_op jit(solution)/shard_map/all_gather | solution.py:65
  1453.9 50.7 %reduce-scatter.16.cloned.1.call-done = f32[1280,352]{0,1:T(8,128)} async-done(((f32[1280,704]{0,1:T(8,128)}), f32[1280,352]{0,1:T(8,128)}) %reduce-scatter.16.cloned.1.call-update) | async-done | bytes 1802256 | tf_op jit(solution)/shard_map/reduce_scatter | solution.py:31
  1510.1 141.1 %reduce-scatter.24.cloned.1.call-done = bf16[16,90,2048]{2,1,0:T(8,128)(2,1)} async-done(((bf16[32,90,2048]{2,1,0:T(8,128)(2,1)}), bf16[16,90,2048]{2,1,0:T(8,128)(2,1)}) %reduce-scatter.24.cloned.1.call-update) | async-done | bytes 5898256 | tf_op jit(solution)/shard_map/reduce_scatter | solution.py:69
  1657.0 26.1 %all-gather.26.cloned.1.call-done = bf16[1280,704]{0,1:T(8,128)(2,1)} async-done(((bf16[1280,352]{0,1:T(8,128)(2,1)}), bf16[1280,704]{0,1:T(8,128)(2,1)}) %all-gather.26.cloned.1.call-update) | async-done | bytes 1802256 | tf_op jit(solution)/shard_map/all_gather | solution.py:37
  1689.3 25.8 all-gather.28.cloned.1.call-done
  1723.5 72.9 %all-to-all-done.6 = bf16[16,90,2048]{2,1,0:T(8,128)(2,1)} async-done(((bf16[16,90,2048]{2,1,0:T(8,128)(2,1)}), bf16[16,90,2048]{2,1,0:T(8,128)(2,1)}, u32[]{:S(2)}, u32[]{:S(2)}) %all-to-all-start.6) | async-done | bytes 5898272 | tf_op jit(solution)/shard_map/all_to_all | solution.py:61
  1862.4 22.9 all-gather.30.cloned.1.call-done
  1924.0 33.0 %reduce-scatter.30.cloned.1.call-done = f32[1280,256]{1,0:T(8,128)} async-done(((f32[1280,512]{1,0:T(8,128)}), f32[1280,256]{1,0:T(8,128)}) %reduce-scatter.30.cloned.1.call-update) | async-done | bytes 1310736 | tf_op jit(solution)/shard_map/reduce_scatter | solution.py:31
  1997.0 61.0 %all-reduce.10.cloned.1.call-done = f32[1280,576]{0,1:T(8,128)} async-done(((f32[1280,576]{0,1:T(8,128)}), f32[1280,576]{0,1:T(8,128)}) %all-reduce.10.cloned.1.call-update) | async-done | bytes 2949136 | tf_op jit(solution)/shard_map/psum | solution.py:47
  2067.8 24.2 all-gather.32.cloned.1.call-done
  2184.0 186.7 %all-reduce.14.cloned.1.call-done = (bf16[1024,768]{1,0:T(8,128)(2,1)}, bf16[1,256,576]{1,2,0:T(8,128)(2,1)}, bf16[512,512]{1,0:T(8,128)(2,1)}, bf16[512,1024]{1...) async-done(((bf16[1024,768]{1,0:T(8,128)(2,1)}, bf16[1,256,576]{1,2,0:T(8,128)(2,1)}, bf16[512,512]{1,0:T(8,128)(2,1)}, ...) | async-done | bytes 7766032 | tf_op jit(solution)/shard_map/psum | solution.py:463
  2385.5 37.9 %reduce-scatter.32.cloned.1.call-done = f32[320,1024]{1,0:T(8,128)} async-done(((f32[1280,1024]{1,0:T(8,128)}), f32[320,1024]{1,0:T(8,128)}) %reduce-scatter.32.cloned.1.call-update) | async-done | bytes 1310736 | tf_op jit(solution)/shard_map/reduce_scatter | solution.py:43
  2432.6 44.8 %reduce-scatter.20.cloned.1.call-done = f32[320,1024]{1,0:T(8,128)} async-done(((f32[1280,1024]{1,0:T(8,128)}), f32[320,1024]{1,0:T(8,128)}) %reduce-scatter.20.cloned.1.call-update) | async-done | bytes 1310736 | tf_op jit(solution)/shard_map/reduce_scatter | solution.py:43
  2483.1 39.5 %all-reduce.1 = (f32[2048]{0:T(1024)}, f32[2048]{0:T(1024)}) all-reduce(f32[2048]{0:T(1024)S(1)} %dynamic_update_slice.10, f32[2048]{0:T(1024)} %copy-done.80), channel_id=1, replica_groups=mesh['row'=4,'col'=2,'exp'=4] {'row','col','exp'}, use_global_device_ids=true, to_apply=%region_48.50 | all-reduce | flops 4096 | bytes 32768 | tf_op jit(solution)/shard_map/psum | solution.py:459
  2522.7 83.3 %all-reduce.12.cloned.1.call-done = f32[2048,16]{0,1:T(8,128)} async-done(((f32[2048,16]{0,1:T(8,128)}), f32[2048,16]{0,1:T(8,128)}) %all-reduce.12.cloned.1.call-update) | async-done | bytes 131088 | tf_op jit(solution)/shard_map/psum | solution.py:459
  (519 shorter events, 810.1 us)
Async XLA Ops:
  48.9 123.1 %reduce-scatter.12.cloned.1.call-start = ((), (), s32[]{:S(2)}) async-start(), calls=%async_computation.21 | async-start | bytes 5898240 | tf_op jit(solution)/shard_map/reduce_scatter | solution.py:31
  55.3 159.2 %all-gather.14.cloned.1.call-start = ((), (), s32[]{:S(2)}) async-start(), calls=%async_computation.22 | async-start | bytes 1966080 | tf_op jit(solution)/shard_map/all_gather | solution.py:37
  286.1 319.4 %all-gather.20.cloned.1.call-start = ((), (), s32[]{:S(2)}) async-start(), calls=%async_computation.29 | async-start | bytes 17694720 | tf_op jit(solution)/shard_map/all_gather | solution.py:65
  463.8 377.1 %reduce-scatter.22.cloned.1.call-start = ((), (), s32[]{:S(2)}) async-start(), calls=%async_computation.30 | async-start | bytes 18874368 | tf_op jit(solution)/shard_map/reduce_scatter | solution.py:69
  840.9 145.2 %all-to-all-start.2 = ((bf16[16,90,2048]{2,1,0:T(8,128)(2,1)}), bf16[16,90,2048]{2,1,0:T(8,128)(2,1)}, u32[]{:S(2)}, u32[]{:S(2)}) async-start(bf16[16,90,2048]{2,1,0:T(8,128)(2,1)} %reduce-scatter.22.cloned.1.call-done), calls=%async_computation.8 | async-start | bytes 12582912 | tf_op jit(solution)/shard_map/all_to_all | solution.py:61
  1057.6 144.1 %all-to-all-start.5 = ((bf16[16,90,2048]{2,1,0:T(8,128)(2,1)}), bf16[16,90,2048]{2,1,0:T(8,128)(2,1)}, u32[]{:S(2)}, u32[]{:S(2)}) async-start(bf16[16,90,2048]{2,1,0:T(8,128)(2,1)} %select_select_fusion), calls=%async_computation.11 | async-start | bytes 12582912 | tf_op jit(solution)/shard_map/all_to_all | solution.py:61
  1062.3 148.0 %all-gather.24.cloned.1.call-start = ((), (), s32[]{:S(2)}) async-start(), calls=%async_computation.33 | async-start | bytes 3276800 | tf_op jit(solution)/shard_map/all_gather | solution.py:27
  1063.0 153.7 %all-gather.16.cloned.1.call-start = ((), (), s32[]{:S(2)}) async-start(), calls=%async_computation.24 | async-start | bytes 3276800 | tf_op jit(solution)/shard_map/all_gather | solution.py:27
  1063.8 288.2 %all-gather.22.cloned.1.call-start = ((), (), s32[]{:S(2)}) async-start(), calls=%async_computation.31 | async-start | bytes 17694720 | tf_op jit(solution)/shard_map/all_gather | solution.py:65
  1210.3 234.4 %reduce-scatter.26.cloned.1.call-start = ((), (), s32[]{:S(2)}) async-start(), calls=%async_computation.34 | async-start | bytes 5406720 | tf_op jit(solution)/shard_map/reduce_scatter | solution.py:31
  1216.7 237.2 %reduce-scatter.18.cloned.1.call-start = ((), (), s32[]{:S(2)}) async-start(), calls=%async_computation.26 | async-start | bytes 5406720 | tf_op jit(solution)/shard_map/reduce_scatter | solution.py:31
  1224.0 280.6 %reduce-scatter.16.cloned.1.call-start = ((), (), s32[]{:S(2)}) async-start(), calls=%async_computation.25 | async-start | bytes 5406720 | tf_op jit(solution)/shard_map/reduce_scatter | solution.py:31
  1230.5 420.8 %reduce-scatter.24.cloned.1.call-start = ((), (), s32[]{:S(2)}) async-start(), calls=%async_computation.32 | async-start | bytes 18874368 | tf_op jit(solution)/shard_map/reduce_scatter | solution.py:69
  1444.6 238.6 %all-gather.26.cloned.1.call-start = ((), (), s32[]{:S(2)}) async-start(), calls=%async_computation.35 | async-start | bytes 2703360 | tf_op jit(solution)/shard_map/all_gather | solution.py:37
  1509.6 205.5 %all-gather.28.cloned.1.call-start = ((), (), s32[]{:S(2)}) async-start(), calls=%async_computation.36 | async-start | bytes 2703360 | tf_op jit(solution)/shard_map/all_gather | solution.py:37
  1651.3 145.2 %all-to-all-start.6 = ((bf16[16,90,2048]{2,1,0:T(8,128)(2,1)}), bf16[16,90,2048]{2,1,0:T(8,128)(2,1)}, u32[]{:S(2)}, u32[]{:S(2)}) async-start(bf16[16,90,2048]{2,1,0:T(8,128)(2,1)} %reduce-scatter.24.cloned.1.call-done), calls=%async_computation.13 | async-start | bytes 12582912 | tf_op jit(solution)/shard_map/all_to_all | solution.py:61
  1657.0 186.8 %reduce-scatter.28.cloned.1.call-start = ((), (), s32[]{:S(2)}) async-start(), calls=%async_computation.37 | async-start | bytes 6553600 | tf_op jit(solution)/shard_map/reduce_scatter | solution.py:43
  1890.4 167.7 %all-reduce.10.cloned.1.call-start = ((), (), s32[]{:S(2)}) async-start(), calls=%async_computation.41 | async-start | bytes 5898240 | tf_op jit(solution)/shard_map/psum | solution.py:47
  1990.2 101.7 %all-gather.32.cloned.1.call-start = ((), (), s32[]{:S(2)}) async-start(), calls=%async_computation.40 | async-start | bytes 2949120 | tf_op jit(solution)/shard_map/all_gather | solution.py:37
  1993.0 377.7 %all-reduce.14.cloned.1.call-start = ((), (), s32[]{:S(2)}) async-start(), calls=%async_computation.44 | async-start | bytes 15532032 | tf_op jit(solution)/shard_map/psum | solution.py:463
  2097.7 325.6 %reduce-scatter.32.cloned.1.call-start = ((), (), s32[]{:S(2)}) async-start(), calls=%async_computation.42 | async-start | bytes 6553600 | tf_op jit(solution)/shard_map/reduce_scatter | solution.py:43
  2108.4 369.0 %reduce-scatter.20.cloned.1.call-start = ((), (), s32[]{:S(2)}) async-start(), calls=%async_computation.28 | async-start | bytes 6553600 | tf_op jit(solution)/shard_map/reduce_scatter | solution.py:43
  2124.6 352.8 %all-to-all-start.3 = ((bf16[160,2,1024]{2,0,1:T(8,128)(2,1)}), bf16[160,2,1024]{2,0,1:T(8,128)(2,1)}, u32[]{:S(2)}, u32[]{:S(2)}) async-start(bf16[160,2,1024]{2,0,1:T(8,128)(2,1)} %bitcast.165), calls=%async_computation.9 | async-start | bytes 1310720 | tf_op jit(solution)/shard_map/all_to_all | solution.py:55
  2128.9 477.1 %all-reduce.12.cloned.1.call-start = ((), (), s32[]{:S(2)}) async-start(), calls=%async_computation.43 | async-start | bytes 262144 | tf_op jit(solution)/shard_map/psum | solution.py:459
  (133 other events, 4357.6 us)
Sparse Core Ops, SparseCore 0:
  18.2 27.3 all-gather.11
  49.5 67.6 all-reduce.7
  120.0 51.9 reduce-scatter.11
  190.2 24.2 all-gather.13
  220.2 51.2 reduce-scatter.13
  463.9 141.5 all-gather.19
  690.6 150.2 reduce-scatter.21
  1064.7 79.3 all-gather.23
  1210.4 141.5 all-gather.21
  1354.8 48.3 reduce-scatter.25
  1405.4 48.3 reduce-scatter.17
  1456.1 48.3 reduce-scatter.15
  1506.8 144.4 reduce-scatter.23
  1653.3 29.8 all-gather.25
  1685.2 29.7 all-gather.27
  1722.9 51.3 reduce-scatter.27
  1886.8 29.7 all-gather.17
  1919.3 37.5 reduce-scatter.29
  1990.4 67.6 all-reduce.9
  2060.3 31.6 all-gather.31
  2097.8 272.8 all-reduce.13
  2373.1 50.1 reduce-scatter.31
  2426.0 51.3 reduce-scatter.19
  2483.4 122.4 all-reduce.11
  (2 shorter events, 45.1 us)
where the time goes:
time: 2620 us; the launch traced here: 2610 us
  waiting for transfers between devices  1660 us (63%)
  matrix products  277 us (11%)
  local copies, waits for them, and re-layouts  263 us (10%)
  blocking collectives  239 us (9%)
  other arithmetic  124 us (5%)
  starting transfers between devices  32 us (1%)
    all_to_all x3, waiting for transfers between devices, expert_swap(): lax.all_to_all(value, ('row', 'exp'), split_axis=0, concat_axis=0, tiled=...  320 us
    reduce_scatter x2, waiting for transfers between devices, expert_sums(): lax.psum_scatter(value.astype(jnp.bfloat16), 'col', scatter_dimension=0,...  271 us
    all_gather x2, waiting for transfers between devices, expert_rows(): return lax.all_gather(value, 'col', axis=0, tiled=True)  263 us
    psum x1, waiting for transfers between devices, per_device(): lax.psum(grad_w_query.astype(jnp.bfloat16), 'exp').astype(jnp.float32)  187 us
    all_to_all x1, blocking collectives, expert_swap(): lax.all_to_all(value, ('row', 'exp'), split_axis=0, concat_axis=0, tiled=...  144 us
    reduce_scatter x5, waiting for transfers between devices, sum_cols(): return lax.psum_scatter(value, 'col', scatter_dimension=1, tiled=True)  139 us
    psum x2, waiting for transfers between devices, latent_total(): return lax.psum(value, ('row', 'col'))  119 us
    all_gather x5, waiting for transfers between devices, gather_cols(): lax.all_gather(as_sent(value), 'col', axis=1, tiled=True)  117 us
  transfers between devices with their start and end apart: 32, of which 27 were waited for; matrix products, arithmetic and copies ran while one was open for 15% of the time, Pallas kernels for 0%

commit v1 on v0

v1 whole, which is shorter than its diff:
```python
import functools
import math

import jax
import jax.numpy as jnp
from jax import lax
from jax.experimental import pallas as pl
from jax.experimental.pallas import tpu as pltpu
from jax.sharding import PartitionSpec as P

QK_NOPE = 128
ROPE = 64
KV_RANK = 512
V_DIM = 128

epsilon = 1e-06
theta_base = 10000.0
SWAP = [(0, 1), (1, 0)]


MESH = pl.DeviceIdType.MESH


class Place:
    def __init__(self, layers):
        self.layers = layers
        self.row, self.col = lax.axis_index("row"), lax.axis_index("col")
        self.layer = lax.axis_index("exp") if layers > 1 else 0
        self.core = lax.rem(self.row, 2)
        self.x_row = lax.rem(self.row + 2, 4)
        self.core_row = self.row + 1 - 2 * self.core
        self.y_col = 1 - self.col
        self.to_x = {"row": self.x_row}
        self.to_y = {"col": self.y_col}
        self.to_core = {"row": self.core_row}
        self.above = {"exp": self.layer + 1}
        self.below = {"exp": self.layer - 1}

    def greet(self):
        barrier = pltpu.get_barrier_semaphore()
        for target in (self.to_x, self.to_y, self.to_core):
            pl.semaphore_signal(barrier, inc=1, device_id=target, device_id_type=MESH)
        if self.layers > 1:

            @pl.when(self.layer > 0)
            def _():
                pl.semaphore_signal(barrier, inc=1, device_id=self.below, device_id_type=MESH)

            @pl.when(self.layer < self.layers - 1)
            def _():
                pl.semaphore_signal(barrier, inc=1, device_id=self.above, device_id_type=MESH)

        peers = 3
        if self.layers > 1:
            peers = peers + jnp.where(self.layer > 0, 1, 0) + jnp.where(self.layer < self.layers - 1, 1, 0)
        pl.semaphore_wait(barrier, peers)


def remote(src, dst, send, recv, target):
    return pltpu.make_async_remote_copy(
        src_ref=src, dst_ref=dst, send_sem=send, recv_sem=recv, device_id=target, device_id_type=MESH
    )


def first_part(rows):
    return (rows // 2 + 15) // 16 * 16


def gather_body(
    layers, src, out, held, store_sem, up_send, down_send, z_recv, send, recv, diag_send, diag_recv
):
    me = Place(layers)
    rows, width = src.shape
    part = first_part(rows)
    spans = ((0, part), (part, rows - part))

    owners = (
        (me.row, me.col),
        (me.x_row, me.col),
        (me.row, me.y_col),
        (me.x_row, me.y_col),
    )
    sides = (me.to_x, me.to_y)

    def area(where, row, col, layer, span=(0, rows)):
        first = pl.multiple_of((row * layers + layer) * rows + span[0], 16)
        return where.at[pl.ds(first, span[1]), pl.ds(pl.multiple_of(col * width, 128), width)]

    def held_piece(kind, layer, span=(0, rows)):
        return area(held, *owners[kind], layer, span)

    def partner_piece(where, kind, layer):
        row, col = owners[kind]
        return area(where, row + 1 - 2 * me.core, col, layer)

    def store(kind, layer, partner):
        if partner:
            pair = (partner_piece(held, kind, layer), partner_piece(out, kind, layer))
        else:
            pair = (held_piece(kind, layer), area(out, *owners[kind], layer))
        return pltpu.make_async_copy(*pair, store_sem.at[1 if partner else 0, kind, layer])

    def to_core(kind, layer):
        piece = held_piece(kind, layer)
        return remote(piece, piece, send.at[4, kind, layer], recv.at[4, kind, layer], me.to_core)

    def from_core(kind, layer):
        piece = partner_piece(held, kind, layer)
        return remote(piece, piece, send.at[4, kind, layer], recv.at[4, kind, layer], me.to_core)

    def beside(axis, half, layer, incoming=False):
        piece = held_piece(axis + 1 if incoming else 0, layer, spans[half])
        sems = (2 * axis + half, 0, layer)
        return remote(piece, piece, send.at[sems], recv.at[sems], sides[axis])

    def corner(axis, layer, incoming=False):
        piece = held_piece(3 if incoming else axis + 1, layer, spans[axis])
        return remote(
            piece, piece, diag_send.at[axis, layer], diag_recv.at[axis, layer], sides[1 - axis]
        )

    def along(up, layer):
        piece = held_piece(0, layer)
        return remote(
            piece,
            piece,
            (up_send if up else down_send).at[layer],
            z_recv.at[layer],
            me.above if up else me.below,
        )

    def spread(layer):
        beside(0, 0, layer).start()
        beside(1, 1, layer).start()
        beside(0, 1, layer).start()
        beside(1, 0, layer).start()
        to_core(0, layer).start()

    def at_distance(distance, act):
        if distance == 0:
            act(me.layer, None)
            return

        @pl.when(me.layer >= distance)
        def _():
            act(me.layer - distance, True)

        @pl.when(me.layer + distance < layers)
        def _():
            act(me.layer + distance, False)

    own = pltpu.make_async_copy(src, held_piece(0, me.layer), store_sem.at[0, 0, me.layer])
    own.start()
    me.greet()
    own.wait()
    if layers > 1:

        @pl.when(me.layer < layers - 1)
        def _():
            along(True, me.layer).start()

        @pl.when(me.layer > 0)
        def _():
            along(False, me.layer).start()

    spread(me.layer)
    store(0, me.layer, False).start()

    def arrived(layer, upward):
        along(upward, layer).wait_recv()
        if upward:

            @pl.when(me.layer < layers - 1)
            def _():
                along(True, layer).start()
        else:

            @pl.when(me.layer > 0)
            def _():
                along(False, layer).start()

        spread(layer)
        store(0, layer, False).start()

    def second(layer, upward):
        for axis in (0, 1):
            beside(axis, axis, layer, True).wait_recv()
            corner(axis, layer).start()
        for axis in (0, 1):
            beside(axis, 1 - axis, layer, True).wait_recv()
            to_core(axis + 1, layer).start()
            store(axis + 1, layer, False).start()

    def third(layer, upward):
        for axis in (0, 1):
            corner(axis, layer, True).wait_recv()
        to_core(3, layer).start()
        store(3, layer, False).start()
        for kind in range(4):
            from_core(kind, layer).wait_recv()
            store(kind, layer, True).start()

    for step in range(1, layers + 2):
        if step < layers:
            at_distance(step, arrived)
        if step - 1 < layers:
            at_distance(step - 1, second)
        if 0 <= step - 2 < layers:
            at_distance(step - 2, third)
    for layer in range(layers):
        for kind in range(4):
            to_core(kind, layer).wait_send()
            store(kind, layer, False).wait()
            store(kind, layer, True).wait()
        for axis in (0, 1):
            for half in (0, 1):
                beside(axis, half, layer).wait_send()
            corner(axis, layer).wait_send()
    if layers > 1:
        for layer in range(layers):

            @pl.when((me.layer < layers - 1) & (layer <= me.layer))
            def _():
                along(True, layer).wait_send()

            @pl.when((me.layer > 0) & (layer >= me.layer))
            def _():
                along(False, layer).wait_send()


def gather(value, layers, collective_id):
    rows, width = value.shape
    dma = pltpu.SemaphoreType.DMA
    whole = (4 * layers * rows, 2 * width)
    return pl.pallas_call(
        functools.partial(gather_body, layers),
        out_shape=jax.ShapeDtypeStruct(whole, value.dtype),
        in_specs=[pl.BlockSpec(memory_space=pl.ANY)],
        out_specs=pl.BlockSpec(memory_space=pl.ANY),
        scratch_shapes=[
            pltpu.VMEM(whole, value.dtype),
            dma((2, 4, layers)),
            dma((layers,)),
            dma((layers,)),
            dma((layers,)),
            dma((5, 4, layers)),
            dma((5, 4, layers)),
            dma((2, layers)),
            dma((2, layers)),
        ],
        compiler_params=pltpu.CompilerParams(
            collective_id=collective_id,
            has_side_effects=True,
            vmem_limit_bytes=56 * 1024 * 1024,
        ),
    )(value)


def scatter_body(
    layers,
    src,
    out,
    acc,
    core_in,
    diag_a,
    diag_b,
    side_in,
    line_in,
    load_sem,
    core_send,
    core_recv,
    diag_send,
    diag_recv,
    side_send,
    side_recv,
    line_send,
    line_recv,
):
    me = Place(layers)
    rows, width = out.shape
    part = first_part(rows)
    owners = (
        (me.row, me.col),
        (me.x_row, me.col),
        (me.row, me.y_col),
        (me.x_row, me.y_col),
    )

    def layer_at(step):
        if layers == 1:
            return 0
        found = 0
        for layer in range(layers):
            order = sorted(range(layers), key=lambda other: (-abs(other - layer), -other))
            found = found + jnp.where(me.layer == layer, order[step], 0)
        return found

    layer_of = [layer_at(step) for step in range(layers)]

    def area(row, col, layer):
        first = pl.multiple_of((row * layers + layer) * rows, 16)
        return src.at[pl.ds(first, rows), pl.ds(pl.multiple_of(col * width, 128), width)]

    def load(step, kind):
        return pltpu.make_async_copy(
            area(*owners[kind], layer_of[step]), acc.at[step, kind], load_sem.at[step, kind]
        )

    def to_core(step, kind):
        row, col = owners[kind]
        return remote(
            area(row + 1 - 2 * me.core, col, layer_of[step]),
            core_in.at[step, kind],
            core_send.at[step, kind],
            core_recv.at[step, kind],
            me.to_core,
        )

    def diag(step, axis):
        start, size = ((0, part), (part, rows - part))[axis]
        return remote(
            acc.at[step, 3, pl.ds(start, size)],
            (diag_a, diag_b)[axis].at[step],
            diag_send.at[axis, step],
            diag_recv.at[axis, step],
            (me.to_y, me.to_x)[axis],
        )

    def side(step, axis):
        return remote(
            acc.at[step, axis + 1],
            side_in.at[axis, step],
            side_send.at[axis, step],
            side_recv.at[axis, step],
            (me.to_x, me.to_y)[axis],
        )

    def line(step, up):
        layer = layer_of[step]
        way = 0 if up else 1
        return remote(
            acc.at[step, 0],
            line_in.at[way, layer],
            line_send.at[step],
            line_recv.at[way, layer],
            me.above if up else me.below,
        )

    lanes = 32 if rows % 32 == 0 else 16

    def add(target, others, start=0, size=rows, into=None):
        def step(i, carry):
            first = pl.multiple_of(i * lanes, 16)
            total = target[pl.ds(start + first, lanes), :].astype(jnp.float32)
            for other in others:
                total = total + other[pl.ds(first, lanes), :].astype(jnp.float32)
            if into is None:
                target[pl.ds(start + first, lanes), :] = total.astype(target.dtype)
            else:
                into[pl.ds(first, lanes), :] = total.astype(into.dtype)
            return carry

        lax.fori_loop(0, size // lanes, step, 0)

    me.greet()
    kinds = (3, 1, 2, 0)
    for step in range(layers):
        for kind in kinds:
            to_core(step, kind).start()
            load(step, kind).start()

    def ready(step, kind):
        load(step, kind).wait()
        to_core(step, kind).wait_recv()

    def stage_a(step):
        ready(step, 3)
        add(acc.at[step, 3], [core_in.at[step, 3]])
        diag(step, 0).start()
        diag(step, 1).start()

    def stage_b(step):
        for axis, buffer, start, size in (
            (0, diag_a, 0, part),
            (1, diag_b, part, rows - part),
        ):
            kind = axis + 1
            ready(step, kind)
            add(acc.at[step, kind], [core_in.at[step, kind]])
            diag(step, axis).wait_recv()
            add(acc.at[step, kind], [buffer.at[step]], start, size)
            side(step, axis).start()

    def stage_c(step):
        ready(step, 0)
        side(step, 0).wait_recv()
        side(step, 1).wait_recv()
        parts = [core_in.at[step, 0], side_in.at[0, step], side_in.at[1, step]]
        if layers == 1:
            add(acc.at[step, 0], parts, into=out)
            return
        add(acc.at[step, 0], parts)
        layer = layer_of[step]
        if step < layers - 1:

            @pl.when((layer > me.layer) & (me.layer > 0))
            def _():
                line(step, True).wait_recv()
                add(acc.at[step, 0], [line_in.at[0, layer]])

            @pl.when((layer < me.layer) & (me.layer < layers - 1))
            def _():
                line(step, False).wait_recv()
                add(acc.at[step, 0], [line_in.at[1, layer]])

            @pl.when(layer > me.layer)
            def _():
                line(step, True).start()

            @pl.when(layer < me.layer)
            def _():
                line(step, False).start()
        else:
            inner = (me.layer > 0) & (me.layer < layers - 1)

            @pl.when(me.layer > 0)
            def _():
                line(step, True).wait_recv()

            @pl.when(me.layer < layers - 1)
            def _():
                line(step, False).wait_recv()

            @pl.when(inner)
            def _():
                add(acc.at[step, 0], [line_in.at[0, layer], line_in.at[1, layer]], into=out)

            @pl.when(me.layer == 0)
            def _():
                add(acc.at[step, 0], [line_in.at[1, layer]], into=out)

            @pl.when(me.layer == layers - 1)
            def _():
                add(acc.at[step, 0], [line_in.at[0, layer]], into=out)

    for step in range(layers + 2):
        if step < layers:
            stage_a(step)
        if 0 <= step - 1 < layers:
            stage_b(step - 1)
        if 0 <= step - 2 < layers:
            stage_c(step - 2)
    for step in range(layers):
        for kind in kinds:
            to_core(step, kind).wait_send()
        for axis in (0, 1):
            diag(step, axis).wait_send()
            side(step, axis).wait_send()
        if step < layers - 1:

            @pl.when(layer_of[step] > me.layer)
            def _():
                line(step, True).wait_send()

            @pl.when(layer_of[step] < me.layer)
            def _():
                line(step, False).wait_send()


def scatter(value, layers, collective_id):
    rows, width = value.shape[0] // (4 * layers), value.shape[1] // 2
    part = first_part(rows)
    dma = pltpu.SemaphoreType.DMA
    buffer = lambda *lead: pltpu.VMEM((*lead, rows, width), value.dtype)
    return pl.pallas_call(
        functools.partial(scatter_body, layers),
        out_shape=jax.ShapeDtypeStruct((rows, width), jnp.float32),
        in_specs=[pl.BlockSpec(memory_space=pl.ANY)],
        out_specs=pl.BlockSpec(memory_space=pltpu.VMEM),
        scratch_shapes=[
            buffer(layers, 4),
            buffer(layers, 4),
            pltpu.VMEM((layers, part, width), value.dtype),
            pltpu.VMEM((layers, rows - part, width), value.dtype),
            buffer(2, layers),
            buffer(2, layers),
            dma((layers, 4)),
            dma((layers, 4)),
            dma((layers, 4)),
            dma((2, layers)),
            dma((2, layers)),
            dma((2, layers)),
            dma((2, layers)),
            dma((layers,)),
            dma((2, layers)),
        ],
        compiler_params=pltpu.CompilerParams(
            collective_id=collective_id,
            has_side_effects=True,
            vmem_limit_bytes=56 * 1024 * 1024,
        ),
    )(value)


def dot_nn(left, right):
    return jnp.dot(left, right, preferred_element_type=jnp.float32)


def dot_nt(left, right):
    return lax.dot_general(
        left, right, (((1,), (1,)), ((), ())), preferred_element_type=jnp.float32
    )


def dot_tn(left, right):
    return lax.dot_general(
        left, right, (((0,), (0,)), ((), ())), preferred_element_type=jnp.float32
    )


def rotate(value, cosine, sine):
    half = value.shape[-1] // 2
    first, second = (value[..., :half], value[..., half:])
    return jnp.concatenate(
        [first * cosine - second * sine, first * sine + second * cosine], axis=-1
    )


def unrotate(value, cosine, sine):
    half = value.shape[-1] // 2
    first, second = (value[..., :half], value[..., half:])
    return jnp.concatenate(
        [first * cosine + second * sine, second * cosine - first * sine], axis=-1
    )


def sequence_layout(lengths_row, group):
    ends = jnp.cumsum(lengths_row)
    starts = ends - lengths_row
    index = jnp.arange(group, dtype=jnp.int32)
    seq_ids = jnp.sum((index[:, None] >= ends[None, :]).astype(jnp.int32), axis=1)
    member = seq_ids[:, None] == jnp.arange(lengths_row.shape[0], dtype=jnp.int32)[None, :]
    begins = jnp.sum(jnp.where(member, starts[None, :], 0), axis=1)
    return (seq_ids, index - begins)


def rotary_tables(places):
    half = ROPE // 2
    freqs = jnp.power(theta_base, -jnp.arange(half, dtype=jnp.float32) * (2.0 / ROPE))
    angle = places.astype(jnp.float32)[..., None] * freqs
    return (jnp.cos(angle), jnp.sin(angle))


def norm_back(value, factor, gain, grad, width):
    weighted = grad * gain
    inner = lax.psum(jnp.sum(weighted * value, axis=1), "col")
    d_value = (
        factor[:, None] * weighted - value * (factor * factor * factor * inner / width)[:, None]
    )
    d_gain = jnp.sum(grad * value * factor[:, None], axis=0)
    return (d_value, d_gain)


def masked_scores(query_block, keys, seq_ids, first, scale):
    size = query_block.shape[0]
    group = keys.shape[0]
    scored = (
        jnp.einsum("qhd,khd->hqk", query_block, keys, preferred_element_type=jnp.float32) * scale
    )
    query_index = first + jnp.arange(size, dtype=jnp.int32)
    key_index = jnp.arange(group, dtype=jnp.int32)
    allowed = (seq_ids[first : first + size][:, None] == seq_ids[None, :group]) & (
        key_index[None, :] <= query_index[:, None]
    )
    return jnp.where(allowed[None, :, :], scored, -1e30)


def own_slice(value, index, axis):
    size = value.shape[axis] // 2
    return lax.dynamic_slice_in_dim(value, index * size, size, axis)


def col_pair(mine, sent, axis):
    received = lax.ppermute(sent, "col", SWAP)
    first = lax.axis_index("col") == 0
    return jnp.where(
        first,
        jnp.concatenate([mine, received], axis=axis),
        jnp.concatenate([received, mine], axis=axis),
    )


def trade(value, split, join):
    col = lax.axis_index("col")
    return col_pair(own_slice(value, col, split), own_slice(value, 1 - col, split), join)


def routed_and_shared(
    tok_dev, capacity, layers, router, expert_weights, shared_own, normed_own, grads_own, chosen
):
    bf16 = jnp.bfloat16
    col_id = lax.axis_index("col")
    own_expert = lax.axis_index("row") * layers + lax.axis_index("exp")
    experts = router.shape[1]
    block, half_width = normed_own.shape
    width = 2 * half_width
    tokens = chosen.shape[0]
    few = min(tok_dev, block)
    slots = -(-min(capacity, few) // 16) * 16
    blocks = tokens // few
    gather_layers = layers
    grads_all = gather(grads_own, gather_layers, 3)
    normed_all = gather(normed_own, gather_layers, 3)

    router_probs = jax.nn.softmax(dot_nn(normed_all, router), axis=1)
    picks = jnp.any(
        chosen[:, :, None] == jnp.arange(experts, dtype=jnp.int32)[None, None, :], axis=1
    )
    selected = jnp.where(picks, router_probs, 0.0)
    selected_total = jnp.sum(selected, axis=1, keepdims=True)
    gates = selected / selected_total
    is_own = jnp.arange(experts, dtype=jnp.int32)[None, :] == own_expert
    own_gate = jnp.sum(jnp.where(is_own, gates, 0.0), axis=1).reshape(blocks, few)
    own_pick = jnp.any(picks & is_own, axis=1).reshape(blocks, few)
    place = jnp.cumsum(own_pick.astype(jnp.int32), axis=1) - 1
    onehot = (place[:, None, :] == jnp.arange(slots, dtype=jnp.int32)[None, :, None]) & own_pick[
        :, None, :
    ]
    slot_gate = jnp.sum(jnp.where(onehot, own_gate[:, None, :], 0.0), axis=2).reshape(-1, 1)
    pick_rows = onehot.astype(bf16)

    def to_slots(value):
        return (
            jnp.einsum(
                "bsi,bid->bsd",
                pick_rows,
                value.reshape(blocks, few, width),
                preferred_element_type=jnp.float32,
            )
            .astype(bf16)
            .reshape(blocks * slots, width)
        )

    def from_slots(value):
        return jnp.einsum(
            "bsi,bsd->bid",
            pick_rows,
            value.reshape(blocks, slots, width),
            preferred_element_type=jnp.float32,
        ).reshape(tokens, width)

    slot_rows = to_slots(normed_all)
    slot_grads = to_slots(grads_all)
    gate_weight, up_weight, down_weight = expert_weights

    def feed_forward(rows, grads, gate_of, gate_w, up_w, down_w):
        gate_pre = dot_nn(rows, gate_w)
        up_pre = dot_nn(rows, up_w)
        sigmoid = jax.nn.sigmoid(gate_pre)
        silu = gate_pre * sigmoid
        hidden = (silu * up_pre).astype(bf16).astype(jnp.float32)
        d_raw = dot_nn(grads, down_w)
        d_gate_of = jnp.sum(d_raw * hidden, axis=1)
        d_hidden = d_raw if gate_of is None else d_raw * gate_of
        hidden = hidden if gate_of is None else hidden * gate_of
        d_up = (d_hidden * silu).astype(bf16)
        d_gate = (d_hidden * up_pre * sigmoid * (1.0 + gate_pre * (1.0 - sigmoid))).astype(bf16)
        return (hidden.astype(bf16), d_gate, d_up, d_gate_of)

    hidden, d_gate, d_up, d_gates_slots = feed_forward(
        slot_rows, slot_grads, slot_gate, gate_weight, up_weight, down_weight
    )
    shared_hidden, d_shared_gate, d_shared_up, _ = feed_forward(
        normed_all, grads_all, None, shared_own[0].T, shared_own[1].T, shared_own[2].T
    )
    d_pair = (dot_nt(d_gate, gate_weight) + dot_nt(d_up, up_weight)).astype(bf16)
    d_normed = scatter(
        (
            from_slots(d_pair)
            + dot_nn(d_shared_gate, shared_own[0])
            + dot_nn(d_shared_up, shared_own[1])
        ).astype(bf16),
        layers,
        4,
    )
    result = dot_nt(hidden, down_weight).astype(bf16)
    branch = scatter(
        (from_slots(result) + dot_nn(shared_hidden, shared_own[2])).astype(bf16), layers, 4
    )
    grad_gate = dot_tn(slot_rows, d_gate)
    grad_up = dot_tn(slot_rows, d_up)
    grad_down = dot_tn(slot_grads, hidden)
    grad_shared = jnp.stack(
        [
            dot_tn(d_shared_gate, normed_all),
            dot_tn(d_shared_up, normed_all),
            dot_tn(shared_hidden, grads_all),
        ]
    )

    d_gates_dense = jnp.sum(
        jnp.where(onehot, d_gates_slots.reshape(blocks, slots, 1), 0.0), axis=1
    ).reshape(experts, block)
    d_gates = lax.psum(
        lax.all_to_all(d_gates_dense, ("row", "exp"), split_axis=0, concat_axis=0, tiled=True), "col"
    ).T

    def own_rows(value):
        return lax.dynamic_slice_in_dim(value, own_expert * block, block, 0)

    own_probs, own_gates, own_total = own_rows(router_probs), own_rows(gates), own_rows(selected_total)
    d_selected = (d_gates - jnp.sum(d_gates * own_gates, axis=1, keepdims=True)) / own_total
    d_router_probs = jnp.where(own_rows(picks), d_selected, 0.0)
    d_logits = own_probs * (
        d_router_probs - jnp.sum(own_probs * d_router_probs, axis=1, keepdims=True)
    )
    router_half = lax.dynamic_slice_in_dim(router, col_id * half_width, half_width, 0)
    grad_router = lax.dot_general(
        normed_own.astype(jnp.float32),
        d_logits,
        (((0,), (0,)), ((), ())),
        precision=lax.Precision.HIGHEST,
        preferred_element_type=jnp.float32,
    )
    d_normed = d_normed + lax.dot_general(
        d_logits,
        router_half.astype(jnp.float32),
        (((1,), (1,)), ((), ())),
        precision=lax.Precision.HIGHEST,
        preferred_element_type=jnp.float32,
    )
    return (d_normed, branch, (grad_gate, grad_up, grad_down, grad_shared, grad_router))


def per_device(
    layer_input,
    lengths,
    routes,
    norm1_gain,
    w_query,
    w_latent,
    latent_gain,
    w_kv,
    w_out,
    norm2_gain,
    shared_gate,
    shared_up,
    shared_down,
    router,
    expert_gate,
    expert_up,
    expert_down,
    cotangent,
):
    row_id = lax.axis_index("row")
    col_id = lax.axis_index("col")
    exp_id = lax.axis_index("exp")
    rows_n, cols_n, exps_n = (lax.axis_size(name) for name in ("row", "col", "exp"))
    experts = rows_n * exps_n
    own_expert = row_id * exps_n + exp_id
    tok_dev = routes.shape[1]
    topk_count = routes.shape[2]
    capacity = max(2, 3 * tok_dev * topk_count // (2 * experts))
    slots = -(-capacity // 16) * 16
    block, half_width = layer_input.shape
    width = half_width * cols_n
    group = block * rows_n
    tokens = group * exps_n
    heads_here = w_kv.shape[1] // (QK_NOPE + V_DIM)
    head_dim = QK_NOPE + ROPE
    scale = 1.0 / math.sqrt(head_dim)
    query_rows = group // 2
    bf16 = jnp.bfloat16

    w_query_own = trade(w_query, 1, 0)
    w_latent_all = lax.all_gather(w_latent[0].T, ("col", "row"), axis=1, tiled=True)
    w_out_own = trade(w_out, 0, 1)
    units = shared_gate.shape[1] // (cols_n * exps_n)
    shared_parts = jnp.stack(
        [
            lax.dynamic_index_in_dim(
                part.reshape(cols_n, exps_n, units, half_width), exp_id, 1, keepdims=False
            )
            for part in (shared_gate.T, shared_up.T, shared_down)
        ]
    )
    shared_own = trade(shared_parts, 1, 3)[:, 0]

    chosen_all = lax.all_gather(routes[0], ("row", "exp", "col"), axis=0, tiled=True)

    seq_ids, places = sequence_layout(lengths[0], group)
    cosine, sine = rotary_tables(places)

    group_input = gather(layer_input, 1, 1).astype(jnp.float32)
    factor_group = lax.rsqrt(jnp.mean(group_input * group_input, axis=1) + epsilon)
    normed_group = (group_input * factor_group[:, None] * norm1_gain).astype(bf16)
    query_pre = dot_nn(normed_group, w_query_own).reshape(group, heads_here, head_dim)
    queries = jnp.concatenate(
        [
            query_pre[..., :QK_NOPE],
            rotate(query_pre[..., QK_NOPE:], cosine[:, None, :], sine[:, None, :]),
        ],
        axis=2,
    ).astype(bf16)
    latent = dot_nt(normed_group, w_latent_all)
    compressed_raw = latent[:, :KV_RANK]
    kv_factor = lax.rsqrt(jnp.mean(compressed_raw * compressed_raw, axis=1) + epsilon)
    compressed = (compressed_raw * kv_factor[:, None] * latent_gain).astype(bf16)
    rotary_key = rotate(latent[:, KV_RANK:], cosine, sine).astype(bf16)
    key_value = (
        dot_nn(compressed, w_kv).astype(bf16).reshape(group, heads_here, QK_NOPE + V_DIM)
    )
    keys = jnp.concatenate(
        [
            key_value[..., :QK_NOPE],
            jnp.broadcast_to(rotary_key[:, None, :], (group, heads_here, ROPE)),
        ],
        axis=2,
    )
    values = key_value[..., QK_NOPE:]
    block_outputs = []
    block_totals = []
    for first in range(0, group, query_rows):
        last = first + query_rows
        scores = masked_scores(queries[first:last], keys[:last], seq_ids, first, scale)
        highest = jnp.max(scores, axis=2, keepdims=True)
        log_total = highest + jnp.log(jnp.sum(jnp.exp(scores - highest), axis=2, keepdims=True))
        probs_low = jnp.exp(scores - log_total).astype(bf16)
        block_outputs.append(
            jnp.einsum(
                "hqk,khd->qhd", probs_low, values[:last], preferred_element_type=jnp.float32
            ).astype(bf16)
        )
        block_totals.append(log_total)
    attended = jnp.concatenate(block_outputs, axis=0).reshape(group, heads_here * V_DIM)

    input_wide = layer_input.astype(jnp.float32)
    hidden_state = input_wide + scatter(dot_nn(attended, w_out_own).astype(bf16), 1, 2)
    gain_two = lax.dynamic_slice_in_dim(norm2_gain, col_id * half_width, half_width)
    square = lax.psum(jnp.sum(hidden_state * hidden_state, axis=1), "col")
    factor_two = lax.rsqrt(square / width + epsilon)
    normed_two = (hidden_state * factor_two[:, None] * gain_two).astype(bf16)
    pieces = max(1, exps_n // 4)
    feed = functools.partial(
        routed_and_shared,
        tok_dev,
        capacity,
        exps_n,
        router,
        (expert_gate[0], expert_up[0], expert_down[0]),
        shared_own,
    )
    if pieces == 1:
        d_normed, branch, weight_grads = feed(normed_two, cotangent, chosen_all)
    else:
        piece_rows = block // pieces

        def one_piece(total, items):
            d_rows, branch_rows, grads = feed(*items)
            return (jax.tree.map(jnp.add, total, grads), (d_rows, branch_rows))

        split = lambda value: value.reshape(pieces, piece_rows, half_width)
        chosen_pieces = chosen_all.reshape(experts, pieces, piece_rows, topk_count)
        items = (
            split(normed_two),
            split(cotangent),
            chosen_pieces.transpose(1, 0, 2, 3).reshape(pieces, -1, topk_count),
        )
        shapes = jax.eval_shape(lambda: feed(*(item[0] for item in items))[2])
        start = jax.tree.map(lambda leaf: jnp.zeros(leaf.shape, leaf.dtype), shapes)
        weight_grads, (d_normed, branch) = lax.scan(one_piece, start, items)
        d_normed, branch = (v.reshape(block, half_width) for v in (d_normed, branch))
    grad_gate, grad_up, grad_down, grad_shared, grad_router = weight_grads
    output = (hidden_state + branch).astype(bf16)
    grad_shared = trade(grad_shared.astype(bf16)[:, None], 3, 1)
    grad_shared = lax.all_gather(grad_shared, "exp", axis=2, tiled=False)
    grad_shared = grad_shared.reshape(3, cols_n * exps_n * units, half_width).astype(jnp.float32)
    d_norm_two, grad_gain_two = norm_back(hidden_state, factor_two, gain_two, d_normed, width)
    d_hidden_state = cotangent.astype(jnp.float32) + d_norm_two

    d_branch = gather(d_hidden_state.astype(bf16), 1, 1)
    grad_w_out = dot_tn(attended, d_branch)
    d_attended = dot_nt(d_branch, w_out_own).astype(bf16).reshape(group, heads_here, V_DIM)
    d_query_blocks = []
    d_keys = jnp.zeros((group, heads_here, head_dim), jnp.float32)
    d_values = jnp.zeros((group, heads_here, V_DIM), jnp.float32)
    for number, first in enumerate(range(0, group, query_rows)):
        last = first + query_rows
        query_block = queries[first:last]
        d_block = d_attended[first:last]
        scores = masked_scores(query_block, keys[:last], seq_ids, first, scale)
        probs = jnp.exp(scores - block_totals[number])
        d_probs = jnp.einsum(
            "qhd,khd->hqk", d_block, values[:last], preferred_element_type=jnp.float32
        )
        delta = jnp.sum(probs * d_probs, axis=2, keepdims=True)
        d_scores = (probs * (d_probs - delta)).astype(bf16)
        d_query_blocks.append(
            jnp.einsum("hqk,khd->qhd", d_scores, keys[:last], preferred_element_type=jnp.float32)
            * scale
        )
        d_keys = d_keys.at[:last].add(
            jnp.einsum("hqk,qhd->khd", d_scores, query_block, preferred_element_type=jnp.float32)
            * scale
        )
        d_values = d_values.at[:last].add(
            jnp.einsum(
                "hqk,qhd->khd", probs.astype(bf16), d_block, preferred_element_type=jnp.float32
            )
        )
    d_query = jnp.concatenate(d_query_blocks, axis=0)
    d_query_pre = (
        jnp.concatenate(
            [
                d_query[..., :QK_NOPE],
                unrotate(d_query[..., QK_NOPE:], cosine[:, None, :], sine[:, None, :]),
            ],
            axis=2,
        )
        .astype(bf16)
        .reshape(group, heads_here * head_dim)
    )
    d_key_value = (
        jnp.concatenate([d_keys[..., :QK_NOPE], d_values], axis=2)
        .astype(bf16)
        .reshape(group, heads_here * (QK_NOPE + V_DIM))
    )
    grad_w_kv = dot_tn(compressed, d_key_value)
    d_latent_sum = lax.psum(
        jnp.concatenate(
            [dot_nt(d_key_value, w_kv), jnp.sum(d_keys[..., QK_NOPE:], axis=1)], axis=1
        ).astype(bf16),
        ("row", "col"),
    ).astype(jnp.float32)
    d_compressed = d_latent_sum[:, :KV_RANK]
    weighted = d_compressed * latent_gain
    grad_latent_gain = jnp.sum(d_compressed * compressed_raw * kv_factor[:, None], axis=0)
    inner = jnp.sum(weighted * compressed_raw, axis=1)
    d_raw = (
        kv_factor[:, None] * weighted
        - compressed_raw * (kv_factor * kv_factor * kv_factor * inner / KV_RANK)[:, None]
    )
    d_latent = jnp.concatenate(
        [d_raw, unrotate(d_latent_sum[:, KV_RANK:], cosine, sine)], axis=1
    ).astype(bf16)
    slab = w_latent.shape[1]
    slab_start = col_id * half_width + row_id * slab
    normed_slab = lax.dynamic_slice_in_dim(normed_group, slab_start, slab, 1)
    grad_w_latent = dot_tn(d_latent, normed_slab)
    grad_w_query = dot_tn(normed_group, d_query_pre)
    d_gathered = dot_nt(d_query_pre, w_query_own)
    piece = lax.dynamic_slice_in_dim(d_gathered, slab_start, slab, 1) + dot_nt(
        d_latent, w_latent[0]
    )
    d_gathered = lax.dynamic_update_slice_in_dim(d_gathered, piece, slab_start, 1)
    d_first = scatter(d_gathered.astype(bf16), 1, 2)
    gain_one = lax.dynamic_slice_in_dim(norm1_gain, col_id * half_width, half_width)
    factor_one = lax.dynamic_slice_in_dim(factor_group, row_id * block, block)
    d_norm_one, grad_gain_one = norm_back(input_wide, factor_one, gain_one, d_first, width)
    input_grad = d_hidden_state + d_norm_one

    latent_share = grad_latent_gain / (rows_n * cols_n)
    small = jnp.concatenate(
        [grad_gain_one[None], grad_gain_two[None], grad_router.T], axis=0
    )
    small = lax.psum(small, ("row", "exp"))
    small = lax.all_gather(small, "col", axis=1, tiled=True)
    summed_latent_gain = lax.psum(latent_share, ("row", "col", "exp"))

    summed = lax.psum(
        tuple(g.astype(bf16) for g in (grad_w_query, grad_w_latent, grad_w_kv, grad_w_out)), "exp"
    )
    out_w_query = trade(summed[0], 0, 1).astype(jnp.float32)
    out_w_out = trade(summed[3], 1, 0).astype(jnp.float32)
    return (
        output,
        input_grad,
        small[0],
        out_w_query,
        summed[1].T.astype(jnp.float32)[None],
        summed_latent_gain,
        summed[2].astype(jnp.float32),
        out_w_out,
        small[1],
        grad_shared[0].T,
        grad_shared[1].T,
        grad_shared[2],
        small[2:].T,
        grad_gate[None],
        grad_up[None],
        grad_down[None],
    )


def solution(mesh):
    placed = (
        P(("row", "exp"), "col"),
        P("exp", None),
        P("col", ("row", "exp"), None),
        P(),
        P("col", "row"),
        P("col", "row", None),
        P(),
        P(None, ("row", "col")),
        P("row", "col"),
        P(),
        P("col", "row"),
        P("col", "row"),
        P("row", "col"),
        P(),
        P(("row", "exp"), None, "col"),
        P(("row", "exp"), None, "col"),
        P(("row", "exp"), None, "col"),
        P(("row", "exp"), "col"),
    )
    return jax.shard_map(
        per_device,
        mesh=mesh,
        in_specs=placed,
        out_specs=(
            P(("row", "exp"), "col"),
            P(("row", "exp"), "col"),
            P(),
            P("col", "row"),
            P("col", "row", None),
            P(),
            P(None, ("row", "col")),
            P("row", "col"),
            P(),
            P("col", "row"),
            P("col", "row"),
            P("row", "col"),
            P(),
            P(("row", "exp"), None, "col"),
            P(("row", "exp"), None, "col"),
            P(("row", "exp"), None, "col"),
        ),
        check_vma=False,
    )
```

time: 2620 us -> 1390 us (0.53)
  waiting for transfers between devices: 1660 us -> 108 us
  Pallas kernels: 0 us -> 517 us
  local copies, waits for them, and re-layouts: 263 us -> 37.6 us
  matrix products: 277 us -> 412 us
  other arithmetic: 124 us -> 76.3 us
  blocking collectives: 239 us -> 205 us
    pallas_call x0 -> x8, Pallas kernels: none -> 517 us  [the longest x4 279 us: scatter(): pl.pallas_call(functools.partial(scatter_body, layers), out_shape=jax.Sha...]
    reduce_scatter x11 -> x0, waiting for transfers between devices: 507 us -> none  [the longest x2 271 us: expert_sums(): lax.psum_scatter(value.astype(jnp.bfloat16), 'col', scatter_dimension=0,...]
    all_gather x11 -> x2, waiting for transfers between devices: 430 us -> 44.1 us  [the longest x1 44.1 us: per_device(): grad_shared = lax.all_gather(grad_shared, 'exp', axis=2, tiled=False)]
    psum x4 -> x3, waiting for transfers between devices: 389 us -> 42.4 us  [the longest x1 42.4 us: per_device(): lax.psum(jnp.concatenate([dot_nt(d_key_value, w_kv), jnp.sum(d_keys[...,...]
    all_to_all x6 -> x1, waiting for transfers between devices: 335 us -> 0.01 us  [routed_and_shared(): lax.all_to_all(d_gates_dense, ('row', 'exp'), split_axis=0, concat_axis=0...]
    all_to_all x2 -> x0, blocking collectives: 165 us -> none  [the longest x1 144 us: expert_swap(): lax.all_to_all(value, ('row', 'exp'), split_axis=0, concat_axis=0, tiled=...]
    dot_general x22 -> x27, matrix products: 119 us -> 260 us  [the longest x13 180 us: dot_nn(): return jnp.dot(left, right, preferred_element_type=jnp.float32)]
    all_gather x0 -> x2, blocking collectives: none -> 136 us  [the longest x1 131 us: per_device(): lax.all_gather(routes[0], ('row', 'exp', 'col'), axis=0, tiled=True)]
  transfers between devices with their start and end apart: 32 -> 12, of which waited for: 27 -> 4; matrix products, arithmetic and copies ran while one was open for 15% -> 27% of each run, Pallas kernels for 0% -> 29%
where the time goes in v1:
time: 1390 us; the launch traced here: 1380 us
  Pallas kernels  517 us (37%)
  matrix products  412 us (30%)
  blocking collectives  205 us (15%)
  waiting for transfers between devices  108 us (8%)
  other arithmetic  76.3 us (5%)
  local copies, waits for them, and re-layouts  37.6 us (3%)
  between operations  15.5 us (1%)
    pallas_call x4, Pallas kernels, scatter(): pl.pallas_call(functools.partial(scatter_body, layers), out_shape=jax.Sha...  279 us
    pallas_call x4, Pallas kernels, gather(): pl.pallas_call(functools.partial(gather_body, layers), out_shape=jax.Shap...  238 us
    dot_general x13, matrix products, dot_nn(): return jnp.dot(left, right, preferred_element_type=jnp.float32)  180 us
    all_gather x1, blocking collectives, per_device(): lax.all_gather(routes[0], ('row', 'exp', 'col'), axis=0, tiled=True)  131 us
    dot_general x10, matrix products, dot_tn(): lax.dot_general(left, right, (((0,), (0,)), ((), ())), preferred_element_...  82.5 us
    dot_general x8, matrix products, dot_nt(): lax.dot_general(left, right, (((1,), (1,)), ((), ())), preferred_element_...  65.1 us
    psum x1, blocking collectives, per_device(): summed_latent_gain = lax.psum(latent_share, ('row', 'col', 'exp'))  46 us
    all_gather x1, waiting for transfers between devices, per_device(): grad_shared = lax.all_gather(grad_shared, 'exp', axis=2, tiled=False)  44.1 us
  transfers between devices with their start and end apart: 12, of which 4 were waited for; matrix products, arithmetic and copies ran while one was open for 27% of the time, Pallas kernels for 29%

profile of v1, /device:TPU:0, one launch (start us, length us, event | category | flops | bytes accessed | tf_op | source)
XLA Modules:
  0.0 1384.7 jit_solution(2937230572331954382)
XLA Ops:
  22.9 130.7 %all-gather = s32[1,5120,6]{2,0,1:T(1,128)} all-gather(s32[1,160,6]{2,0,1:T(1,128)S(1)} %copy.75), channel_id=2, replica_groups=mesh['row'=4,'col'=2,'exp'=4] {'row','exp','col'}, dimensions={1}, use_global_device_ids=true | all-gather | bytes 126720 | tf_op jit(solution)/shard_map/all_gather | solution.py:789
  157.5 27.1 %shard_map.307 = bf16[1280,2048]{1,0:T(8,128)(2,1)} custom-call(bf16[320,1024]{1,0:T(8,128)(2,1)} %src.2), custom_call_target="tpu_custom_call" | custom-call | tf_op jit(solution)/shard_map/pallas_call | solution.py:235
  188.4 93.4 %shard_map.311 = bf16[5120,2048]{1,0:T(8,128)(2,1)} custom-call(bf16[320,1024]{1,0:T(8,128)(2,1)} %src.3), custom_call_target="tpu_custom_call" | custom-call | tf_op jit(solution)/shard_map/pallas_call | solution.py:235
  338.8 29.3 %shard_map.308 = f32[320,1024]{1,0:T(8,128)} custom-call(bf16[1280,2048]{1,0:T(8,128)(2,1)} %convolution_convert_fusion.1.src), custom_call_target="tpu_custom_call" | custom-call | tf_op jit(solution)/shard_map/pallas_call | solution.py:475
  378.0 92.1 %shard_map.309 = bf16[5120,2048]{1,0:T(8,128)(2,1)} custom-call(bf16[320,1024]{1,0:T(8,128)(2,1)} %multiply_convert_fusion.9.src), custom_call_target="tpu_custom_call" | custom-call | tf_op jit(solution)/shard_map/pallas_call | solution.py:235
  514.2 16.2 %fusion.82 = f32[5120,2048]{1,0:T(8,128)} fusion(bf16[5120,88]{0,1:T(8,128)(2,1)S(1)} %get-tuple-element.108, bf16[3,1,88,2048]{3,2,1,0:T(8,128)(2,1)S(1)} %copy-done.15), kind=kOutput, calls=%fused_computation.187 | convolution fusion | flops 1845493760 | bytes 43204608 | tf_op jit(solution)/shard_map/dot_general | solution.py:506
  554.6 15.4 %fusion.23 = f32[3072,704]{0,1:T(8,128)} fusion(bf16[3072,2048]{1,0:T(8,128)(2,1)} %bitcast.226, bf16[1,2048,704]{1,2,0:T(8,128)(2,1)} %param.45), kind=kOutput, calls=%fused_computation.51 | convolution fusion | flops 8858370048 | bytes 24117248 | tf_op jit(solution)/shard_map/dot_general | solution.py:506
  570.0 15.2 %fusion.27 = f32[3072,704]{0,1:T(8,128)} fusion(bf16[3072,2048]{1,0:T(8,128)(2,1)} %bitcast.227, bf16[1,2048,704]{1,2,0:T(8,128)(2,1)} %param.44), kind=kOutput, calls=%fused_computation.55 | convolution fusion | flops 8858370048 | bytes 24117248 | tf_op jit(solution)/shard_map/dot_general | solution.py:506
  600.4 20.1 %fusion.7 = (f32[3072]{0:T(1024)S(1)}, bf16[3072,704]{0,1:T(8,128)(2,1)}, f32[3072,704]{0,1:T(8,128)}) fusion(f32[3072,704]{0,1:T(8,128)} %fusion.23, f32[3072,704]{0,1:T(8,128)} %fusion.27, bf16[3072,2048]{1,0:T(8,128)(2,1)} %bitcast.224, bf16[1,2048,704]{1,2,0:T(8,128)(2,1)S(1)} %copy-done), kind=kOutput, calls=%fused_computation.15 | convolution fusion | flops 8877831168 | bytes 45756416 | tf_op jit(solution)/shard_map/dot_general | solution.py:506
  668.6 18.5 %add_convert_fusion = bf16[3072,2048]{1,0:T(8,128)(2,1)} fusion(f32[3072,2048]{1,0:T(8,128)} %fusion.25, bf16[3072,704]{0,1:T(8,128)(2,1)} %get-tuple-element.102, bf16[1,2048,704]{1,2,0:T(8,128)(2,1)S(1)} %copy-done.97), kind=kOutput, calls=%fused_computation.5 | convolution fusion | flops 8870952960 | bytes 44957696 | tf_op jit(solution)/shard_map/dot_general | solution.py:510
  687.1 20.3 %fusion.31 = f32[32,160,2048]{2,1,0:T(8,128)} fusion(bf16[32,96,2048]{2,1,0:T(8,128)(2,1)} %bitcast.223, s32[32,160]{1,0:T(8,128)S(1)} %slice_add_fusion, pred[32,160]{1,0:T(8,128)(4,1)S(1)} %reshape.601), kind=kOutput, calls=%fused_computation.69 | convolution fusion | flops 2014248960 | bytes 54551552 | tf_op jit(solution)/shard_map/bsi,bsd->bid/dot_general | solution.py:645
  707.4 34.7 %fusion.1.src = bf16[5120,2048]{1,0:T(8,128)(2,1)} fusion(f32[5120,2048]{1,0:T(8,128)} %fusion.82, f32[32,160,2048]{2,1,0:T(8,128)} %fusion.31, bf16[5120,88]{0,1:T(8,128)(2,1)S(1)} %copy-done.24, bf16[3,1,88,2048]{3,2,1,0:T(8,128)(2,1)} %maximum_select_fusion.2), kind=kOutput, calls=%fused_computation.2 | convolution fusion | flops 1876951040 | bytes 106119168 | tf_op jit(solution)/shard_map/dot_general | solution.py:506
  742.2 20.2 %fusion.34 = f32[32,160,2048]{2,1,0:T(8,128)} fusion(bf16[32,96,2048]{2,1,0:T(8,128)(2,1)} %bitcast.222, s32[32,160]{1,0:T(8,128)S(1)} %slice_add_fusion, pred[32,160]{1,0:T(8,128)(4,1)S(1)} %reshape.601), kind=kOutput, calls=%fused_computation.70 | convolution fusion | flops 2014248960 | bytes 54551552 | tf_op jit(solution)/shard_map/bsi,bsd->bid/dot_general | solution.py:645
  763.2 96.2 %shard_map.312 = f32[320,1024]{1,0:T(8,128)} custom-call(bf16[5120,2048]{1,0:T(8,128)(2,1)} %fusion.1.src), custom_call_target="tpu_custom_call" | custom-call | tf_op jit(solution)/shard_map/pallas_call | solution.py:475
  879.0 25.7 %shard_map.313 = bf16[1280,2048]{1,0:T(8,128)(2,1)} custom-call(bf16[320,1024]{1,0:T(8,128)(2,1)} %fusion.134.src), custom_call_target="tpu_custom_call" | custom-call | tf_op jit(solution)/shard_map/pallas_call | solution.py:235
  948.2 42.4 %all-reduce.8.cloned.1.call-done = bf16[1280,576]{0,1:T(8,128)(2,1)} async-done(((bf16[1280,576]{0,1:T(8,128)(2,1)}), bf16[1280,576]{0,1:T(8,128)(2,1)}) %all-reduce.8.cloned.1.call-update) | async-done | bytes 1474576 | tf_op jit(solution)/shard_map/psum | solution.py:929
  1005.6 30.2 %shard_map.314 = f32[320,1024]{1,0:T(8,128)} custom-call(bf16[1280,2048]{1,0:T(8,128)(2,1)} %convert_element_type.209.src), custom_call_target="tpu_custom_call" | custom-call | tf_op jit(solution)/shard_map/pallas_call | solution.py:475
  1041.8 21.7 %fusion.2.src = bf16[5120,2048]{1,0:T(8,128)(2,1)} fusion(f32[32,160,2048]{2,1,0:T(8,128)} %fusion.34, bf16[5120,88]{0,1:T(8,128)(2,1)S(1)} %copy-done.22, bf16[3,1,88,2048]{3,2,1,0:T(8,128)(2,1)} %maximum_select_fusion.2), kind=kOutput, calls=%fused_computation.4 | convolution fusion | flops 1866465280 | bytes 64176128 | tf_op jit(solution)/shard_map/dot_general | solution.py:506
  1063.5 14.9 %convolution_bitcast_fusion.1 = f32[1,2048,704]{1,2,0:T(8,128)} fusion(bf16[3072,704]{0,1:T(8,128)(2,1)} %get-tuple-element.102, bf16[3072,2048]{1,0:T(8,128)(2,1)} %bitcast.228), kind=kOutput, calls=%fused_computation.33 | convolution fusion | flops 8858370048 | bytes 22675456 | tf_op jit(solution)/shard_map/dot_general | solution.py:516
  1078.4 123.1 %shard_map.310 = f32[320,1024]{1,0:T(8,128)} custom-call(bf16[5120,2048]{1,0:T(8,128)(2,1)} %fusion.2.src), custom_call_target="tpu_custom_call" | custom-call | tf_op jit(solution)/shard_map/pallas_call | solution.py:475
  1204.2 15.1 %convolution_bitcast_fusion.2 = f32[1,2048,704]{1,2,0:T(8,128)} fusion(bf16[3072,704]{0,1:T(8,128)(2,1)} %copy-done.25, bf16[3072,2048]{1,0:T(8,128)(2,1)} %bitcast.229), kind=kOutput, calls=%fused_computation.34 | convolution fusion | flops 8858370048 | bytes 22675456 | tf_op jit(solution)/shard_map/dot_general | solution.py:516
  1219.3 15.0 %fusion.13 = f32[1,2048,704]{1,2,0:T(8,128)} fusion(bf16[3072,2048]{1,0:T(8,128)(2,1)} %bitcast.225, bf16[3072,704]{0,1:T(8,128)(2,1)} %get-tuple-element.99, f32[3072]{0:T(1024)S(1)} %copy-done.76), kind=kOutput, calls=%fused_computation.32 | convolution fusion | flops 8864858112 | bytes 22687744 | tf_op jit(solution)/shard_map/dot_general | solution.py:516
  1234.3 46.0 %psum.85 = f32[512]{0:T(512)} all-reduce(f32[512]{0:T(512)S(1)} %broadcast_multiply_fusion), channel_id=1, replica_groups=mesh['row'=4,'col'=2,'exp'=4] {'row','col','exp'}, use_global_device_ids=true, to_apply=%region_40.41 | all-reduce | flops 512 | bytes 4096 | tf_op jit(solution)/shard_map/psum | solution.py:968
  1327.6 44.1 %all-gather.6.cloned.1.call-done = bf16[3,2,4,88,1024]{4,3,2,1,0:T(8,128)(2,1)} async-done(((bf16[3,2,1,88,1024]{4,3,2,1,0:T(8,128)(2,1)}), bf16[3,2,4,88,1024]{4,3,2,1,0:T(8,128)(2,1)}) %all-gather.6.cloned.1.call-update) | async-done | bytes 4325392 | tf_op jit(solution)/shard_map/all_gather | solution.py:876
  (395 shorter events, 361.6 us)
Async XLA Ops:
  7.2 593.2 %copy-start = (bf16[1,2048,704]{1,2,0:T(8,128)(2,1)S(1)}, bf16[1,2048,704]{1,2,0:T(8,128)(2,1)}, u32[]{:S(2)}) copy-start(bf16[1,2048,704]{1,2,0:T(8,128)(2,1)} %param.46) | copy-start | bytes 8650756
  7.2 304.7 %all-gather.4.cloned.1.call-start = ((), (), s32[]{:S(2)}) async-start(), calls=%async_computation.1 | async-start | bytes 2654208 | tf_op jit(solution)/shard_map/all_gather | solution.py:776
  11.4 290.1 %collective-permute-start.2 = (bf16[3,1,88,1024]{3,2,1,0:T(8,128)(2,1)}, bf16[3,1,88,1024]{3,2,1,0:T(8,128)(2,1)}, u32[]{:S(2)}, u32[]{:S(2)}) collective-permute-start(bf16[3,1,88,1024]{3,2,1,0:T(8,128)(2,1)} %get-tuple-element.126), channel_id=1, source_target_pairs={{0,4},{4,0},{1,5},{5,1},{2,6},{6,2},{3,7},{7,3},{8,12},{12,8},{9,1... | collective-permute-start | bytes 1622024 | tf_op jit(solution)/shard_map/ppermute | solution.py:584
  16.6 316.1 %collective-permute-start.1 = (bf16[256,1024]{1,0:T(8,128)(2,1)}, bf16[256,1024]{1,0:T(8,128)(2,1)}, u32[]{:S(2)}, u32[]{:S(2)}) collective-permute-start(bf16[256,1024]{1,0:T(8,128)(2,1)} %get-tuple-element.130), channel_id=1, source_target_pairs={{0,4},{4,0},{1,5},{5,1},{2,6},{6,2},{3,7},{7,3},{8,12},{12,8},{9,1... | collective-permute-start | bytes 1572872 | tf_op jit(solution)/shard_map/ppermute | solution.py:584
  19.3 285.1 %collective-permute-start = (bf16[1024,384]{1,0:T(8,128)(2,1)}, bf16[1024,384]{1,0:T(8,128)(2,1)}, u32[]{:S(2)}, u32[]{:S(2)}) collective-permute-start(bf16[1024,384]{1,0:T(8,128)(2,1)} %get-tuple-element.119), channel_id=1, source_target_pairs={{0,4},{4,0},{1,5},{5,1},{2,6},{6,2},{3,7},{7,3},{8,12},{12,8},{9,1... | collective-permute-start | bytes 2359304 | tf_op jit(solution)/shard_map/ppermute | solution.py:584
  21.7 298.1 %copy-start.65 = (f32[1280]{0:T(1024)}, f32[1280]{0:T(1024)S(1)}, u32[]{:S(2)}) copy-start(f32[1280]{0:T(1024)S(1)} %subtract_convert_fusion.3) | copy-start | bytes 15364
  156.4 384.2 %copy-start.43 = (pred[5120,16]{0,1:T(8,128)(4,1)}, pred[5120,16]{0,1:T(8,128)(4,1)S(1)}, u32[]{:S(2)}) copy-start(pred[5120,16]{0,1:T(8,128)(4,1)S(1)} %fusion.42) | copy-start | bytes 245764
  184.6 97.2 %slice-start.7 = ((s8[5242880]{0:T(1024)(128)(4,1)}), s8[4194304]{0:T(1024)(128)(4,1)S(1)}, s32[]{:S(2)}) async-start(s8[5242880]{0:T(1024)(128)(4,1)} %bitcast.220), calls=%async_computation.13 | async-start | bytes 8388608
  188.4 110.7 %copy-start.71 = (f32[1280]{0:T(1024)}, f32[1280]{0:T(1024)S(1)}, u32[]{:S(2)}) copy-start(f32[1280]{0:T(1024)S(1)} %add_rsqrt_fusion.1) | copy-start | bytes 15364
  375.7 94.4 %copy-start.72 = (f32[320]{0:T(512)}, f32[320]{0:T(512)S(1)}, u32[]{:S(2)}) copy-start(f32[320]{0:T(512)S(1)} %add_rsqrt_fusion.2) | copy-start | bytes 3844
  599.6 601.9 %collective-permute-start.5 = (bf16[3,1,88,1024]{3,2,0,1:T(8,128)(2,1)}, bf16[3,1,88,1024]{3,2,0,1:T(8,128)(2,1)}, u32[]{:S(2)}, u32[]{:S(2)}) collective-permute-start(bf16[3,1,88,1024]{3,2,0,1:T(8,128)(2,1)} %get-tuple-element.124), channel_id=1, source_target_pairs={{0,4},{4,0},{1,5},{5,1},{2,6},{6,2},{3,7},{7,3},{8,12},{12,8},{9,1... | collective-permute-start | bytes 1622024 | tf_op jit(solution)/shard_map/ppermute | solution.py:584
  625.5 233.9 %all-to-all-start = ((f32[16,1,320]{2,1,0:T(1,128)}), f32[16,1,320]{2,1,0:T(1,128)}, u32[]{:S(2)}, u32[]{:S(2)}) async-start(f32[16,1,320]{2,1,0:T(1,128)} %all_to_all.8), calls=%async_computation | async-start | bytes 49152 | tf_op jit(solution)/shard_map/all_to_all | solution.py:705
  629.6 360.9 %all-reduce.8.cloned.1.call-start = ((), (), s32[]{:S(2)}) async-start(), calls=%async_computation.2 | async-start | bytes 2949120 | tf_op jit(solution)/shard_map/psum | solution.py:929
  763.1 106.6 %copy-start.4 = (f32[320,1024]{1,0:T(8,128)S(1)}, f32[320,1024]{1,0:T(8,128)}, u32[]{:S(2)}) copy-start(f32[320,1024]{1,0:T(8,128)} %get-tuple-element.101) | copy-start | bytes 3932164
  763.1 106.6 %copy-start.60 = (bf16[2048,16]{0,1:T(8,128)(2,1)S(1)}, bf16[2048,16]{0,1:T(8,128)(2,1)}, u32[]{:S(2)}) copy-start(bf16[2048,16]{0,1:T(8,128)(2,1)} %param.43) | copy-start | bytes 196612
  763.1 106.6 %copy-start.62 = (f32[1024]{0:T(1024)S(1)}, f32[1024]{0:T(1024)}, u32[]{:S(2)}) copy-start(f32[1024]{0:T(1024)} %copy-done.61) | copy-start | bytes 12292
  763.1 106.6 %copy-start.73 = (f32[320]{0:T(512)S(1)}, f32[320]{0:T(512)}, u32[]{:S(2)}) copy-start(f32[320]{0:T(512)} %copy-done.72) | copy-start | bytes 3844
  932.5 357.8 %all-reduce.10.cloned.1.call-start = ((), (), s32[]{:S(2)}) async-start(), calls=%async_computation.3 | async-start | bytes 196608 | tf_op jit(solution)/shard_map/psum | solution.py:966
  1038.2 257.7 %all-reduce.12.cloned.1.call-start = ((), (), s32[]{:S(2)}) async-start(), calls=%async_computation.5 | async-start | bytes 6881280 | tf_op jit(solution)/shard_map/psum | solution.py:970
  1040.6 331.1 %all-gather.6.cloned.1.call-start = ((), (), s32[]{:S(2)}) async-start(), calls=%async_computation.4 | async-start | bytes 5406720 | tf_op jit(solution)/shard_map/all_gather | solution.py:876
  1078.4 123.1 %copy-start.39 = (bf16[3,1,1,88,1024]{4,3,0,2,1:T(8,128)(2,1)S(1)}, bf16[3,1,1,88,1024]{4,3,0,2,1:T(8,128)(2,1)}, u32[]{:S(2)}) copy-start(bf16[3,1,1,88,1024]{4,3,0,2,1:T(8,128)(2,1)} %get-tuple-element.122) | copy-start | bytes 1622020
  1078.4 123.1 %copy-start.40 = (bf16[3,1,1,88,1024]{4,3,2,1,0:T(8,128)(2,1)S(1)}, bf16[3,1,1,88,1024]{4,3,2,1,0:T(8,128)(2,1)}, u32[]{:S(2)}) copy-start(bf16[3,1,1,88,1024]{4,3,2,1,0:T(8,128)(2,1)} %get-tuple-element.123) | copy-start | bytes 1622020
  1297.4 14.9 %collective-permute-start.4 = (bf16[256,1024]{1,0:T(8,128)(2,1)S(1)}, bf16[256,1024]{1,0:T(8,128)(2,1)S(1)}, u32[]{:S(2)}, u32[]{:S(2)}) collective-permute-start(bf16[256,1024]{1,0:T(8,128)(2,1)S(1)} %get-tuple-element.128), channel_id=1, source_target_pairs={{0,4},{4,0},{1,5},{5,1},{2,6},{6,2},{3,7},{7,3},{8,12},{12,8},{9,1... | collective-permute-start | bytes 1572872 | tf_op jit(solution)/shard_map/ppermute | solution.py:584
  1299.7 26.0 %collective-permute-start.3 = (bf16[1024,384]{1,0:T(8,128)(2,1)S(1)}, bf16[1024,384]{1,0:T(8,128)(2,1)S(1)}, u32[]{:S(2)}, u32[]{:S(2)}) collective-permute-start(bf16[1024,384]{1,0:T(8,128)(2,1)S(1)} %get-tuple-element.117), channel_id=1, source_target_pairs={{0,4},{4,0},{1,5},{5,1},{2,6},{6,2},{3,7},{7,3},{8,12},{12,8},{9,1... | collective-permute-start | bytes 2359304 | tf_op jit(solution)/shard_map/ppermute | solution.py:584
  (99 other events, 1622.4 us)
Sparse Core Ops, SparseCore 0:
  9.9 43.5 all-gather.3
  932.6 57.9 all-reduce.7
  1038.3 86.9 all-reduce.9
  1128.9 158.8 all-reduce.11
  1289.8 81.8 all-gather.5

commit v2 on v1

--- a/solution.py
+++ b/solution.py
@@ -66,8 +66,18 @@
     return (rows // 2 + 15) // 16 * 16
 
 
+def piece_of(where, layers, shape, by_rows, row, col, layer, span=None):
+    rows, width = shape
+    start, size = (0, rows) if span is None else span
+    if by_rows:
+        first = pl.multiple_of((row * 2 + col) * rows + start, 16)
+        return where.at[pl.ds(first, size)]
+    first = pl.multiple_of((row * layers + layer) * rows + start, 16)
+    return where.at[pl.ds(first, size), pl.ds(pl.multiple_of(col * width, 128), width)]
+
+
 def gather_body(
-    layers, src, out, held, store_sem, up_send, down_send, z_recv, send, recv, diag_send, diag_recv
+    layers, by_rows, src, out, held, store_sem, up_send, down_send, z_recv, send, recv, diag_send, diag_recv
 ):
     me = Place(layers)
     rows, width = src.shape
@@ -82,11 +92,10 @@
     )
     sides = (me.to_x, me.to_y)
 
-    def area(where, row, col, layer, span=(0, rows)):
-        first = pl.multiple_of((row * layers + layer) * rows + span[0], 16)
-        return where.at[pl.ds(first, span[1]), pl.ds(pl.multiple_of(col * width, 128), width)]
-
-    def held_piece(kind, layer, span=(0, rows)):
+    def area(where, row, col, layer, span=None):
+        return piece_of(where, layers, (rows, width), by_rows, row, col, layer, span)
+
+    def held_piece(kind, layer, span=None):
         return area(held, *owners[kind], layer, span)
 
     def partner_piece(where, kind, layer):
@@ -228,12 +237,12 @@
                 along(False, layer).wait_send()
 
 
-def gather(value, layers, collective_id):
+def gather(value, layers, collective_id, by_rows=False):
     rows, width = value.shape
     dma = pltpu.SemaphoreType.DMA
-    whole = (4 * layers * rows, 2 * width)
+    whole = (8 * rows, width) if by_rows else (4 * layers * rows, 2 * width)
     return pl.pallas_call(
-        functools.partial(gather_body, layers),
+        functools.partial(gather_body, layers, by_rows),
         out_shape=jax.ShapeDtypeStruct(whole, value.dtype),
         in_specs=[pl.BlockSpec(memory_space=pl.ANY)],
         out_specs=pl.BlockSpec(memory_space=pl.ANY),
@@ -258,6 +267,7 @@
 
 def scatter_body(
     layers,
+    by_rows,
     src,
     out,
     acc,
@@ -298,8 +308,7 @@
     layer_of = [layer_at(step) for step in range(layers)]
 
     def area(row, col, layer):
-        first = pl.multiple_of((row * layers + layer) * rows, 16)
-        return src.at[pl.ds(first, rows), pl.ds(pl.multiple_of(col * width, 128), width)]
+        return piece_of(src, layers, (rows, width), by_rows, row, col, layer)
 
     def load(step, kind):
         return pltpu.make_async_copy(
@@ -346,7 +355,7 @@
             me.above if up else me.below,
         )
 
-    lanes = 32 if rows % 32 == 0 else 16
+    lanes = 32 if part % 32 == 0 and rows % 32 == 0 else 16
 
     def add(target, others, start=0, size=rows, into=None):
         def step(i, carry):
@@ -467,13 +476,16 @@
                 line(step, False).wait_send()
 
 
-def scatter(value, layers, collective_id):
-    rows, width = value.shape[0] // (4 * layers), value.shape[1] // 2
+def scatter(value, layers, collective_id, by_rows=False):
+    if by_rows:
+        rows, width = value.shape[0] // 8, value.shape[1]
+    else:
+        rows, width = value.shape[0] // (4 * layers), value.shape[1] // 2
     part = first_part(rows)
     dma = pltpu.SemaphoreType.DMA
     buffer = lambda *lead: pltpu.VMEM((*lead, rows, width), value.dtype)
     return pl.pallas_call(
-        functools.partial(scatter_body, layers),
+        functools.partial(scatter_body, layers, by_rows),
         out_shape=jax.ShapeDtypeStruct((rows, width), jnp.float32),
         in_specs=[pl.BlockSpec(memory_space=pl.ANY)],
         out_specs=pl.BlockSpec(memory_space=pltpu.VMEM),
@@ -518,6 +530,271 @@
     )
 
 
+def small_sum_body(layers, src, out, core_in, mid, x_in, near, line_in, total, send, recv, line_send, line_recv):
+    me = Place(layers)
+    width = src.shape[1]
+    barrier = pltpu.get_barrier_semaphore()
+    for target in (me.to_x, me.to_y, me.to_core):
+        pl.semaphore_signal(barrier, inc=1, device_id=target, device_id_type=MESH)
+    for step in range(1, layers):
+        other = {"exp": lax.rem(me.layer + step, layers)}
+        pl.semaphore_signal(barrier, inc=1, device_id=other, device_id_type=MESH)
+    pl.semaphore_wait(barrier, 3 + layers - 1)
+    swap = remote(src, core_in, send.at[0], recv.at[0], me.to_core)
+    swap.start()
+    swap.wait()
+    mid[...] = src[...] + core_in[...]
+    swap = remote(mid, x_in, send.at[1], recv.at[1], me.to_x)
+    swap.start()
+    swap.wait()
+    near[...] = mid[...] + x_in[...]
+    line_in[me.layer] = near[...]
+
+    def along(step, incoming):
+        layer = lax.rem(me.layer + (layers - step if incoming else 0), layers)
+        return remote(
+            near,
+            line_in.at[layer],
+            line_send.at[step],
+            line_recv.at[step],
+            {"exp": lax.rem(me.layer + step, layers)},
+        )
+
+    for step in range(1, layers):
+        along(step, False).start()
+    for step in range(1, layers):
+        along(step, True).wait_recv()
+    summed = line_in[0]
+    for layer in range(1, layers):
+        summed = summed + line_in[layer]
+    total[...] = summed
+    mine = pl.ds(pl.multiple_of(me.col * width, 128), width)
+    theirs = pl.ds(pl.multiple_of(me.y_col * width, 128), width)
+    out[:, mine] = summed
+    remote(total, out.at[:, mine], send.at[2], recv.at[2], me.to_y).start()
+    remote(total, out.at[:, theirs], send.at[2], recv.at[2], me.to_y).wait()
+    for step in range(1, layers):
+        along(step, False).wait_send()
+
+
+def small_sum(value, layers, collective_id):
+    rows, width = value.shape
+    dma = pltpu.SemaphoreType.DMA
+    buffer = lambda *lead: pltpu.VMEM((*lead, rows, width), value.dtype)
+    in_vmem = pl.BlockSpec(memory_space=pltpu.VMEM)
+    return pl.pallas_call(
+        functools.partial(small_sum_body, layers),
+        out_shape=jax.ShapeDtypeStruct((rows, 2 * width), value.dtype),
+        in_specs=[in_vmem],
+        out_specs=in_vmem,
+        scratch_shapes=[
+            buffer(),
+            buffer(),
+            buffer(),
+            buffer(),
+            buffer(layers),
+            buffer(),
+            dma((3,)),
+            dma((3,)),
+            dma((layers,)),
+            dma((layers,)),
+        ],
+        compiler_params=pltpu.CompilerParams(
+            collective_id=collective_id,
+            has_side_effects=True,
+            vmem_limit_bytes=32 * 1024 * 1024,
+        ),
+    )(value)
+
+
+def expert_body(
+    layers,
+    few,
+    slots,
+    units,
+    experts,
+    rows_ref,
+    grads_ref,
+    pick_ref,
+    spread_ref,
+    words_ref,
+    gate_w,
+    up_w,
+    down_w,
+    side_w,
+    side_down,
+    d_rows_ref,
+    out_ref,
+    slot_rows_ref,
+    slot_grads_ref,
+    hidden_ref,
+    d_gate_ref,
+    d_up_ref,
+    d_gates_ref,
+    grad_side_ref,
+    grad_side_down_ref,
+    d_slots,
+    slot_out,
+    side_hidden_ref,
+    d_side_ref,
+):
+    bf16, f32 = jnp.bfloat16, jnp.float32
+    own_expert = lax.axis_index("row") * layers + lax.axis_index("exp")
+    count = rows_ref.shape[0] // few
+    block, half = grads_ref.shape[2:]
+    lanes = side_down.shape[0]
+
+    side = dot_nt(rows_ref[...], side_w[...])
+    side_gate, side_up = side[:, :lanes], side[:, lanes:]
+    lane = lax.broadcasted_iota(jnp.int32, side_gate.shape, 1)
+    expert = lane - units
+    is_expert = (expert >= 0) & (expert < experts)
+    highest = jnp.max(jnp.where(is_expert, side_gate, -jnp.inf), axis=1, keepdims=True)
+    words = words_ref[...]
+    word = words[:, 0:1]
+    for i in range(1, words.shape[1]):
+        word = jnp.where(expert >= 16 * i, words[:, i : i + 1], word)
+    picked = lax.shift_right_logical(
+        jnp.broadcast_to(word, expert.shape), jnp.bitwise_and(expert, 15)
+    )
+    picked = is_expert & (jnp.bitwise_and(picked, 1) == 1)
+    chosen = jnp.where(picked, jnp.exp(jnp.where(is_expert, side_gate - highest, 0.0)), 0.0)
+    total = jnp.sum(chosen, axis=1, keepdims=True)
+    own = jnp.sum(jnp.where(expert == own_expert, chosen, 0.0), axis=1, keepdims=True) / total
+
+    def two_parts(value):
+        high = value.astype(bf16).astype(f32)
+        at = lax.broadcasted_iota(jnp.int32, (value.shape[0], lanes), 1)
+        return jnp.where(at == 0, high, jnp.where(at == 1, value - high, 0.0)).astype(bf16)
+
+    own_parts = two_parts(own)
+    slot_gates = []
+    for b in range(count):
+        tokens, here = pl.ds(b * few, few), pl.ds(b * slots, slots)
+        pick = pick_ref[here, :]
+        slot_rows_ref[here, :] = dot_nn(pick, rows_ref[tokens, :]).astype(bf16)
+        first = b * few % block
+        for c in range(2):
+            slot_grads_ref[here, c * half : (c + 1) * half] = dot_nn(
+                pick, grads_ref[b * few // block, c, first : first + few, :]
+            ).astype(bf16)
+        parts = dot_nn(pick, own_parts[b * few : (b + 1) * few])
+        slot_gates.append(jnp.sum(parts, axis=1, keepdims=True))
+    slot_gate = jnp.concatenate(slot_gates, axis=0)
+
+    gate_pre = dot_nt(slot_rows_ref[...], gate_w[...])
+    up_pre = dot_nt(slot_rows_ref[...], up_w[...])
+    d_raw = dot_nt(slot_grads_ref[...], down_w[...])
+    sigmoid = 1.0 / (1.0 + jnp.exp(-gate_pre))
+    silu = gate_pre * sigmoid
+    hidden = (silu * up_pre).astype(bf16).astype(f32)
+    d_gates = jnp.sum(d_raw * hidden, axis=1, keepdims=True)
+    hidden_ref[...] = (hidden * slot_gate).astype(bf16)
+    d_hidden = d_raw * slot_gate
+    d_up_ref[...] = (d_hidden * silu).astype(bf16)
+    d_gate_ref[...] = (
+        d_hidden * up_pre * sigmoid * (1.0 + gate_pre * (1.0 - sigmoid))
+    ).astype(bf16)
+    d_slots[...] = (dot_nn(d_gate_ref[...], gate_w[...]) + dot_nn(d_up_ref[...], up_w[...])).astype(
+        bf16
+    )
+    slot_out[...] = dot_nn(hidden_ref[...], down_w[...]).astype(bf16)
+
+    side_sigmoid = 1.0 / (1.0 + jnp.exp(-side_gate))
+    side_silu = side_gate * side_sigmoid
+    side_hidden_ref[...] = (side_silu * side_up).astype(bf16)
+    d_side_hidden = sum(
+        dot_nt(grads_ref[:, c].reshape(-1, half), side_down[:, c * half : (c + 1) * half])
+        for c in range(2)
+    )
+    d_side_ref[:, lanes:] = (d_side_hidden * side_silu).astype(bf16)
+    d_side_ref[:, :lanes] = (
+        d_side_hidden * side_up * side_sigmoid * (1.0 + side_gate * (1.0 - side_sigmoid))
+    ).astype(bf16)
+
+    @pl.when(pl.program_id(0) == 0)
+    def _():
+        grad_side_ref[...] = jnp.zeros_like(grad_side_ref)
+        grad_side_down_ref[...] = jnp.zeros_like(grad_side_down_ref)
+
+    grad_side_ref[...] += dot_tn(d_side_ref[...], rows_ref[...])
+    for c in range(2):
+        grad_side_down_ref[:, c * half : (c + 1) * half] += dot_tn(
+            side_hidden_ref[...], grads_ref[:, c].reshape(-1, half)
+        )
+
+    d_gate_parts = two_parts(d_gates)
+    for b in range(count):
+        tokens, here = pl.ds(b * few, few), pl.ds(b * slots, slots)
+        spread = spread_ref[tokens, :]
+        d_rows_ref[tokens, :] = (
+            dot_nn(spread, d_slots[here, :]) + dot_nn(d_side_ref[tokens, :], side_w[...])
+        ).astype(bf16)
+        out_ref[tokens, :] = (
+            dot_nn(spread, slot_out[here, :]) + dot_nn(side_hidden_ref[tokens, :], side_down[...])
+        ).astype(bf16)
+        back = dot_nn(spread, d_gate_parts[b * slots : (b + 1) * slots])
+        d_gates_ref[tokens, :] = jnp.sum(back, axis=1, keepdims=True)
+
+
+def expert_pass(layers, few, slots, units, experts, rows, grads, pick, spread, words, weights, side_w, side_down):
+    tokens, width = rows.shape
+    hidden = weights[0].shape[0]
+    block = grads.shape[2]
+    blocks = tokens // few
+    count = next(n for n in (4, 2, 1) if blocks % n == 0 and n * few <= 640)
+    lanes = side_down.shape[0]
+    grid = (blocks // count,)
+    by_step = lambda n, w: pl.BlockSpec((count * n, w), lambda i: (i, 0))
+    whole = lambda value: pl.BlockSpec(
+        value.shape, lambda i: (0, 0), pipeline_mode=pl.Buffered(1)
+    )
+    shape = lambda n, w, kind=jnp.bfloat16: jax.ShapeDtypeStruct((blocks * n, w), kind)
+    return pl.pallas_call(
+        functools.partial(expert_body, layers, few, slots, units, experts),
+        grid=grid,
+        in_specs=[
+            by_step(few, width),
+            pl.BlockSpec((count * few // block, 2, block, width // 2), lambda i: (i, 0, 0, 0)),
+            by_step(slots, few),
+            by_step(few, slots),
+            by_step(few, words.shape[1]),
+            *(whole(w) for w in (*weights, side_w, side_down)),
+        ],
+        out_specs=[
+            by_step(few, width),
+            by_step(few, width),
+            by_step(slots, width),
+            by_step(slots, width),
+            by_step(slots, hidden),
+            by_step(slots, hidden),
+            by_step(slots, hidden),
+            by_step(few, 1),
+            pl.BlockSpec((2 * lanes, width), lambda i: (0, 0)),
+            pl.BlockSpec((lanes, width), lambda i: (0, 0)),
+        ],
+        out_shape=[
+            shape(few, width),
+            shape(few, width),
+            shape(slots, width),
+            shape(slots, width),
+            shape(slots, hidden),
+            shape(slots, hidden),
+            shape(slots, hidden),
+            shape(few, 1, jnp.float32),
+            jax.ShapeDtypeStruct((2 * lanes, width), jnp.float32),
+            jax.ShapeDtypeStruct((lanes, width), jnp.float32),
+        ],
+        scratch_shapes=[
+            pltpu.VMEM((count * slots, width), jnp.bfloat16),
+            pltpu.VMEM((count * slots, width), jnp.bfloat16),
+            pltpu.VMEM((count * few, lanes), jnp.bfloat16),
+            pltpu.VMEM((count * few, 2 * lanes), jnp.bfloat16),
+        ],
+        compiler_params=pltpu.CompilerParams(vmem_limit_bytes=62 * 1024 * 1024),
+    )(rows, grads, pick, spread, words, *weights, side_w, side_down)
+
+
 def rotate(value, cosine, sine):
     half = value.shape[-1] // 2
     first, second = (value[..., :half], value[..., half:])
@@ -596,121 +873,96 @@
 
 
 def routed_and_shared(
-    tok_dev, capacity, layers, router, expert_weights, shared_own, normed_own, grads_own, chosen
+    tok_dev, capacity, layers, router, expert_weights, shared_own, normed_own, grads_own, words
 ):
     bf16 = jnp.bfloat16
     col_id = lax.axis_index("col")
     own_expert = lax.axis_index("row") * layers + lax.axis_index("exp")
     experts = router.shape[1]
+    units = shared_own.shape[1]
     block, half_width = normed_own.shape
-    width = 2 * half_width
-    tokens = chosen.shape[0]
+    tokens = words.shape[0]
     few = min(tok_dev, block)
     slots = -(-min(capacity, few) // 16) * 16
     blocks = tokens // few
-    gather_layers = layers
-    grads_all = gather(grads_own, gather_layers, 3)
-    normed_all = gather(normed_own, gather_layers, 3)
-
-    router_probs = jax.nn.softmax(dot_nn(normed_all, router), axis=1)
-    picks = jnp.any(
-        chosen[:, :, None] == jnp.arange(experts, dtype=jnp.int32)[None, None, :], axis=1
-    )
-    selected = jnp.where(picks, router_probs, 0.0)
-    selected_total = jnp.sum(selected, axis=1, keepdims=True)
-    gates = selected / selected_total
-    is_own = jnp.arange(experts, dtype=jnp.int32)[None, :] == own_expert
-    own_gate = jnp.sum(jnp.where(is_own, gates, 0.0), axis=1).reshape(blocks, few)
-    own_pick = jnp.any(picks & is_own, axis=1).reshape(blocks, few)
-    place = jnp.cumsum(own_pick.astype(jnp.int32), axis=1) - 1
-    onehot = (place[:, None, :] == jnp.arange(slots, dtype=jnp.int32)[None, :, None]) & own_pick[
-        :, None, :
-    ]
-    slot_gate = jnp.sum(jnp.where(onehot, own_gate[:, None, :], 0.0), axis=2).reshape(-1, 1)
-    pick_rows = onehot.astype(bf16)
-
-    def to_slots(value):
-        return (
-            jnp.einsum(
-                "bsi,bid->bsd",
-                pick_rows,
-                value.reshape(blocks, few, width),
-                preferred_element_type=jnp.float32,
-            )
-            .astype(bf16)
-            .reshape(blocks * slots, width)
-        )
-
-    def from_slots(value):
-        return jnp.einsum(
-            "bsi,bsd->bid",
-            pick_rows,
-            value.reshape(blocks, slots, width),
-            preferred_element_type=jnp.float32,
-        ).reshape(tokens, width)
-
-    slot_rows = to_slots(normed_all)
-    slot_grads = to_slots(grads_all)
-    gate_weight, up_weight, down_weight = expert_weights
-
-    def feed_forward(rows, grads, gate_of, gate_w, up_w, down_w):
-        gate_pre = dot_nn(rows, gate_w)
-        up_pre = dot_nn(rows, up_w)
-        sigmoid = jax.nn.sigmoid(gate_pre)
-        silu = gate_pre * sigmoid
-        hidden = (silu * up_pre).astype(bf16).astype(jnp.float32)
-        d_raw = dot_nn(grads, down_w)
-        d_gate_of = jnp.sum(d_raw * hidden, axis=1)
-        d_hidden = d_raw if gate_of is None else d_raw * gate_of
-        hidden = hidden if gate_of is None else hidden * gate_of
-        d_up = (d_hidden * silu).astype(bf16)
-        d_gate = (d_hidden * up_pre * sigmoid * (1.0 + gate_pre * (1.0 - sigmoid))).astype(bf16)
-        return (hidden.astype(bf16), d_gate, d_up, d_gate_of)
-
-    hidden, d_gate, d_up, d_gates_slots = feed_forward(
-        slot_rows, slot_grads, slot_gate, gate_weight, up_weight, down_weight
-    )
-    shared_hidden, d_shared_gate, d_shared_up, _ = feed_forward(
-        normed_all, grads_all, None, shared_own[0].T, shared_own[1].T, shared_own[2].T
-    )
-    d_pair = (dot_nt(d_gate, gate_weight) + dot_nt(d_up, up_weight)).astype(bf16)
-    d_normed = scatter(
-        (
-            from_slots(d_pair)
-            + dot_nn(d_shared_gate, shared_own[0])
-            + dot_nn(d_shared_up, shared_own[1])
-        ).astype(bf16),
+
+    own_word = lax.dynamic_index_in_dim(words, own_expert // 16, 1, keepdims=False)
+    own_pick = (jnp.bitwise_and(lax.shift_right_logical(own_word, own_expert % 16), 1) == 1).reshape(
+        blocks, few
+    )
+    order = jnp.arange(few, dtype=jnp.int32)
+    place = dot_nn(own_pick.astype(bf16), (order[:, None] < order[None, :]).astype(bf16)).astype(
+        jnp.int32
+    )
+    places = jnp.arange(slots, dtype=jnp.int32)
+    pick = ((place[:, None, :] == places[None, :, None]) & own_pick[:, None, :]).astype(bf16)
+    spread = ((place[:, :, None] == places[None, None, :]) & own_pick[:, :, None]).astype(bf16)
+    lanes = -(-(units + experts) // 128) * 128
+    fill = lambda value, n: jnp.pad(value, ((0, n - value.shape[0]), (0, 0)))
+    side_w = jnp.concatenate(
+        [fill(jnp.concatenate([shared_own[0], router.T]), lanes), fill(shared_own[1], lanes)]
+    )
+    side_down = fill(shared_own[2], lanes)
+
+    grads_all = lax.all_gather(grads_own, ("row", "exp", "col"), axis=0)
+    grads_all = grads_all.reshape(experts, 2, block, half_width)
+    normed_all = gather(normed_own, layers, 3)
+    (
+        d_rows,
+        out_rows,
+        slot_rows,
+        slot_grads,
+        hidden,
+        d_gate,
+        d_up,
+        d_gates_all,
+        grad_side,
+        grad_side_down,
+    ) = expert_pass(
         layers,
-        4,
-    )
-    result = dot_nt(hidden, down_weight).astype(bf16)
-    branch = scatter(
-        (from_slots(result) + dot_nn(shared_hidden, shared_own[2])).astype(bf16), layers, 4
-    )
-    grad_gate = dot_tn(slot_rows, d_gate)
-    grad_up = dot_tn(slot_rows, d_up)
-    grad_down = dot_tn(slot_grads, hidden)
+        few,
+        slots,
+        units,
+        experts,
+        normed_all,
+        grads_all,
+        pick.reshape(blocks * slots, few),
+        spread.reshape(tokens, slots),
+        words,
+        expert_weights,
+        side_w,
+        side_down,
+    )
+    d_normed = scatter(d_rows, layers, 4)
+    grad_gate = dot_tn(d_gate, slot_rows)
+    grad_up = dot_tn(d_up, slot_rows)
+    grad_down = dot_tn(hidden, slot_grads)
     grad_shared = jnp.stack(
-        [
-            dot_tn(d_shared_gate, normed_all),
-            dot_tn(d_shared_up, normed_all),
-            dot_tn(shared_hidden, grads_all),
-        ]
-    )
-
-    d_gates_dense = jnp.sum(
-        jnp.where(onehot, d_gates_slots.reshape(blocks, slots, 1), 0.0), axis=1
-    ).reshape(experts, block)
+        [grad_side[:units], grad_side[lanes : lanes + units], grad_side_down[:units]]
+    )
+
     d_gates = lax.psum(
-        lax.all_to_all(d_gates_dense, ("row", "exp"), split_axis=0, concat_axis=0, tiled=True), "col"
+        lax.all_to_all(
+            d_gates_all.reshape(experts, block), ("row", "exp"), split_axis=0, concat_axis=0, tiled=True
+        ),
+        "col",
     ).T
-
-    def own_rows(value):
-        return lax.dynamic_slice_in_dim(value, own_expert * block, block, 0)
-
-    own_probs, own_gates, own_total = own_rows(router_probs), own_rows(gates), own_rows(selected_total)
+    own_probs = jax.nn.softmax(
+        dot_nn(lax.dynamic_slice_in_dim(normed_all, own_expert * block, block, 0), router), axis=1
+    )
+    own_words = lax.dynamic_slice_in_dim(words, own_expert * block, block, 0)
+    numbers = jnp.arange(experts, dtype=jnp.int32)
+    picks = (
+        jnp.bitwise_and(
+            lax.shift_right_logical(own_words[:, numbers // 16], (numbers % 16)[None, :]), 1
+        )
+        == 1
+    )
+    selected = jnp.where(picks, own_probs, 0.0)
+    own_total = jnp.sum(selected, axis=1, keepdims=True)
+    own_gates = selected / own_total
     d_selected = (d_gates - jnp.sum(d_gates * own_gates, axis=1, keepdims=True)) / own_total
-    d_router_probs = jnp.where(own_rows(picks), d_selected, 0.0)
+    d_router_probs = jnp.where(picks, d_selected, 0.0)
     d_logits = own_probs * (
         d_router_probs - jnp.sum(own_probs * d_router_probs, axis=1, keepdims=True)
     )
@@ -729,7 +981,7 @@
         precision=lax.Precision.HIGHEST,
         preferred_element_type=jnp.float32,
     )
-    return (d_normed, branch, (grad_gate, grad_up, grad_down, grad_shared, grad_router))
+    return (d_normed, out_rows, (grad_gate, grad_up, grad_down, grad_shared, grad_router))
 
 
 def per_device(
@@ -774,6 +1026,13 @@
 
     w_query_own = trade(w_query, 1, 0)
     w_latent_all = lax.all_gather(w_latent[0].T, ("col", "row"), axis=1, tiled=True)
+    seq_ids, places = sequence_layout(lengths[0], group)
+    cosine, sine = rotary_tables(places)
+
+    group_input = gather(layer_input, 1, 1)
+    group_input, w_out, shared_gate, shared_up, shared_down, cotangent = lax.optimization_barrier(
+        (group_input, w_out, shared_gate, shared_up, shared_down, cotangent)
+    )
     w_out_own = trade(w_out, 0, 1)
     units = shared_gate.shape[1] // (cols_n * exps_n)
     shared_parts = jnp.stack(
@@ -786,12 +1045,7 @@
     )
     shared_own = trade(shared_parts, 1, 3)[:, 0]
 
-    chosen_all = lax.all_gather(routes[0], ("row", "exp", "col"), axis=0, tiled=True)
-
-    seq_ids, places = sequence_layout(lengths[0], group)
-    cosine, sine = rotary_tables(places)
-
-    group_input = gather(layer_input, 1, 1).astype(jnp.float32)
+    group_input = group_input.astype(jnp.float32)
     factor_group = lax.rsqrt(jnp.mean(group_input * group_input, axis=1) + epsilon)
     normed_group = (group_input * factor_group[:, None] * norm1_gain).astype(bf16)
     query_pre = dot_nn(normed_group, w_query_own).reshape(group, heads_here, head_dim)
@@ -836,6 +1090,18 @@
 
     input_wide = layer_input.astype(jnp.float32)
     hidden_state = input_wide + scatter(dot_nn(attended, w_out_own).astype(bf16), 1, 2)
+    words_n = -(-experts // 16)
+    word_of = jnp.arange(words_n, dtype=jnp.int32)[:, None, None]
+    bits = jnp.where(routes // 16 == word_of, jnp.left_shift(1, routes % 16), 0)
+    bits = jnp.sum(bits, axis=2).astype(jnp.float32)
+    padded = -(-tok_dev // 128) * 128
+    bits = jnp.pad(bits, ((0, 0), (0, padded - tok_dev)))
+    is_here = jnp.arange(experts, dtype=jnp.int32) == own_expert
+    bits = jnp.where(is_here[:, None, None], bits[None], 0.0).reshape(experts * words_n, padded)
+    bits, hidden_state = lax.optimization_barrier((bits, hidden_state))
+    bits = small_sum(bits, exps_n, 8).reshape(experts, words_n, cols_n, padded)[..., :tok_dev]
+    words_all = bits.astype(jnp.int32).transpose(0, 2, 3, 1).reshape(tokens, words_n)
+
     gain_two = lax.dynamic_slice_in_dim(norm2_gain, col_id * half_width, half_width)
     square = lax.psum(jnp.sum(hidden_state * hidden_state, axis=1), "col")
     factor_two = lax.rsqrt(square / width + epsilon)
@@ -847,39 +1113,38 @@
         capacity,
         exps_n,
         router,
-        (expert_gate[0], expert_up[0], expert_down[0]),
+        (expert_gate[0].T, expert_up[0].T, expert_down[0].T),
         shared_own,
     )
     if pieces == 1:
-        d_normed, branch, weight_grads = feed(normed_two, cotangent, chosen_all)
+        d_normed, out_rows, weight_grads = feed(normed_two, cotangent, words_all)
     else:
         piece_rows = block // pieces
 
         def one_piece(total, items):
-            d_rows, branch_rows, grads = feed(*items)
-            return (jax.tree.map(jnp.add, total, grads), (d_rows, branch_rows))
+            d_rows, out_rows, grads = feed(*items)
+            return (jax.tree.map(jnp.add, total, grads), (d_rows, scatter(out_rows, exps_n, 4)))
 
         split = lambda value: value.reshape(pieces, piece_rows, half_width)
-        chosen_pieces = chosen_all.reshape(experts, pieces, piece_rows, topk_count)
+        word_pieces = words_all.reshape(experts, pieces, piece_rows, words_n)
         items = (
             split(normed_two),
             split(cotangent),
-            chosen_pieces.transpose(1, 0, 2, 3).reshape(pieces, -1, topk_count),
+            word_pieces.transpose(1, 0, 2, 3).reshape(pieces, -1, words_n),
         )
         shapes = jax.eval_shape(lambda: feed(*(item[0] for item in items))[2])
         start = jax.tree.map(lambda leaf: jnp.zeros(leaf.shape, leaf.dtype), shapes)
         weight_grads, (d_normed, branch) = lax.scan(one_piece, start, items)
         d_normed, branch = (v.reshape(block, half_width) for v in (d_normed, branch))
     grad_gate, grad_up, grad_down, grad_shared, grad_router = weight_grads
-    output = (hidden_state + branch).astype(bf16)
     grad_shared = trade(grad_shared.astype(bf16)[:, None], 3, 1)
+    d_normed, grad_shared = lax.optimization_barrier((d_normed, grad_shared))
     grad_shared = lax.all_gather(grad_shared, "exp", axis=2, tiled=False)
-    grad_shared = grad_shared.reshape(3, cols_n * exps_n * units, half_width).astype(jnp.float32)
     d_norm_two, grad_gain_two = norm_back(hidden_state, factor_two, gain_two, d_normed, width)
     d_hidden_state = cotangent.astype(jnp.float32) + d_norm_two
 
     d_branch = gather(d_hidden_state.astype(bf16), 1, 1)
-    grad_w_out = dot_tn(attended, d_branch)
+    grad_w_out = trade(dot_tn(attended, d_branch).astype(bf16), 1, 0)
     d_attended = dot_nt(d_branch, w_out_own).astype(bf16).reshape(group, heads_here, V_DIM)
     d_query_blocks = []
     d_keys = jnp.zeros((group, heads_here, head_dim), jnp.float32)
@@ -926,28 +1191,42 @@
         .reshape(group, heads_here * (QK_NOPE + V_DIM))
     )
     grad_w_kv = dot_tn(compressed, d_key_value)
-    d_latent_sum = lax.psum(
+    d_latent_sum = scatter(
         jnp.concatenate(
             [dot_nt(d_key_value, w_kv), jnp.sum(d_keys[..., QK_NOPE:], axis=1)], axis=1
         ).astype(bf16),
-        ("row", "col"),
-    ).astype(jnp.float32)
+        1,
+        5,
+        by_rows=True,
+    )
+    own_first = (row_id * cols_n + col_id) * (group // (rows_n * cols_n))
+
+    def own_tokens(value):
+        return lax.dynamic_slice_in_dim(value, own_first, group // (rows_n * cols_n), 0)
+
+    raw_own, factor_own = own_tokens(compressed_raw), own_tokens(kv_factor)
     d_compressed = d_latent_sum[:, :KV_RANK]
     weighted = d_compressed * latent_gain
-    grad_latent_gain = jnp.sum(d_compressed * compressed_raw * kv_factor[:, None], axis=0)
-    inner = jnp.sum(weighted * compressed_raw, axis=1)
+    grad_latent_gain = jnp.sum(d_compressed * raw_own * factor_own[:, None], axis=0)
+    inner = jnp.sum(weighted * raw_own, axis=1)
     d_raw = (
-        kv_factor[:, None] * weighted
-        - compressed_raw * (kv_factor * kv_factor * kv_factor * inner / KV_RANK)[:, None]
-    )
-    d_latent = jnp.concatenate(
-        [d_raw, unrotate(d_latent_sum[:, KV_RANK:], cosine, sine)], axis=1
-    ).astype(bf16)
+        factor_own[:, None] * weighted
+        - raw_own * (factor_own * factor_own * factor_own * inner / KV_RANK)[:, None]
+    )
+    d_latent = gather(
+        jnp.concatenate(
+            [d_raw, unrotate(d_latent_sum[:, KV_RANK:], own_tokens(cosine), own_tokens(sine))],
+            axis=1,
+        ).astype(bf16),
+        1,
+        6,
+        by_rows=True,
+    )
     slab = w_latent.shape[1]
     slab_start = col_id * half_width + row_id * slab
     normed_slab = lax.dynamic_slice_in_dim(normed_group, slab_start, slab, 1)
     grad_w_latent = dot_tn(d_latent, normed_slab)
-    grad_w_query = dot_tn(normed_group, d_query_pre)
+    grad_w_query = trade(dot_tn(normed_group, d_query_pre).astype(bf16), 0, 1)
     d_gathered = dot_nt(d_query_pre, w_query_own)
     piece = lax.dynamic_slice_in_dim(d_gathered, slab_start, slab, 1) + dot_nt(
         d_latent, w_latent[0]
@@ -958,37 +1237,46 @@
     factor_one = lax.dynamic_slice_in_dim(factor_group, row_id * block, block)
     d_norm_one, grad_gain_one = norm_back(input_wide, factor_one, gain_one, d_first, width)
     input_grad = d_hidden_state + d_norm_one
-
-    latent_share = grad_latent_gain / (rows_n * cols_n)
+    if pieces == 1:
+        out_rows, input_grad = lax.optimization_barrier((out_rows, input_grad))
+        branch = scatter(out_rows, exps_n, 4)
+    output = (hidden_state + branch).astype(bf16)
+
     small = jnp.concatenate(
-        [grad_gain_one[None], grad_gain_two[None], grad_router.T], axis=0
-    )
-    small = lax.psum(small, ("row", "exp"))
-    small = lax.all_gather(small, "col", axis=1, tiled=True)
-    summed_latent_gain = lax.psum(latent_share, ("row", "col", "exp"))
-
+        [
+            grad_gain_one[None],
+            grad_gain_two[None],
+            jnp.pad(grad_latent_gain, (0, half_width - KV_RANK))[None],
+            grad_router.T,
+        ],
+        axis=0,
+    )
+    small = jnp.pad(small, ((0, -small.shape[0] % 8), (0, 0)))
+    small = small_sum(small, exps_n, 7)
+    summed_latent_gain = small[2, :KV_RANK] + small[2, half_width : half_width + KV_RANK]
+
+    grad_shared, grad_w_query = lax.optimization_barrier((grad_shared, grad_w_query))
+    grad_shared = grad_shared.reshape(3, cols_n * exps_n * units, half_width).astype(jnp.float32)
     summed = lax.psum(
-        tuple(g.astype(bf16) for g in (grad_w_query, grad_w_latent, grad_w_kv, grad_w_out)), "exp"
-    )
-    out_w_query = trade(summed[0], 0, 1).astype(jnp.float32)
-    out_w_out = trade(summed[3], 1, 0).astype(jnp.float32)
+        (grad_w_query, grad_w_latent.astype(bf16), grad_w_kv.astype(bf16), grad_w_out), "exp"
+    )
     return (
         output,
         input_grad,
         small[0],
-        out_w_query,
+        summed[0].astype(jnp.float32),
         summed[1].T.astype(jnp.float32)[None],
         summed_latent_gain,
         summed[2].astype(jnp.float32),
-        out_w_out,
+        summed[3].astype(jnp.float32),
         small[1],
         grad_shared[0].T,
         grad_shared[1].T,
         grad_shared[2],
-        small[2:].T,
-        grad_gate[None],
-        grad_up[None],
-        grad_down[None],
+        small[3 : 3 + experts].T,
+        grad_gate.T[None],
+        grad_up.T[None],
+        grad_down.T[None],
     )
 
 

time: 1390 us -> 977 us (0.70)
  matrix products: 412 us -> 107 us
  blocking collectives: 205 us -> 22.3 us
  Pallas kernels: 517 us -> 677 us
  waiting for transfers between devices: 108 us -> 19.2 us
    dot_general x13 -> x5, matrix products: 180 us -> 12.2 us  [dot_nn(): return jnp.dot(left, right, preferred_element_type=jnp.float32)]
    pallas_call x8 -> x12, Pallas kernels: 517 us -> 677 us  [the longest x5 316 us: scatter(): pl.pallas_call(functools.partial(scatter_body, layers, by_rows), out_shap...]
    all_gather x2 -> x0, blocking collectives: 136 us -> none  [the longest x1 131 us: per_device(): lax.all_gather(routes[0], ('row', 'exp', 'col'), axis=0, tiled=True)]
    dot_general x4 -> x0, matrix products: 66 us -> none  [the longest x2 40.5 us: from_slots(): jnp.einsum('bsi,bsd->bid', pick_rows, value.reshape(blocks, slots, width)...]
    dot_general x8 -> x5, matrix products: 65.1 us -> 18 us  [dot_nt(): lax.dot_general(left, right, (((1,), (1,)), ((), ())), preferred_element_...]
    psum x2 -> x1, blocking collectives: 53.8 us -> 7.36 us  [routed_and_shared(): lax.psum(lax.all_to_all(d_gates_all.reshape(experts, block), ('row', 'exp...]
    psum x3 -> x1, waiting for transfers between devices: 42.4 us -> 0.01 us  [per_device(): lax.psum((grad_w_query, grad_w_latent.astype(bf16), grad_w_kv.astype(bf16...]
    all_gather x1, waiting for transfers between devices: 44.1 us -> 5.85 us  [per_device(): grad_shared = lax.all_gather(grad_shared, 'exp', axis=2, tiled=False)]
  transfers between devices with their start and end apart: 12 -> 11, of which waited for: 4 -> 2; matrix products, arithmetic and copies ran while one was open for 27% -> 16% of each run, Pallas kernels for 29% -> 51%
where the time goes in v2:
time: 977 us; the launch traced here: 968 us
  Pallas kernels  677 us (69%)
  matrix products  107 us (11%)
  other arithmetic  76.4 us (8%)
  local copies, waits for them, and re-layouts  37.9 us (4%)
  blocking collectives  22.3 us (2%)
  waiting for transfers between devices  19.2 us (2%)
  between operations  15.6 us (2%)
  starting transfers between devices  11.8 us (1%)
    pallas_call x5, Pallas kernels, scatter(): pl.pallas_call(functools.partial(scatter_body, layers, by_rows), out_shap...  316 us
    pallas_call x4, Pallas kernels, gather(): pl.pallas_call(functools.partial(gather_body, layers, by_rows), out_shape...  166 us
    pallas_call x1, Pallas kernels, expert_pass(): pl.pallas_call(functools.partial(expert_body, layers, few, slots, units,...  157 us
    dot_general x7, matrix products, dot_tn(): lax.dot_general(left, right, (((0,), (0,)), ((), ())), preferred_element_...  53.7 us
    pallas_call x2, Pallas kernels, small_sum(): pl.pallas_call(functools.partial(small_sum_body, layers), out_shape=jax.S...  38.1 us
  transfers between devices with their start and end apart: 11, of which 2 were waited for; matrix products, arithmetic and copies ran while one was open for 16% of the time, Pallas kernels for 51%

profile of v2, /device:TPU:0, one launch (start us, length us, event | category | flops | bytes accessed | tf_op | source)
XLA Modules:
  0.0 967.8 jit_solution(16016711446476440052)
XLA Ops:
  8.0 31.5 %shard_map.307 = bf16[1280,2048]{1,0:T(8,128)(2,1)} custom-call(bf16[320,1024]{1,0:T(8,128)(2,1)} %src.1), custom_call_target="tpu_custom_call" | custom-call | tf_op jit(solution)/shard_map/pallas_call | solution.py:244
  53.1 6.0 fusion.2
  65.9 12.5 %collective-permute-done = bf16[1024,384]{1,0:T(8,128)(2,1)} collective-permute-done((bf16[1024,384]{1,0:T(8,128)(2,1)}, bf16[1024,384]{1,0:T(8,128)(2,1)}, u32[]{:S(2)}, u32[]{:S(2)}) %collective-permute-start) | collective-permute-done | bytes 786464 | tf_op jit(solution)/shard_map/ppermute | solution.py:861
  83.7 7.0 fusion.99
  114.5 5.4 convolution_convert_fusion.src
  119.9 53.5 %shard_map.308 = f32[320,1024]{1,0:T(8,128)} custom-call(bf16[1280,2048]{1,0:T(8,128)(2,1)} %convolution_convert_fusion.src), custom_call_target="tpu_custom_call" | custom-call | tf_op jit(solution)/shard_map/pallas_call | solution.py:487
  174.9 13.5 %shard_map.310 = f32[16,512]{1,0:T(8,128)S(1)} custom-call(f32[16,256]{1,0:T(8,128)S(1)} %broadcast_select_fusion.src), custom_call_target="tpu_custom_call" | custom-call | tf_op jit(solution)/shard_map/pallas_call | solution.py:585
  196.7 96.9 %shard_map.309.rows_ref = bf16[5120,2048]{1,0:T(8,128)(2,1)} custom-call(bf16[320,1024]{1,0:T(8,128)(2,1)} %multiply_convert_fusion.3.src), custom_call_target="tpu_custom_call" | custom-call | tf_op jit(solution)/shard_map/pallas_call | solution.py:244
  303.6 156.7 %shard_map.311 = (bf16[5120,2048]{1,0:T(8,128)(2,1)}, bf16[5120,2048]{1,0:T(8,128)(2,1)}, bf16[3072,2048]{1,0:T(8,128)(2,1)}, bf16[3072,2048]{1,0:T(8,128)(2,1)}...) custom-call(bf16[5120,2048]{1,0:T(8,128)(2,1)} %shard_map.309.rows_r, ...), custom_call_target="tpu_custom_call" | custom-call | tf_op jit(solution)/shard_map/pallas_call | solution.py:753
  460.3 15.3 %convolution_bitcast_fusion.1 = f32[1,2048,704]{1,2,0:T(8,128)} fusion(bf16[3072,2048]{1,0:T(8,128)(2,1)} %get-tuple-element.123, bf16[3072,704]{1,0:T(8,128)(2,1)} %get-tuple-element.125), kind=kOutput, calls=%fused_computation.13 | convolution fusion | flops 8858370048 | bytes 22675456 | tf_op jit(solution)/shard_map/dot_general | solution.py:528
  475.6 11.4 %convolution_bitcast_fusion.2 = f32[1,2048,704]{1,2,0:T(8,128)} fusion(bf16[3072,2048]{1,0:T(8,128)(2,1)S(1)} %copy-done.71, bf16[3072,704]{1,0:T(8,128)(2,1)S(1)} %copy-done.72), kind=kOutput, calls=%fused_computation.14 | convolution fusion | flops 8858370048 | bytes 22675456 | tf_op jit(solution)/shard_map/dot_general | solution.py:528
  493.8 5.0 all-to-all-start
  498.9 15.5 %convolution_bitcast_fusion = f32[1,2048,704]{1,2,0:T(8,128)} fusion(bf16[3072,2048]{1,0:T(8,128)(2,1)} %get-tuple-element.126, bf16[3072,704]{1,0:T(8,128)(2,1)} %get-tuple-element.127), kind=kOutput, calls=%fused_computation.12 | convolution fusion | flops 8858370048 | bytes 22675456 | tf_op jit(solution)/shard_map/dot_general | solution.py:528
  514.4 96.1 %shard_map.312 = f32[320,1024]{1,0:T(8,128)} custom-call(bf16[5120,2048]{1,0:T(8,128)(2,1)} %get-tuple-element.113.src), custom_call_target="tpu_custom_call" | custom-call | tf_op jit(solution)/shard_map/pallas_call | solution.py:487
  610.6 7.4 psum.57
  624.4 5.1 psum.58
  631.8 26.1 %shard_map.313 = bf16[1280,2048]{1,0:T(8,128)(2,1)} custom-call(bf16[320,1024]{1,0:T(8,128)(2,1)} %fusion.91.src), custom_call_target="tpu_custom_call" | custom-call | tf_op jit(solution)/shard_map/pallas_call | solution.py:244
  701.8 22.5 %shard_map.314 = f32[160,576]{1,0:T(8,128)} custom-call(bf16[1280,576]{1,0:T(8,128)(2,1)} %pad_maximum_fusion.src), custom_call_target="tpu_custom_call" | custom-call | tf_op jit(solution)/shard_map/pallas_call | solution.py:487
  728.7 11.5 %shard_map.315 = bf16[1280,576]{1,0:T(8,128)(2,1)} custom-call(bf16[160,576]{1,0:T(8,128)(2,1)} %pad_maximum_fusion.15.src), custom_call_target="tpu_custom_call" | custom-call | tf_op jit(solution)/shard_map/pallas_call | solution.py:244
  751.2 5.9 all-gather.10.cloned.1.call-done
  766.0 30.9 %shard_map.316 = f32[320,1024]{1,0:T(8,128)} custom-call(bf16[1280,2048]{1,0:T(8,128)(2,1)} %convert_element_type.191.src), custom_call_target="tpu_custom_call" | custom-call | tf_op jit(solution)/shard_map/pallas_call | solution.py:487
  798.8 24.6 %shard_map.318 = f32[24,2048]{1,0:T(8,128)S(1)} custom-call(f32[24,1024]{1,0:T(8,128)S(1)} %select_maximum_fusion.src), custom_call_target="tpu_custom_call" | custom-call | tf_op jit(solution)/shard_map/pallas_call | solution.py:585
  823.5 4.9 psum.59
  832.5 113.5 %shard_map.317 = f32[320,1024]{1,0:T(8,128)} custom-call(bf16[5120,2048]{1,0:T(8,128)(2,1)} %get-tuple-element.118.src), custom_call_target="tpu_custom_call" | custom-call | tf_op jit(solution)/shard_map/pallas_call | solution.py:487
  (331 shorter events, 173.4 us)
Async XLA Ops:
  7.2 32.3 %copy-start = (bf16[1024,704]{0,1:T(8,128)(2,1)S(1)}, bf16[1024,704]{0,1:T(8,128)(2,1)}, u32[]{:S(2)}) copy-start(bf16[1024,704]{0,1:T(8,128)(2,1)} %param.40) | copy-start | bytes 4325380
  7.2 76.5 %all-gather.6.cloned.1.call-start = ((), (), s32[]{:S(2)}) async-start(), calls=%async_computation.1 | async-start | bytes 2654208 | tf_op jit(solution)/shard_map/all_gather | solution.py:1028
  7.9 295.7 %all-gather.8.cloned.1.call-start = ((), (), s32[]{:S(2)}) async-start(), calls=%async_computation.2 | async-start | bytes 21626880 | tf_op jit(solution)/shard_map/all_gather | solution.py:907
  41.7 20.4 %collective-permute-start.2 = (bf16[3,1,88,1024]{3,2,1,0:T(8,128)(2,1)}, bf16[3,1,88,1024]{3,2,1,0:T(8,128)(2,1)}, u32[]{:S(2)}, u32[]{:S(2)}) collective-permute-start(bf16[3,1,88,1024]{3,2,1,0:T(8,128)(2,1)} %get-tuple-element.241), channel_id=1, source_target_pairs={{0,4},{4,0},{1,5},{5,1},{2,6},{6,2},{3,7},{7,3},{8,12},{12,8},{9,1... | collective-permute-start | bytes 1622024 | tf_op jit(solution)/shard_map/ppermute | solution.py:861
  45.5 32.9 %copy-start.24 = (bf16[1024,384]{1,0:T(8,128)(2,1)}, bf16[1024,384]{1,0:T(8,128)(2,1)S(1)}, u32[]{:S(2)}) copy-start(bf16[1024,384]{1,0:T(8,128)(2,1)S(1)} %get-tuple-element.233) | copy-start | bytes 2359300
  45.5 32.9 %collective-permute-start = (bf16[1024,384]{1,0:T(8,128)(2,1)}, bf16[1024,384]{1,0:T(8,128)(2,1)}, u32[]{:S(2)}, u32[]{:S(2)}) collective-permute-start(bf16[1024,384]{1,0:T(8,128)(2,1)} %get-tuple-element.234), channel_id=1, source_target_pairs={{0,4},{4,0},{1,5},{5,1},{2,6},{6,2},{3,7},{7,3},{8,12},{12,8},{9,1... | collective-permute-start | bytes 2359304 | tf_op jit(solution)/shard_map/ppermute | solution.py:861
  47.2 67.3 %collective-permute-start.1 = (bf16[256,1024]{1,0:T(8,128)(2,1)}, bf16[256,1024]{1,0:T(8,128)(2,1)}, u32[]{:S(2)}, u32[]{:S(2)}) collective-permute-start(bf16[256,1024]{1,0:T(8,128)(2,1)} %get-tuple-element.247), channel_id=1, source_target_pairs={{0,4},{4,0},{1,5},{5,1},{2,6},{6,2},{3,7},{7,3},{8,12},{12,8},{9,1... | collective-permute-start | bytes 1572872 | tf_op jit(solution)/shard_map/ppermute | solution.py:861
  59.1 239.5 %copy-start.66 = (s32[16]{0:T(128)}, s32[16]{0:T(128)S(1)}, u32[]{:S(2)}) copy-start(s32[16]{0:T(128)S(1)} %and_select_fusion.2) | copy-start | bytes 196
  101.8 194.3 %copy-start.57 = (f32[1280]{0:T(1024)}, f32[1280]{0:T(1024)S(1)}, u32[]{:S(2)}) copy-start(f32[1280]{0:T(1024)S(1)} %add_rsqrt_fusion) | copy-start | bytes 15364
  119.9 53.5 %copy-start.14 = (bf16[320,1024]{1,0:T(8,128)(2,1)S(1)}, bf16[320,1024]{1,0:T(8,128)(2,1)}, u32[]{:S(2)}) copy-start(bf16[320,1024]{1,0:T(8,128)(2,1)} %src.1) | copy-start | bytes 1966084
  174.9 454.7 %copy-start.3 = (f32[320,1024]{1,0:T(8,128)}, f32[320,1024]{1,0:T(8,128)S(1)}, u32[]{:S(2)}) copy-start(f32[320,1024]{1,0:T(8,128)S(1)} %convert_add_fusion) | copy-start | bytes 3932164
  195.7 98.0 %copy-start.64 = (f32[320]{0:T(512)}, f32[320]{0:T(512)S(1)}, u32[]{:S(2)}) copy-start(f32[320]{0:T(512)S(1)} %psum.56) | copy-start | bytes 3844
  489.6 131.7 %collective-permute-start.3 = (bf16[3,1,88,1024]{3,2,1,0:T(8,128)(2,1)}, bf16[3,1,88,1024]{3,2,1,0:T(8,128)(2,1)}, u32[]{:S(2)}, u32[]{:S(2)}) collective-permute-start(bf16[3,1,88,1024]{3,2,1,0:T(8,128)(2,1)} %get-tuple-element.236), channel_id=1, source_target_pairs={{0,4},{4,0},{1,5},{5,1},{2,6},{6,2},{3,7},{7,3},{8,12},{12,8},{9,1... | collective-permute-start | bytes 1622024 | tf_op jit(solution)/shard_map/ppermute | solution.py:861
  493.8 116.7 %all-to-all-start = ((f32[16,1,320]{2,1,0:T(1,128)}), f32[16,1,320]{2,1,0:T(1,128)S(1)}, u32[]{:S(2)}, u32[]{:S(2)}) async-start(f32[16,1,320]{2,1,0:T(1,128)} %all_to_all.11), calls=%async_computation | async-start | bytes 49152 | tf_op jit(solution)/shard_map/all_to_all | solution.py:945
  498.8 258.3 %all-gather.10.cloned.1.call-start = ((), (), s32[]{:S(2)}) async-start(), calls=%async_computation.3 | async-start | bytes 5406720 | tf_op jit(solution)/shard_map/all_gather | solution.py:1142
  514.4 103.5 %copy-start.67 = (s32[16]{0:T(128)S(1)}, s32[16]{0:T(128)}, u32[]{:S(2)}) copy-start(s32[16]{0:T(128)} %copy-done.66) | copy-start | bytes 196
  514.4 103.7 %copy-start.20 = (bf16[320,1024]{1,0:T(8,128)(2,1)S(1)}, bf16[320,1024]{1,0:T(8,128)(2,1)}, u32[]{:S(2)}) copy-start(bf16[320,1024]{1,0:T(8,128)(2,1)} %multiply_convert_fusion.3.src) | copy-start | bytes 1966084
  674.9 279.2 %all-reduce.11.cloned.1.call-start = ((), (), s32[]{:S(2)}) async-start(), calls=%async_computation.4 | async-start | bytes 6881280 | tf_op jit(solution)/shard_map/psum | solution.py:1260
  682.9 65.2 %collective-permute-start.4 = (bf16[1024,384]{0,1:T(8,128)(2,1)}, bf16[1024,384]{0,1:T(8,128)(2,1)}, u32[]{:S(2)}, u32[]{:S(2)}) collective-permute-start(bf16[1024,384]{0,1:T(8,128)(2,1)} %get-tuple-element.232), channel_id=1, source_target_pairs={{0,4},{4,0},{1,5},{5,1},{2,6},{6,2},{3,7},{7,3},{8,12},{12,8},{9,1... | collective-permute-start | bytes 2359304 | tf_op jit(solution)/shard_map/ppermute | solution.py:861
  686.1 59.3 %collective-permute-start.5 = (bf16[256,1024]{1,0:T(8,128)(2,1)}, bf16[256,1024]{1,0:T(8,128)(2,1)}, u32[]{:S(2)}, u32[]{:S(2)}) collective-permute-start(bf16[256,1024]{1,0:T(8,128)(2,1)} %get-tuple-element.243), channel_id=1, source_target_pairs={{0,4},{4,0},{1,5},{5,1},{2,6},{6,2},{3,7},{7,3},{8,12},{12,8},{9,1... | collective-permute-start | bytes 1572872 | tf_op jit(solution)/shard_map/ppermute | solution.py:861
  766.0 32.8 %copy-start.53 = (f32[16,1024]{1,0:T(8,128)S(1)}, f32[16,1024]{1,0:T(8,128)}, u32[]{:S(2)}) copy-start(f32[16,1024]{1,0:T(8,128)} %fusion.63) | copy-start | bytes 196612
  796.9 32.3 %copy-start.4 = (f32[320,1024]{1,0:T(8,128)S(1)}, f32[320,1024]{1,0:T(8,128)}, u32[]{:S(2)}) copy-start(f32[320,1024]{1,0:T(8,128)} %copy-done.3) | copy-start | bytes 3932164
  832.5 117.7 %slice-start.2 = ((s8[4325376]{0:T(1024)(128)(4,1)}), s8[4194304]{0:T(1024)(128)(4,1)S(1)}, s32[]{:S(2)}) async-start(s8[4325376]{0:T(1024)(128)(4,1)} %bitcast.174), calls=%async_computation.7 | async-start | bytes 8388608
  832.5 117.7 %slice-start.3 = ((s8[4325376]{0:T(1024)(128)(4,1)}), s8[131072]{0:T(1024)(128)(4,1)S(1)}, s32[]{:S(2)}) async-start(s8[4325376]{0:T(1024)(128)(4,1)} %bitcast.174), calls=%async_computation.8 | async-start | bytes 262144
  (67 other events, 456.7 us)
Sparse Core Ops, SparseCore 0:
  9.9 35.5 all-gather.5
  48.3 161.0 all-gather.7
  675.0 82.0 all-gather.9
  760.1 154.6 all-reduce.10

commit v3 on v2

--- a/solution.py
+++ b/solution.py
@@ -76,76 +76,91 @@
     return where.at[pl.ds(first, size), pl.ds(pl.multiple_of(col * width, 128), width)]
 
 
-def gather_body(
-    layers, by_rows, src, out, held, store_sem, up_send, down_send, z_recv, send, recv, diag_send, diag_recv
-):
-    me = Place(layers)
-    rows, width = src.shape
-    part = first_part(rows)
-    spans = ((0, part), (part, rows - part))
-
-    owners = (
-        (me.row, me.col),
-        (me.x_row, me.col),
-        (me.row, me.y_col),
-        (me.x_row, me.y_col),
-    )
-    sides = (me.to_x, me.to_y)
-
-    def area(where, row, col, layer, span=None):
-        return piece_of(where, layers, (rows, width), by_rows, row, col, layer, span)
-
-    def held_piece(kind, layer, span=None):
-        return area(held, *owners[kind], layer, span)
-
-    def partner_piece(where, kind, layer):
-        row, col = owners[kind]
-        return area(where, row + 1 - 2 * me.core, col, layer)
-
-    def store(kind, layer, partner):
-        if partner:
-            pair = (partner_piece(held, kind, layer), partner_piece(out, kind, layer))
-        else:
-            pair = (held_piece(kind, layer), area(out, *owners[kind], layer))
-        return pltpu.make_async_copy(*pair, store_sem.at[1 if partner else 0, kind, layer])
-
-    def to_core(kind, layer):
-        piece = held_piece(kind, layer)
-        return remote(piece, piece, send.at[4, kind, layer], recv.at[4, kind, layer], me.to_core)
-
-    def from_core(kind, layer):
-        piece = partner_piece(held, kind, layer)
-        return remote(piece, piece, send.at[4, kind, layer], recv.at[4, kind, layer], me.to_core)
-
-    def beside(axis, half, layer, incoming=False):
-        piece = held_piece(axis + 1 if incoming else 0, layer, spans[half])
+class Gather:
+    def __init__(self, me, layers, by_rows, shape, held, sems):
+        self.me, self.layers, self.by_rows, self.shape, self.held = me, layers, by_rows, shape, held
+        self.up_send, self.down_send, self.z_recv = sems[:3]
+        self.send, self.recv, self.diag_send, self.diag_recv = sems[3:]
+        part = first_part(shape[0])
+        self.spans = ((0, part), (part, shape[0] - part))
+        self.owners = (
+            (me.row, me.col),
+            (me.x_row, me.col),
+            (me.row, me.y_col),
+            (me.x_row, me.y_col),
+        )
+        self.sides = (me.to_x, me.to_y)
+
+    @staticmethod
+    def semaphores(layers):
+        dma = pltpu.SemaphoreType.DMA
+        line = [dma((layers,)) for _ in range(3)]
+        return [*line, dma((5, 4, layers)), dma((5, 4, layers)), dma((2, layers)), dma((2, layers))]
+
+    def area(self, where, row, col, layer, span=None):
+        return piece_of(where, self.layers, self.shape, self.by_rows, row, col, layer, span)
+
+    def piece(self, kind, layer, span=None):
+        return self.area(self.held, *self.owners[kind], layer, span)
+
+    def partner_piece(self, where, kind, layer):
+        row, col = self.owners[kind]
+        return self.area(where, row + 1 - 2 * self.me.core, col, layer)
+
+    def to_core(self, kind, layer):
+        piece = self.piece(kind, layer)
+        sems = (4, kind, layer)
+        return remote(piece, piece, self.send.at[sems], self.recv.at[sems], self.me.to_core)
+
+    def from_core(self, kind, layer):
+        piece = self.partner_piece(self.held, kind, layer)
+        sems = (4, kind, layer)
+        return remote(piece, piece, self.send.at[sems], self.recv.at[sems], self.me.to_core)
+
+    def beside(self, axis, half, layer, incoming=False):
+        piece = self.piece(axis + 1 if incoming else 0, layer, self.spans[half])
         sems = (2 * axis + half, 0, layer)
-        return remote(piece, piece, send.at[sems], recv.at[sems], sides[axis])
-
-    def corner(axis, layer, incoming=False):
-        piece = held_piece(3 if incoming else axis + 1, layer, spans[axis])
+        return remote(piece, piece, self.send.at[sems], self.recv.at[sems], self.sides[axis])
+
+    def corner(self, axis, layer, incoming=False):
+        piece = self.piece(3 if incoming else axis + 1, layer, self.spans[axis])
+        sems = (axis, layer)
         return remote(
-            piece, piece, diag_send.at[axis, layer], diag_recv.at[axis, layer], sides[1 - axis]
-        )
-
-    def along(up, layer):
-        piece = held_piece(0, layer)
+            piece, piece, self.diag_send.at[sems], self.diag_recv.at[sems], self.sides[1 - axis]
+        )
+
+    def along(self, up, layer):
+        piece = self.piece(0, layer)
         return remote(
             piece,
             piece,
-            (up_send if up else down_send).at[layer],
-            z_recv.at[layer],
-            me.above if up else me.below,
-        )
-
-    def spread(layer):
-        beside(0, 0, layer).start()
-        beside(1, 1, layer).start()
-        beside(0, 1, layer).start()
-        beside(1, 0, layer).start()
-        to_core(0, layer).start()
-
-    def at_distance(distance, act):
+            (self.up_send if up else self.down_send).at[layer],
+            self.z_recv.at[layer],
+            self.me.above if up else self.me.below,
+        )
+
+    def pass_on(self, up, layer):
+        me = self.me
+
+        @pl.when((me.layer < self.layers - 1) if up else (me.layer > 0))
+        def _():
+            self.along(up, layer).start()
+
+    def spread(self, layer):
+        self.beside(0, 0, layer).start()
+        self.beside(1, 1, layer).start()
+        self.beside(0, 1, layer).start()
+        self.beside(1, 0, layer).start()
+        self.to_core(0, layer).start()
+
+    def begin(self):
+        if self.layers > 1:
+            self.pass_on(True, self.me.layer)
+            self.pass_on(False, self.me.layer)
+        self.spread(self.me.layer)
+
+    def at_distance(self, distance, act):
+        me = self.me
         if distance == 0:
             act(me.layer, None)
             return
@@ -154,87 +169,95 @@
         def _():
             act(me.layer - distance, True)
 
-        @pl.when(me.layer + distance < layers)
+        @pl.when(me.layer + distance < self.layers)
         def _():
             act(me.layer + distance, False)
 
-    own = pltpu.make_async_copy(src, held_piece(0, me.layer), store_sem.at[0, 0, me.layer])
+    def arrived(self, layer, upward):
+        self.along(upward, layer).wait_recv()
+        self.pass_on(upward, layer)
+        self.spread(layer)
+
+    def second(self, layer):
+        for axis in (0, 1):
+            self.beside(axis, axis, layer, True).wait_recv()
+            self.corner(axis, layer).start()
+        for axis in (0, 1):
+            self.beside(axis, 1 - axis, layer, True).wait_recv()
+            self.to_core(axis + 1, layer).start()
+
+    def third(self, layer):
+        for axis in (0, 1):
+            self.corner(axis, layer, True).wait_recv()
+        self.to_core(3, layer).start()
+
+    def finish(self):
+        me, layers = self.me, self.layers
+        for layer in range(layers):
+            for kind in range(4):
+                self.to_core(kind, layer).wait_send()
+            for axis in (0, 1):
+                for half in (0, 1):
+                    self.beside(axis, half, layer).wait_send()
+                self.corner(axis, layer).wait_send()
+        if layers > 1:
+            for layer in range(layers):
+
+                @pl.when((me.layer < layers - 1) & (layer <= me.layer))
+                def _():
+                    self.along(True, layer).wait_send()
+
+                @pl.when((me.layer > 0) & (layer >= me.layer))
+                def _():
+                    self.along(False, layer).wait_send()
+
+
+def gather_body(layers, by_rows, src, out, held, store_sem, *sems):
+    me = Place(layers)
+    work = Gather(me, layers, by_rows, src.shape, held, sems)
+
+    def store(kind, layer, partner):
+        if partner:
+            pair = (work.partner_piece(held, kind, layer), work.partner_piece(out, kind, layer))
+        else:
+            pair = (work.piece(kind, layer), work.area(out, *work.owners[kind], layer))
+        return pltpu.make_async_copy(*pair, store_sem.at[1 if partner else 0, kind, layer])
+
+    own = pltpu.make_async_copy(src, work.piece(0, me.layer), store_sem.at[0, 0, me.layer])
     own.start()
     me.greet()
     own.wait()
-    if layers > 1:
-
-        @pl.when(me.layer < layers - 1)
-        def _():
-            along(True, me.layer).start()
-
-        @pl.when(me.layer > 0)
-        def _():
-            along(False, me.layer).start()
-
-    spread(me.layer)
+    work.begin()
     store(0, me.layer, False).start()
 
     def arrived(layer, upward):
-        along(upward, layer).wait_recv()
-        if upward:
-
-            @pl.when(me.layer < layers - 1)
-            def _():
-                along(True, layer).start()
-        else:
-
-            @pl.when(me.layer > 0)
-            def _():
-                along(False, layer).start()
-
-        spread(layer)
+        work.arrived(layer, upward)
         store(0, layer, False).start()
 
     def second(layer, upward):
-        for axis in (0, 1):
-            beside(axis, axis, layer, True).wait_recv()
-            corner(axis, layer).start()
-        for axis in (0, 1):
-            beside(axis, 1 - axis, layer, True).wait_recv()
-            to_core(axis + 1, layer).start()
-            store(axis + 1, layer, False).start()
+        work.second(layer)
+        for kind in (1, 2):
+            store(kind, layer, False).start()
 
     def third(layer, upward):
-        for axis in (0, 1):
-            corner(axis, layer, True).wait_recv()
-        to_core(3, layer).start()
+        work.third(layer)
         store(3, layer, False).start()
         for kind in range(4):
-            from_core(kind, layer).wait_recv()
+            work.from_core(kind, layer).wait_recv()
             store(kind, layer, True).start()
 
     for step in range(1, layers + 2):
         if step < layers:
-            at_distance(step, arrived)
+            work.at_distance(step, arrived)
         if step - 1 < layers:
-            at_distance(step - 1, second)
+            work.at_distance(step - 1, second)
         if 0 <= step - 2 < layers:
-            at_distance(step - 2, third)
+            work.at_distance(step - 2, third)
     for layer in range(layers):
         for kind in range(4):
-            to_core(kind, layer).wait_send()
             store(kind, layer, False).wait()
             store(kind, layer, True).wait()
-        for axis in (0, 1):
-            for half in (0, 1):
-                beside(axis, half, layer).wait_send()
-            corner(axis, layer).wait_send()
-    if layers > 1:
-        for layer in range(layers):
-
-            @pl.when((me.layer < layers - 1) & (layer <= me.layer))
-            def _():
-                along(True, layer).wait_send()
-
-            @pl.when((me.layer > 0) & (layer >= me.layer))
-            def _():
-                along(False, layer).wait_send()
+    work.finish()
 
 
 def gather(value, layers, collective_id, by_rows=False):
@@ -249,13 +272,7 @@
         scratch_shapes=[
             pltpu.VMEM(whole, value.dtype),
             dma((2, 4, layers)),
-            dma((layers,)),
-            dma((layers,)),
-            dma((layers,)),
-            dma((5, 4, layers)),
-            dma((5, 4, layers)),
-            dma((2, layers)),
-            dma((2, layers)),
+            *Gather.semaphores(layers),
         ],
         compiler_params=pltpu.CompilerParams(
             collective_id=collective_id,
@@ -530,6 +547,309 @@
     )
 
 
+def made_scatter_body(layers, parts, *refs):
+    slots_hbm, refs = refs[:parts], refs[parts:]
+    weights_hbm, refs = refs[:parts], refs[parts:]
+    spread_hbm, side_hbm, side_w_hbm, out, refs = *refs[:4], refs[4:]
+    slots_in, refs = refs[:parts], refs[parts:]
+    weights, refs = refs[:parts], refs[parts:]
+    spread_in, side_in, side_w, slot_rows, refs = *refs[:4], refs[4:]
+    core_out, acc, core_in, diag_a, diag_b, beside_in, line_in, refs = *refs[:7], refs[7:]
+    in_sem, weight_sem, core_send, core_recv, diag_send, diag_recv, side_send, side_recv = refs[:8]
+    line_send, line_recv = refs[8:]
+    me = Place(layers)
+    rows, width = out.shape
+    part = first_part(rows)
+    f32 = jnp.float32
+    per_block, few, slots = spread_in.shape[2:]
+    x_mine = me.row // 2
+
+    def layer_at(step):
+        return nearest_first(layers, layers - 1 - step, me.layer)
+
+    def loads(unit):
+        step, own = unit // 2, lax.rem(unit, 2)
+        core = me.core * own + (1 - me.core) * (1 - own)
+        slot = lax.rem(unit, 2)
+        layer = layer_at(step)
+        pairs = [*zip(slots_hbm, slots_in), (spread_hbm, spread_in), (side_hbm, side_in)]
+        return [
+            pltpu.make_async_copy(
+                src.at[x_mine if x == 0 else 1 - x_mine, core, layer],
+                dst.at[slot, x],
+                in_sem.at[slot, i, x],
+            )
+            for i, (src, dst) in enumerate(pairs)
+            for x in range(2)
+        ]
+
+    def weight_loads():
+        pairs = [*zip(weights_hbm, weights), (side_w_hbm, side_w)]
+        copies = []
+        for i, (src, dst) in enumerate(pairs):
+            for at, col in enumerate((me.col, me.y_col)):
+                copies.append(
+                    pltpu.make_async_copy(
+                        src.at[:, pl.ds(pl.multiple_of(col * width, 128), width)],
+                        dst.at[:, pl.ds(at * width, width)],
+                        weight_sem.at[i, at],
+                    )
+                )
+        return copies
+
+    def make(unit, put):
+        for copy in loads(unit):
+            copy.wait()
+
+        @pl.when(unit + 1 < 2 * layers)
+        def _():
+            for copy in loads(unit + 1):
+                copy.start()
+
+        slot = lax.rem(unit, 2)
+        total = sum(
+            dot_nn(value[slot].reshape(-1, value.shape[-1]), weight[...])
+            for value, weight in zip(slots_in, weights)
+        )
+        slot_rows[...] = total.astype(slot_rows.dtype)
+        for x in range(2):
+            for j in range(per_block):
+                there = pl.ds(j * few, few)
+                here = pl.ds((x * per_block + j) * slots, slots)
+                made = dot_nn(spread_in[slot, x, j], slot_rows[here, :]) + dot_nn(
+                    side_in[slot, x, there, :], side_w[...]
+                )
+                put(x, there, made[:, :width].astype(acc.dtype))
+                put(x + 2, there, made[:, width:].astype(acc.dtype))
+
+    def to_core(step, kind):
+        return remote(
+            core_out.at[lax.rem(step, 2), kind],
+            core_in.at[step, kind],
+            core_send.at[step, kind],
+            core_recv.at[step, kind],
+            me.to_core,
+        )
+
+    def diag(step, axis):
+        start, size = ((0, part), (part, rows - part))[axis]
+        return remote(
+            acc.at[step, 3, pl.ds(start, size)],
+            (diag_a, diag_b)[axis].at[step],
+            diag_send.at[axis, step],
+            diag_recv.at[axis, step],
+            (me.to_y, me.to_x)[axis],
+        )
+
+    def side(step, axis):
+        return remote(
+            acc.at[step, axis + 1],
+            beside_in.at[axis, step],
+            side_send.at[axis, step],
+            side_recv.at[axis, step],
+            (me.to_x, me.to_y)[axis],
+        )
+
+    def line(step, up):
+        layer = layer_at(step)
+        way = 0 if up else 1
+        return remote(
+            acc.at[step, 0],
+            line_in.at[way, layer],
+            line_send.at[step],
+            line_recv.at[way, layer],
+            me.above if up else me.below,
+        )
+
+    lanes = 32 if part % 32 == 0 and rows % 32 == 0 else 16
+
+    def add(target, others, start=0, size=rows, into=None):
+        def step(i, carry):
+            first = pl.multiple_of(i * lanes, 16)
+            total = target[pl.ds(start + first, lanes), :].astype(f32)
+            for other in others:
+                total = total + other[pl.ds(first, lanes), :].astype(f32)
+            if into is None:
+                target[pl.ds(start + first, lanes), :] = total.astype(target.dtype)
+            else:
+                into[pl.ds(first, lanes), :] = total.astype(into.dtype)
+            return carry
+
+        lax.fori_loop(0, size // lanes, step, 0)
+
+    for copy in (*weight_loads(), *loads(0)):
+        copy.start()
+    me.greet()
+    for copy in weight_loads():
+        copy.wait()
+
+    def produce(step):
+        @pl.when(step >= 2)
+        def _():
+            for kind in range(4):
+                to_core(step - 2, kind).wait_send()
+
+        half = lax.rem(step, 2)
+
+        def to_other(kind, there, value):
+            core_out[half, kind, there, :] = value
+
+        make(2 * step, to_other)
+        for kind in (3, 1, 2, 0):
+            to_core(step, kind).start()
+
+        def to_own(kind, there, value):
+            acc[step, kind, there, :] = value
+
+        make(2 * step + 1, to_own)
+
+    def stage_a(step):
+        to_core(step, 3).wait_recv()
+        add(acc.at[step, 3], [core_in.at[step, 3]])
+        diag(step, 0).start()
+        diag(step, 1).start()
+
+    def stage_b(step):
+        for axis, buffer, start, size in (
+            (0, diag_a, 0, part),
+            (1, diag_b, part, rows - part),
+        ):
+            kind = axis + 1
+            to_core(step, kind).wait_recv()
+            add(acc.at[step, kind], [core_in.at[step, kind]])
+            diag(step, axis).wait_recv()
+            add(acc.at[step, kind], [buffer.at[step]], start, size)
+            side(step, axis).start()
+
+    def stage_c(step):
+        to_core(step, 0).wait_recv()
+        side(step, 0).wait_recv()
+        side(step, 1).wait_recv()
+        add(acc.at[step, 0], [core_in.at[step, 0], beside_in.at[0, step], beside_in.at[1, step]])
+        layer = layer_at(step)
+
+        @pl.when((layer > me.layer) & (me.layer > 0))
+        def _():
+            line(step, True).wait_recv()
+            add(acc.at[step, 0], [line_in.at[0, layer]])
+
+        @pl.when((layer < me.layer) & (me.layer < layers - 1))
+        def _():
+            line(step, False).wait_recv()
+            add(acc.at[step, 0], [line_in.at[1, layer]])
+
+        @pl.when(layer > me.layer)
+        def _():
+            line(step, True).start()
+
+        @pl.when(layer < me.layer)
+        def _():
+            line(step, False).start()
+
+    def stages(step, carry):
+        @pl.when(step < layers)
+        def _():
+            produce(step)
+            stage_a(step)
+
+        @pl.when((step >= 1) & (step <= layers))
+        def _():
+            stage_b(step - 1)
+
+        @pl.when(step >= 2)
+        def _():
+            stage_c(step - 2)
+
+        return carry
+
+    lax.fori_loop(0, layers + 2, stages, 0)
+    last = layers - 1
+
+    @pl.when(me.layer > 0)
+    def _():
+        line(last, True).wait_recv()
+
+    @pl.when(me.layer < last)
+    def _():
+        line(last, False).wait_recv()
+
+    @pl.when((me.layer > 0) & (me.layer < last))
+    def _():
+        add(acc.at[last, 0], [line_in.at[0, me.layer], line_in.at[1, me.layer]], into=out)
+
+    @pl.when(me.layer == 0)
+    def _():
+        add(acc.at[last, 0], [line_in.at[1, me.layer]], into=out)
+
+    @pl.when(me.layer == last)
+    def _():
+        add(acc.at[last, 0], [line_in.at[0, me.layer]], into=out)
+
+    for step in range(layers):
+        if step >= layers - 2:
+            for kind in range(4):
+                to_core(step, kind).wait_send()
+        for axis in (0, 1):
+            diag(step, axis).wait_send()
+            side(step, axis).wait_send()
+        if step < last:
+
+            @pl.when(layer_at(step) > me.layer)
+            def _():
+                line(step, True).wait_send()
+
+            @pl.when(layer_at(step) < me.layer)
+            def _():
+                line(step, False).wait_send()
+
+
+def made_scatter(slots_in, weights, spread, side, side_w, layers, collective_id):
+    block, width = side.shape[3], side_w.shape[1] // 2
+    bf16 = jnp.bfloat16
+    parts = len(weights)
+    part = first_part(block)
+    dma = pltpu.SemaphoreType.DMA
+    buffer = lambda *lead: pltpu.VMEM((*lead, block, width), bf16)
+    ahead = lambda value: pltpu.VMEM((2, 2, *value.shape[3:]), bf16)
+    in_hbm = pl.BlockSpec(memory_space=pl.ANY)
+    return pl.pallas_call(
+        functools.partial(made_scatter_body, layers, parts),
+        out_shape=jax.ShapeDtypeStruct((block, width), jnp.float32),
+        in_specs=[in_hbm] * (2 * parts + 3),
+        out_specs=pl.BlockSpec(memory_space=pltpu.VMEM),
+        scratch_shapes=[
+            *(ahead(value) for value in slots_in),
+            *(pltpu.VMEM(value.shape, bf16) for value in weights),
+            ahead(spread),
+            ahead(side),
+            pltpu.VMEM(side_w.shape, bf16),
+            pltpu.VMEM((2 * slots_in[0].shape[3], 2 * width), bf16),
+            buffer(2, 4),
+            buffer(layers, 4),
+            buffer(layers, 4),
+            pltpu.VMEM((layers, part, width), bf16),
+            pltpu.VMEM((layers, block - part, width), bf16),
+            buffer(2, layers),
+            buffer(2, layers),
+            dma((2, parts + 2, 2)),
+            dma((parts + 1, 2)),
+            dma((layers, 4)),
+            dma((layers, 4)),
+            dma((2, layers)),
+            dma((2, layers)),
+            dma((2, layers)),
+            dma((2, layers)),
+            dma((layers,)),
+            dma((2, layers)),
+        ],
+        compiler_params=pltpu.CompilerParams(
+            collective_id=collective_id,
+            has_side_effects=True,
+            vmem_limit_bytes=62 * 1024 * 1024,
+        ),
+    )(*slots_in, *weights, spread, side, side_w)
+
+
 def small_sum_body(layers, src, out, core_in, mid, x_in, near, line_in, total, send, recv, line_send, line_recv):
     me = Place(layers)
     width = src.shape[1]
@@ -607,50 +927,167 @@
     )(value)
 
 
+def nearest_first(layers, turn, layer):
+    found = 0
+    for here in range(layers):
+        order = sorted(range(layers), key=lambda other: (abs(other - here), other))
+        for at in range(layers):
+            found = found + jnp.where((layer == here) & (turn == at), order[at], 0)
+    return found
+
+
 def expert_body(
     layers,
-    few,
-    slots,
     units,
     experts,
-    rows_ref,
+    src,
     grads_ref,
     pick_ref,
     spread_ref,
     words_ref,
-    gate_w,
-    up_w,
-    down_w,
-    side_w,
-    side_down,
-    d_rows_ref,
-    out_ref,
+    gate_hbm,
+    up_hbm,
+    down_hbm,
+    side_hbm,
+    side_down_hbm,
+    rows_all,
     slot_rows_ref,
     slot_grads_ref,
     hidden_ref,
     d_gate_ref,
     d_up_ref,
     d_gates_ref,
+    side_hidden_ref,
+    d_side_ref,
     grad_side_ref,
     grad_side_down_ref,
-    d_slots,
-    slot_out,
-    side_hidden_ref,
-    d_side_ref,
+    gate_w,
+    up_w,
+    down_w,
+    side_w,
+    side_down,
+    both_rows,
+    side_hidden,
+    d_side,
+    weight_sem,
+    rows_sem,
+    *sems,
 ):
     bf16, f32 = jnp.bfloat16, jnp.float32
-    own_expert = lax.axis_index("row") * layers + lax.axis_index("exp")
-    count = rows_ref.shape[0] // few
-    block, half = grads_ref.shape[2:]
+    me = Place(layers)
+    work = Gather(me, layers, False, src.shape, rows_all, sems)
+    own_expert = me.row * layers + me.layer
+    block, half = src.shape
+    width = 2 * half
+    few, slots = pick_ref.shape[5], pick_ref.shape[4]
+    per_block = block // few
+    count = 2 * per_block
     lanes = side_down.shape[0]
-
-    side = dot_nt(rows_ref[...], side_w[...])
+    step = pl.program_id(0)
+    steps = 2 * layers
+    weight_loads = [
+        pltpu.make_async_copy(src_ref, dst_ref, weight_sem.at[i])
+        for i, (src_ref, dst_ref) in enumerate(
+            (
+                (down_hbm, down_w),
+                (side_down_hbm, side_down),
+                (side_hbm, side_w),
+                (gate_hbm, gate_w),
+                (up_hbm, up_w),
+            )
+        )
+    ]
+
+    def load(which, core):
+        layer = nearest_first(layers, which // 2, me.layer)
+        far = lax.rem(which, 2)
+        x_place = me.row // 2 * (1 - far) + (1 - me.row // 2) * far
+        first = pl.multiple_of(((2 * x_place + core) * layers + layer) * block, 16)
+        slot = lax.rem(which, 2)
+        return pltpu.make_async_copy(
+            rows_all.at[pl.ds(first, block)],
+            both_rows.at[slot, pl.ds(core * block, block)],
+            rows_sem.at[slot, core],
+        )
+
+    def prepare(which):
+        for distance in range(1, layers):
+
+            @pl.when(which == distance - 1)
+            def _():
+                work.at_distance(distance, work.arrived)
+
+        for turn in range(layers):
+            at = nearest_first(layers, turn, me.layer)
+            if turn > 0:
+
+                @pl.when(which == 2 * turn - 1)
+                def _():
+                    work.second(at)
+
+            @pl.when(which == max(1, 2 * turn))
+            def _():
+                work.third(at)
+
+        layer = nearest_first(layers, which // 2, me.layer)
+
+        @pl.when(lax.rem(which, 2) == 0)
+        def _():
+            work.from_core(0, layer).wait_recv()
+            work.from_core(2, layer).wait_recv()
+
+        @pl.when(lax.rem(which, 2) == 1)
+        def _():
+            work.from_core(1, layer).wait_recv()
+            work.from_core(3, layer).wait_recv()
+
+        for core in range(2):
+            load(which, core).start()
+
+    @pl.when(step == 0)
+    def _():
+        own = pltpu.make_async_copy(src, work.piece(0, me.layer), rows_sem.at[0, 0])
+        own.start()
+        for copy in weight_loads:
+            copy.start()
+        me.greet()
+        own.wait()
+        work.begin()
+        for copy in weight_loads:
+            copy.wait()
+        work.second(me.layer)
+        prepare(step)
+
+    rows = both_rows.at[lax.rem(step, 2)]
+
+    def spot(b):
+        core, j = b // per_block, b % per_block
+        return core, j, pl.ds(b * few, few), pl.ds(j * slots, slots)
+
+    for b in range(count):
+        core, j, _, here = spot(b)
+        for c in range(2):
+            slot_grads_ref[0, core, 0, here, c * half : (c + 1) * half] = dot_nn(
+                pick_ref[0, core, 0, j], grads_ref[0, core, 0, c, j * few : (j + 1) * few, :]
+            ).astype(bf16)
+    join = lambda ref: jnp.concatenate([ref[0, core, 0] for core in range(2)], axis=0)
+    d_raw = dot_nt(join(slot_grads_ref), down_w[...])
+    side_grads = [
+        jnp.concatenate([grads_ref[0, core, 0, c] for core in range(2)], axis=0) for c in range(2)
+    ]
+    d_side_hidden = sum(
+        dot_nt(side_grads[c], side_down[:, c * half : (c + 1) * half]) for c in range(2)
+    )
+    for core in range(2):
+        load(step, core).wait()
+
+    side = dot_nt(rows[...], side_w[...])
     side_gate, side_up = side[:, :lanes], side[:, lanes:]
     lane = lax.broadcasted_iota(jnp.int32, side_gate.shape, 1)
     expert = lane - units
     is_expert = (expert >= 0) & (expert < experts)
     highest = jnp.max(jnp.where(is_expert, side_gate, -jnp.inf), axis=1, keepdims=True)
-    words = words_ref[...]
+    words = join(words_ref)
     word = words[:, 0:1]
     for i in range(1, words.shape[1]):
         word = jnp.where(expert >= 16 * i, words[:, i : i + 1], word)
@@ -670,129 +1107,149 @@
     own_parts = two_parts(own)
     slot_gates = []
     for b in range(count):
-        tokens, here = pl.ds(b * few, few), pl.ds(b * slots, slots)
-        pick = pick_ref[here, :]
-        slot_rows_ref[here, :] = dot_nn(pick, rows_ref[tokens, :]).astype(bf16)
-        first = b * few % block
-        for c in range(2):
-            slot_grads_ref[here, c * half : (c + 1) * half] = dot_nn(
-                pick, grads_ref[b * few // block, c, first : first + few, :]
-            ).astype(bf16)
+        core, j, tokens, here = spot(b)
+        pick = pick_ref[0, core, 0, j]
+        slot_rows_ref[0, core, 0, here, :] = dot_nn(pick, rows[tokens, :]).astype(bf16)
         parts = dot_nn(pick, own_parts[b * few : (b + 1) * few])
         slot_gates.append(jnp.sum(parts, axis=1, keepdims=True))
     slot_gate = jnp.concatenate(slot_gates, axis=0)
 
-    gate_pre = dot_nt(slot_rows_ref[...], gate_w[...])
-    up_pre = dot_nt(slot_rows_ref[...], up_w[...])
-    d_raw = dot_nt(slot_grads_ref[...], down_w[...])
+    slot_rows = join(slot_rows_ref)
+    gate_pre = dot_nt(slot_rows, gate_w[...])
+    up_pre = dot_nt(slot_rows, up_w[...])
     sigmoid = 1.0 / (1.0 + jnp.exp(-gate_pre))
     silu = gate_pre * sigmoid
     hidden = (silu * up_pre).astype(bf16).astype(f32)
     d_gates = jnp.sum(d_raw * hidden, axis=1, keepdims=True)
-    hidden_ref[...] = (hidden * slot_gate).astype(bf16)
     d_hidden = d_raw * slot_gate
-    d_up_ref[...] = (d_hidden * silu).astype(bf16)
-    d_gate_ref[...] = (
-        d_hidden * up_pre * sigmoid * (1.0 + gate_pre * (1.0 - sigmoid))
-    ).astype(bf16)
-    d_slots[...] = (dot_nn(d_gate_ref[...], gate_w[...]) + dot_nn(d_up_ref[...], up_w[...])).astype(
-        bf16
-    )
-    slot_out[...] = dot_nn(hidden_ref[...], down_w[...]).astype(bf16)
+    each = per_block * slots
+
+    def keep(ref, value):
+        for core in range(2):
+            ref[0, core, 0] = value[core * each : (core + 1) * each]
+
+    hidden = (hidden * slot_gate).astype(bf16)
+    keep(hidden_ref, hidden)
+    d_up = (d_hidden * silu).astype(bf16)
+    keep(d_up_ref, d_up)
+    d_gate = (d_hidden * up_pre * sigmoid * (1.0 + gate_pre * (1.0 - sigmoid))).astype(bf16)
+    keep(d_gate_ref, d_gate)
+
+    @pl.when(step + 1 < steps)
+    def _():
+        prepare(step + 1)
 
     side_sigmoid = 1.0 / (1.0 + jnp.exp(-side_gate))
     side_silu = side_gate * side_sigmoid
-    side_hidden_ref[...] = (side_silu * side_up).astype(bf16)
-    d_side_hidden = sum(
-        dot_nt(grads_ref[:, c].reshape(-1, half), side_down[:, c * half : (c + 1) * half])
-        for c in range(2)
-    )
-    d_side_ref[:, lanes:] = (d_side_hidden * side_silu).astype(bf16)
-    d_side_ref[:, :lanes] = (
+    side_hidden[...] = (side_silu * side_up).astype(bf16)
+    d_side[:, lanes:] = (d_side_hidden * side_silu).astype(bf16)
+    d_side[:, :lanes] = (
         d_side_hidden * side_up * side_sigmoid * (1.0 + side_gate * (1.0 - side_sigmoid))
     ).astype(bf16)
 
-    @pl.when(pl.program_id(0) == 0)
+    @pl.when(step == 0)
     def _():
         grad_side_ref[...] = jnp.zeros_like(grad_side_ref)
         grad_side_down_ref[...] = jnp.zeros_like(grad_side_down_ref)
 
-    grad_side_ref[...] += dot_tn(d_side_ref[...], rows_ref[...])
+    grad_side_ref[...] += dot_tn(d_side[...], rows[...])
     for c in range(2):
-        grad_side_down_ref[:, c * half : (c + 1) * half] += dot_tn(
-            side_hidden_ref[...], grads_ref[:, c].reshape(-1, half)
-        )
+        grad_side_down_ref[:, c * half : (c + 1) * half] += dot_tn(side_hidden[...], side_grads[c])
 
     d_gate_parts = two_parts(d_gates)
     for b in range(count):
-        tokens, here = pl.ds(b * few, few), pl.ds(b * slots, slots)
-        spread = spread_ref[tokens, :]
-        d_rows_ref[tokens, :] = (
-            dot_nn(spread, d_slots[here, :]) + dot_nn(d_side_ref[tokens, :], side_w[...])
-        ).astype(bf16)
-        out_ref[tokens, :] = (
-            dot_nn(spread, slot_out[here, :]) + dot_nn(side_hidden_ref[tokens, :], side_down[...])
-        ).astype(bf16)
-        back = dot_nn(spread, d_gate_parts[b * slots : (b + 1) * slots])
-        d_gates_ref[tokens, :] = jnp.sum(back, axis=1, keepdims=True)
-
-
-def expert_pass(layers, few, slots, units, experts, rows, grads, pick, spread, words, weights, side_w, side_down):
-    tokens, width = rows.shape
+        core, j, tokens, _ = spot(b)
+        there = pl.ds(j * few, few)
+        back = dot_nn(spread_ref[0, core, 0, j], d_gate_parts[b * slots : (b + 1) * slots])
+        d_gates_ref[0, core, 0, there, :] = jnp.sum(back, axis=1, keepdims=True)
+        side_hidden_ref[0, core, 0, there, :] = side_hidden[tokens, :]
+        d_side_ref[0, core, 0, there, :] = d_side[tokens, :]
+
+    @pl.when(step == steps - 1)
+    def _():
+        work.finish()
+
+
+def expert_pass(layers, few, slots, units, experts, rows_own, grads, pick, spread, words, weights, side_w, side_down):
+    block, half = rows_own.shape
+    width = 2 * half
     hidden = weights[0].shape[0]
-    block = grads.shape[2]
-    blocks = tokens // few
-    count = next(n for n in (4, 2, 1) if blocks % n == 0 and n * few <= 640)
+    per_block = block // few
+    tokens = 4 * layers * block
     lanes = side_down.shape[0]
-    grid = (blocks // count,)
-    by_step = lambda n, w: pl.BlockSpec((count * n, w), lambda i: (i, 0))
-    whole = lambda value: pl.BlockSpec(
-        value.shape, lambda i: (0, 0), pipeline_mode=pl.Buffered(1)
-    )
-    shape = lambda n, w, kind=jnp.bfloat16: jax.ShapeDtypeStruct((blocks * n, w), kind)
-    return pl.pallas_call(
-        functools.partial(expert_body, layers, few, slots, units, experts),
-        grid=grid,
+
+    def by_step(*tail):
+        def place(step):
+            row = lax.axis_index("row")
+            layer = nearest_first(layers, step // 2, lax.axis_index("exp"))
+            far = lax.rem(step, 2)
+            x_place = row // 2 * (1 - far) + (1 - row // 2) * far
+            return (x_place, 0, layer, *(0 for _ in tail))
+
+        return pl.BlockSpec((1, 2, 1, *tail), place)
+
+    shape = lambda *tail, kind=jnp.bfloat16: jax.ShapeDtypeStruct((2, 2, layers, *tail), kind)
+    each = per_block * slots
+    outs = pl.pallas_call(
+        functools.partial(expert_body, layers, units, experts),
+        grid=(2 * layers,),
         in_specs=[
-            by_step(few, width),
-            pl.BlockSpec((count * few // block, 2, block, width // 2), lambda i: (i, 0, 0, 0)),
-            by_step(slots, few),
-            by_step(few, slots),
-            by_step(few, words.shape[1]),
-            *(whole(w) for w in (*weights, side_w, side_down)),
+            pl.BlockSpec(memory_space=pl.ANY),
+            by_step(2, block, half),
+            by_step(per_block, slots, few),
+            by_step(per_block, few, slots),
+            by_step(block, words.shape[1]),
+            *[pl.BlockSpec(memory_space=pl.ANY)] * 5,
         ],
         out_specs=[
-            by_step(few, width),
-            by_step(few, width),
-            by_step(slots, width),
-            by_step(slots, width),
-            by_step(slots, hidden),
-            by_step(slots, hidden),
-            by_step(slots, hidden),
-            by_step(few, 1),
+            pl.BlockSpec(memory_space=pl.ANY),
+            by_step(each, width),
+            by_step(each, width),
+            by_step(each, hidden),
+            by_step(each, hidden),
+            by_step(each, hidden),
+            by_step(block, 1),
+            by_step(block, lanes),
+            by_step(block, 2 * lanes),
             pl.BlockSpec((2 * lanes, width), lambda i: (0, 0)),
             pl.BlockSpec((lanes, width), lambda i: (0, 0)),
         ],
         out_shape=[
-            shape(few, width),
-            shape(few, width),
-            shape(slots, width),
-            shape(slots, width),
-            shape(slots, hidden),
-            shape(slots, hidden),
-            shape(slots, hidden),
-            shape(few, 1, jnp.float32),
+            jax.ShapeDtypeStruct((tokens, width), jnp.bfloat16),
+            shape(each, width),
+            shape(each, width),
+            shape(each, hidden),
+            shape(each, hidden),
+            shape(each, hidden),
+            shape(block, 1, kind=jnp.float32),
+            shape(block, lanes),
+            shape(block, 2 * lanes),
             jax.ShapeDtypeStruct((2 * lanes, width), jnp.float32),
             jax.ShapeDtypeStruct((lanes, width), jnp.float32),
         ],
         scratch_shapes=[
-            pltpu.VMEM((count * slots, width), jnp.bfloat16),
-            pltpu.VMEM((count * slots, width), jnp.bfloat16),
-            pltpu.VMEM((count * few, lanes), jnp.bfloat16),
-            pltpu.VMEM((count * few, 2 * lanes), jnp.bfloat16),
+            *(pltpu.VMEM(w.shape, jnp.bfloat16) for w in (*weights, side_w, side_down)),
+            pltpu.VMEM((2, 2 * block, width), jnp.bfloat16),
+            pltpu.VMEM((2 * block, lanes), jnp.bfloat16),
+            pltpu.VMEM((2 * block, 2 * lanes), jnp.bfloat16),
+            pltpu.SemaphoreType.DMA((5,)),
+            pltpu.SemaphoreType.DMA((2, 2)),
+            *Gather.semaphores(layers),
         ],
-        compiler_params=pltpu.CompilerParams(vmem_limit_bytes=62 * 1024 * 1024),
-    )(rows, grads, pick, spread, words, *weights, side_w, side_down)
+        compiler_params=pltpu.CompilerParams(
+            collective_id=3, has_side_effects=True, vmem_limit_bytes=62 * 1024 * 1024
+        ),
+    )(
+        rows_own,
+        grads.reshape(2, 2, layers, 2, block, half),
+        pick.reshape(2, 2, layers, per_block, slots, few),
+        spread.reshape(2, 2, layers, per_block, few, slots),
+        words.reshape(2, 2, layers, block, -1),
+        *weights,
+        side_w,
+        side_down,
+    )
+    return outs
 
 
 def rotate(value, cosine, sine):
@@ -906,16 +1363,16 @@
 
     grads_all = lax.all_gather(grads_own, ("row", "exp", "col"), axis=0)
     grads_all = grads_all.reshape(experts, 2, block, half_width)
-    normed_all = gather(normed_own, layers, 3)
     (
-        d_rows,
-        out_rows,
+        normed_all,
         slot_rows,
         slot_grads,
         hidden,
         d_gate,
         d_up,
         d_gates_all,
+        side_hidden,
+        d_side,
         grad_side,
         grad_side_down,
     ) = expert_pass(
@@ -924,19 +1381,25 @@
         slots,
         units,
         experts,
-        normed_all,
+        normed_own,
         grads_all,
-        pick.reshape(blocks * slots, few),
-        spread.reshape(tokens, slots),
+        pick,
+        spread,
         words,
         expert_weights,
         side_w,
         side_down,
     )
-    d_normed = scatter(d_rows, layers, 4)
-    grad_gate = dot_tn(d_gate, slot_rows)
-    grad_up = dot_tn(d_up, slot_rows)
-    grad_down = dot_tn(hidden, slot_grads)
+    spread = spread.reshape(2, 2, layers, -1, few, slots)
+    gate_weight, up_weight, down_weight = expert_weights
+    d_normed = made_scatter(
+        (d_gate, d_up), (gate_weight, up_weight), spread, d_side, side_w, layers, 4
+    )
+    out_parts = ((hidden,), (down_weight,), spread, side_hidden, side_down)
+    flat = lambda value: value.reshape(-1, value.shape[-1])
+    grad_gate = dot_tn(flat(d_gate), flat(slot_rows))
+    grad_up = dot_tn(flat(d_up), flat(slot_rows))
+    grad_down = dot_tn(flat(hidden), flat(slot_grads))
     grad_shared = jnp.stack(
         [grad_side[:units], grad_side[lanes : lanes + units], grad_side_down[:units]]
     )
@@ -981,7 +1444,7 @@
         precision=lax.Precision.HIGHEST,
         preferred_element_type=jnp.float32,
     )
-    return (d_normed, out_rows, (grad_gate, grad_up, grad_down, grad_shared, grad_router))
+    return (d_normed, out_parts, (grad_gate, grad_up, grad_down, grad_shared, grad_router))
 
 
 def per_device(
@@ -1117,13 +1580,13 @@
         shared_own,
     )
     if pieces == 1:
-        d_normed, out_rows, weight_grads = feed(normed_two, cotangent, words_all)
+        d_normed, out_parts, weight_grads = feed(normed_two, cotangent, words_all)
     else:
         piece_rows = block // pieces
 
         def one_piece(total, items):
-            d_rows, out_rows, grads = feed(*items)
-            return (jax.tree.map(jnp.add, total, grads), (d_rows, scatter(out_rows, exps_n, 4)))
+            d_rows, out_parts, grads = feed(*items)
+            return (jax.tree.map(jnp.add, total, grads), (d_rows, made_scatter(*out_parts, exps_n, 9)))
 
         split = lambda value: value.reshape(pieces, piece_rows, half_width)
         word_pieces = words_all.reshape(experts, pieces, piece_rows, words_n)
@@ -1238,8 +1701,8 @@
     d_norm_one, grad_gain_one = norm_back(input_wide, factor_one, gain_one, d_first, width)
     input_grad = d_hidden_state + d_norm_one
     if pieces == 1:
-        out_rows, input_grad = lax.optimization_barrier((out_rows, input_grad))
-        branch = scatter(out_rows, exps_n, 4)
+        out_parts, input_grad = lax.optimization_barrier((out_parts, input_grad))
+        branch = made_scatter(*out_parts, exps_n, 9)
     output = (hidden_state + branch).astype(bf16)
 
     small = jnp.concatenate(

time: 977 us -> 905 us (0.926)
  Pallas kernels: 677 us -> 594 us
  starting transfers between devices: 11.8 us -> 21.8 us
    pallas_call x1 -> x3, Pallas kernels: 157 us -> 377 us  [the longest x2 223 us: made_scatter(): pl.pallas_call(functools.partial(made_scatter_body, layers, parts), out_s...]
    pallas_call x5 -> x3, Pallas kernels: 316 us -> 97.4 us  [scatter(): pl.pallas_call(functools.partial(scatter_body, layers, by_rows), out_shap...]
    pallas_call x4 -> x3, Pallas kernels: 166 us -> 80.8 us  [gather(): pl.pallas_call(functools.partial(gather_body, layers, by_rows), out_shape...]
    all_to_all x1, starting transfers between devices: 5.02 us -> 15.1 us  [routed_and_shared(): lax.all_to_all(d_gates_all.reshape(experts, block), ('row', 'exp'), split...]
  transfers between devices with their start and end apart: 11 -> 11, of which waited for: 2 -> 1; matrix products, arithmetic and copies ran while one was open for 16% -> 22% of each run, Pallas kernels for 51% -> 49%
where the time goes in v3:
time: 905 us; the launch traced here: 896 us
  Pallas kernels  594 us (66%)
  matrix products  106 us (12%)
  other arithmetic  77.9 us (9%)
  local copies, waits for them, and re-layouts  42.8 us (5%)
  blocking collectives  23.3 us (3%)
  starting transfers between devices  21.8 us (2%)
  between operations  15.5 us (2%)
  waiting for transfers between devices  15.1 us (2%)
    pallas_call x2, Pallas kernels, made_scatter(): pl.pallas_call(functools.partial(made_scatter_body, layers, parts), out_s...  223 us
    pallas_call x1, Pallas kernels, expert_pass(): pl.pallas_call(functools.partial(expert_body, layers, units, experts), gr...  154 us
    pallas_call x3, Pallas kernels, scatter(): pl.pallas_call(functools.partial(scatter_body, layers, by_rows), out_shap...  97.4 us
    pallas_call x3, Pallas kernels, gather(): pl.pallas_call(functools.partial(gather_body, layers, by_rows), out_shape...  80.8 us
    dot_general x7, matrix products, dot_tn(): lax.dot_general(left, right, (((0,), (0,)), ((), ())), preferred_element_...  54 us
    pallas_call x2, Pallas kernels, small_sum(): pl.pallas_call(functools.partial(small_sum_body, layers), out_shape=jax.S...  38.7 us
  transfers between devices with their start and end apart: 11, of which 1 were waited for; matrix products, arithmetic and copies ran while one was open for 22% of the time, Pallas kernels for 49%

profile of v3, /device:TPU:0, one launch (start us, length us, event | category | flops | bytes accessed | tf_op | source)
XLA Modules:
  0.0 896.0 jit_solution(17096466371295685722)
XLA Ops:
  8.0 31.5 %shard_map.307 = bf16[1280,2048]{1,0:T(8,128)(2,1)} custom-call(bf16[320,1024]{1,0:T(8,128)(2,1)} %src.1), custom_call_target="tpu_custom_call" | custom-call | tf_op jit(solution)/shard_map/pallas_call | solution.py:267
  54.8 6.4 fusion.2
  64.2 14.4 %collective-permute-done.2 = bf16[3,1,88,1024]{3,2,1,0:T(8,128)(2,1)S(1)} collective-permute-done((bf16[3,1,88,1024]{3,2,1,0:T(8,128)(2,1)}, bf16[3,1,88,1024]{3,2,1,0:T(8,128)(2,1)S(1)}, u32[]{:S(2)}, u32[]{:S(2)}) %collective-permute-start.2) | collective-permute-done | bytes 540704 | tf_op jit(solution)/shard_map/ppermute | solution.py:1318
  89.8 7.0 fusion.99
  118.9 6.1 convolution_convert_fusion.src
  125.0 53.5 %shard_map.308 = f32[320,1024]{1,0:T(8,128)} custom-call(bf16[1280,2048]{1,0:T(8,128)(2,1)} %convolution_convert_fusion.src), custom_call_target="tpu_custom_call" | custom-call | tf_op jit(solution)/shard_map/pallas_call | solution.py:504
  180.0 13.7 %shard_map.309 = f32[16,512]{1,0:T(8,128)S(1)} custom-call(f32[16,256]{1,0:T(8,128)S(1)} %broadcast_select_fusion.src), custom_call_target="tpu_custom_call" | custom-call | tf_op jit(solution)/shard_map/pallas_call | solution.py:905
  199.1 4.9 psum.56
  211.2 154.3 %shard_map.310 = (bf16[5120,2048]{1,0:T(8,128)(2,1)}, bf16[2,2,4,192,2048]{4,3,2,1,0:T(8,128)(2,1)}, bf16[2,2,4,192,2048]{4,3,2,1,0:T(8,128)(2,1)}, bf16[2,2,4,1...) custom-call(bf16[320,1024]{1,0:T(8,128)(2,1)} %multiply_convert_fusi, ...), custom_call_target="tpu_custom_call" | custom-call | tf_op jit(solution)/shard_map/pallas_call | solution.py:1193
  368.8 15.1 %all-to-all-start = ((f32[16,1,320]{2,1,0:T(1,128)}), f32[16,1,320]{2,1,0:T(1,128)S(1)}, u32[]{:S(2)}, u32[]{:S(2)}) async-start(f32[16,1,320]{2,1,0:T(1,128)} %all_to_all.8), calls=%async_computation | async-start | bytes 49152 | tf_op jit(solution)/shard_map/all_to_all | solution.py:1408
  385.9 15.9 %convolution_bitcast_fusion.1 = f32[1,2048,704]{1,2,0:T(8,128)} fusion(bf16[2,2,4,192,2048]{4,3,2,1,0:T(8,128)(2,1)} %get-tuple-element.136, bf16[2,2,4,192,704]{4,3,2,1,0:T(8,128)(2,1)} %get-tuple-element.120.refs_1_), kind=kOutput, calls=%fused_computation.13 | convolution fusion | flops 8858370048 | bytes 22675456 | tf_op jit(solution)/shard_map/dot_general | solution.py:545
  401.8 11.4 %convolution_bitcast_fusion.2 = f32[1,2048,704]{1,2,0:T(8,128)} fusion(bf16[2,2,4,192,2048]{4,3,2,1,0:T(8,128)(2,1)S(1)} %bitcast.227, bf16[2,2,4,192,704]{4,3,2,1,0:T(8,128)(2,1)S(1)} %bitcast.196), kind=kOutput, calls=%fused_computation.14 | convolution fusion | flops 8858370048 | bytes 22675456 | tf_op jit(solution)/shard_map/dot_general | solution.py:545
  413.2 107.1 %shard_map.311 = f32[320,1024]{1,0:T(8,128)} custom-call(bf16[2,2,4,192,704]{4,3,2,1,0:T(8,128)(2,1)} %get-tuple-element.119.refs_0_, bf16[2,2,4,192,704]{4,3,2,1,0:T(8,128)(2,1)} %get-tuple-element.120.refs_1_, bf16[704,2048]{1,0:T(8,128)(2,1)} %bitcast.181, bf16[704,2048]{1,0:T(8,128)(2,1)} %bitcast.183, ...), custom_call_target="tpu_custom_call" | custom-call | tf_op jit(solution)/shard_map/pallas_call | solution.py:815
  525.3 15.2 %convolution_bitcast_fusion = f32[1,2048,704]{1,2,0:T(8,128)} fusion(bf16[2,2,4,192,2048]{4,3,2,1,0:T(8,128)(2,1)} %get-tuple-element.137, bf16[2,2,4,192,704]{4,3,2,1,0:T(8,128)(2,1)} %get-tuple-element.127.refs_0_), kind=kOutput, calls=%fused_computation.12 | convolution fusion | flops 8858370048 | bytes 22675456 | tf_op jit(solution)/shard_map/dot_general | solution.py:545
  540.6 8.0 psum.57
  555.2 5.1 psum.58
  562.7 25.4 %shard_map.312 = bf16[1280,2048]{1,0:T(8,128)(2,1)} custom-call(bf16[320,1024]{1,0:T(8,128)(2,1)} %fusion.91.src), custom_call_target="tpu_custom_call" | custom-call | tf_op jit(solution)/shard_map/pallas_call | solution.py:267
  619.3 14.2 %shard_map.313 = f32[160,576]{1,0:T(8,128)} custom-call(bf16[1280,576]{1,0:T(8,128)(2,1)} %pad_maximum_fusion.src), custom_call_target="tpu_custom_call" | custom-call | tf_op jit(solution)/shard_map/pallas_call | solution.py:504
  644.9 23.9 %shard_map.314 = bf16[1280,576]{1,0:T(8,128)(2,1)} custom-call(bf16[160,576]{1,0:T(8,128)(2,1)} %pad_maximum_fusion.15.src), custom_call_target="tpu_custom_call" | custom-call | tf_op jit(solution)/shard_map/pallas_call | solution.py:267
  688.1 29.7 %shard_map.315 = f32[320,1024]{1,0:T(8,128)} custom-call(bf16[1280,2048]{1,0:T(8,128)(2,1)} %convert_element_type.191.src), custom_call_target="tpu_custom_call" | custom-call | tf_op jit(solution)/shard_map/pallas_call | solution.py:504
  719.6 5.2 psum.59
  728.8 25.1 %shard_map.317 = f32[24,2048]{1,0:T(8,128)S(1)} custom-call(f32[24,1024]{1,0:T(8,128)S(1)} %select_maximum_fusion.src), custom_call_target="tpu_custom_call" | custom-call | tf_op jit(solution)/shard_map/pallas_call | solution.py:905
  753.8 115.6 %shard_map.316 = f32[320,1024]{1,0:T(8,128)} custom-call(bf16[2,2,4,192,704]{4,3,2,1,0:T(8,128)(2,1)} %get-tuple-element.127.refs_0_, bf16[704,2048]{1,0:T(8,128)(2,1)} %bitcast.185, bf16[2,2,4,2,160,96]{5,4,3,2,1,0:T(8,128)(2,1)} %fusion.11.spread_ref.refs_4_.refs_2_, bf16[2,2,4,320,128]{4,3,2,1,0:T(8,128)(2,1)} %get-tuple-element.130.refs_3_, ...), custom_call_target="tpu_custom_call" | custom-call | tf_op jit(solution)/shard_map/pallas_call | solution.py:815
  874.0 6.1 fusion.92
  (324 shorter events, 165.9 us)
Async XLA Ops:
  7.2 36.1 %copy-start = (bf16[1024,704]{0,1:T(8,128)(2,1)S(1)}, bf16[1024,704]{0,1:T(8,128)(2,1)}, u32[]{:S(2)}) copy-start(bf16[1024,704]{0,1:T(8,128)(2,1)} %param.40) | copy-start | bytes 4325380
  7.2 82.5 %all-gather.6.cloned.1.call-start = ((), (), s32[]{:S(2)}) async-start(), calls=%async_computation.1 | async-start | bytes 2654208 | tf_op jit(solution)/shard_map/all_gather | solution.py:1491
  7.9 203.2 %all-gather.8.cloned.1.call-start = ((), (), s32[]{:S(2)}) async-start(), calls=%async_computation.2 | async-start | bytes 21626880 | tf_op jit(solution)/shard_map/all_gather | solution.py:1364
  41.9 41.2 %copy-start.25 = (bf16[1024,384]{1,0:T(8,128)(2,1)}, bf16[1024,384]{1,0:T(8,128)(2,1)S(1)}, u32[]{:S(2)}) copy-start(bf16[1024,384]{1,0:T(8,128)(2,1)S(1)} %get-tuple-element.243) | copy-start | bytes 2359300
  41.9 41.2 %collective-permute-start = (bf16[1024,384]{1,0:T(8,128)(2,1)}, bf16[1024,384]{1,0:T(8,128)(2,1)}, u32[]{:S(2)}, u32[]{:S(2)}) collective-permute-start(bf16[1024,384]{1,0:T(8,128)(2,1)} %get-tuple-element.244), channel_id=1, source_target_pairs={{0,4},{4,0},{1,5},{5,1},{2,6},{6,2},{3,7},{7,3},{8,12},{12,8},{9,1... | collective-permute-start | bytes 2359304 | tf_op jit(solution)/shard_map/ppermute | solution.py:1318
  45.6 33.0 %collective-permute-start.2 = (bf16[3,1,88,1024]{3,2,1,0:T(8,128)(2,1)}, bf16[3,1,88,1024]{3,2,1,0:T(8,128)(2,1)S(1)}, u32[]{:S(2)}, u32[]{:S(2)}) collective-permute-start(bf16[3,1,88,1024]{3,2,1,0:T(8,128)(2,1)} %get-tuple-element.251), channel_id=1, source_target_pairs={{0,4},{4,0},{1,5},{5,1},{2,6},{6,2},{3,7},{7,3},{8,12},{12,8},{9,1... | collective-permute-start | bytes 1622024 | tf_op jit(solution)/shard_map/ppermute | solution.py:1318
  48.4 70.4 %collective-permute-start.1 = (bf16[256,1024]{1,0:T(8,128)(2,1)}, bf16[256,1024]{1,0:T(8,128)(2,1)}, u32[]{:S(2)}, u32[]{:S(2)}) collective-permute-start(bf16[256,1024]{1,0:T(8,128)(2,1)} %get-tuple-element.257), channel_id=1, source_target_pairs={{0,4},{4,0},{1,5},{5,1},{2,6},{6,2},{3,7},{7,3},{8,12},{12,8},{9,1... | collective-permute-start | bytes 1572872 | tf_op jit(solution)/shard_map/ppermute | solution.py:1318
  106.1 91.8 %copy-start.55 = (f32[1280]{0:T(1024)}, f32[1280]{0:T(1024)S(1)}, u32[]{:S(2)}) copy-start(f32[1280]{0:T(1024)S(1)} %add_rsqrt_fusion) | copy-start | bytes 15364
  125.0 53.5 %copy-start.13 = (bf16[320,1024]{1,0:T(8,128)(2,1)S(1)}, bf16[320,1024]{1,0:T(8,128)(2,1)}, u32[]{:S(2)}) copy-start(bf16[320,1024]{1,0:T(8,128)(2,1)} %src.1) | copy-start | bytes 1966084
  180.0 545.6 %copy-start.3 = (f32[320,1024]{1,0:T(8,128)}, f32[320,1024]{1,0:T(8,128)S(1)}, u32[]{:S(2)}) copy-start(f32[320,1024]{1,0:T(8,128)S(1)} %convert_add_fusion) | copy-start | bytes 3932164
  368.8 171.8 %all-to-all-start = ((f32[16,1,320]{2,1,0:T(1,128)}), f32[16,1,320]{2,1,0:T(1,128)S(1)}, u32[]{:S(2)}, u32[]{:S(2)}) async-start(f32[16,1,320]{2,1,0:T(1,128)} %all_to_all.8), calls=%async_computation | async-start | bytes 49152 | tf_op jit(solution)/shard_map/all_to_all | solution.py:1408
  383.8 294.5 %all-gather.10.cloned.1.call-start = ((), (), s32[]{:S(2)}) async-start(), calls=%async_computation.3 | async-start | bytes 5406720 | tf_op jit(solution)/shard_map/all_gather | solution.py:1605
  383.9 17.9 %slice-start.4 = ((s8[4718592]{0:T(1024)(128)(4,1)}), s8[4194304]{0:T(1024)(128)(4,1)S(1)}, s32[]{:S(2)}) async-start(s8[4718592]{0:T(1024)(128)(4,1)} %bitcast.195), calls=%async_computation.9 | async-start | bytes 8388608
  383.9 17.9 %slice-start.6 = ((s8[12582912]{0:T(1024)(128)(4,1)}), s8[4194304]{0:T(1024)(128)(4,1)S(1)}, s32[]{:S(2)}) async-start(s8[12582912]{0:T(1024)(128)(4,1)} %bitcast.226), calls=%async_computation.11 | async-start | bytes 8388608
  385.8 15.9 %slice-start.5 = ((s8[4718592]{0:T(1024)(128)(4,1)}), s8[524288]{0:T(1024)(128)(4,1)S(1)}, s32[]{:S(2)}) async-start(s8[4718592]{0:T(1024)(128)(4,1)} %bitcast.195), calls=%async_computation.10 | async-start | bytes 1048576
  524.4 27.6 %collective-permute-start.3 = (bf16[3,1,88,1024]{3,2,1,0:T(8,128)(2,1)}, bf16[3,1,88,1024]{3,2,1,0:T(8,128)(2,1)}, u32[]{:S(2)}, u32[]{:S(2)}) collective-permute-start(bf16[3,1,88,1024]{3,2,1,0:T(8,128)(2,1)} %get-tuple-element.246), channel_id=1, source_target_pairs={{0,4},{4,0},{1,5},{5,1},{2,6},{6,2},{3,7},{7,3},{8,12},{12,8},{9,1... | collective-permute-start | bytes 1622024 | tf_op jit(solution)/shard_map/ppermute | solution.py:1318
  525.2 23.5 %copy-start.18 = (bf16[320,1024]{1,0:T(8,128)(2,1)S(1)}, bf16[320,1024]{1,0:T(8,128)(2,1)}, u32[]{:S(2)}) copy-start(bf16[320,1024]{1,0:T(8,128)(2,1)} %multiply_convert_fusion.3.src) | copy-start | bytes 1966084
  554.8 325.2 %all-reduce.11.cloned.1.call-start = ((), (), s32[]{:S(2)}) async-start(), calls=%async_computation.4 | async-start | bytes 6881280 | tf_op jit(solution)/shard_map/psum | solution.py:1723
  562.7 25.4 %copy-start.46 = (bf16[1280,2,128]{0,2,1:T(8,128)(2,1)S(1)}, bf16[1280,2,128]{0,2,1:T(8,128)(2,1)}, u32[]{:S(2)}) copy-start(bf16[1280,2,128]{0,2,1:T(8,128)(2,1)} %copy-done.45) | copy-start | bytes 1966084
  596.5 77.4 %collective-permute-start.5 = (bf16[256,1024]{1,0:T(8,128)(2,1)}, bf16[256,1024]{1,0:T(8,128)(2,1)}, u32[]{:S(2)}, u32[]{:S(2)}) collective-permute-start(bf16[256,1024]{1,0:T(8,128)(2,1)} %get-tuple-element.253), channel_id=1, source_target_pairs={{0,4},{4,0},{1,5},{5,1},{2,6},{6,2},{3,7},{7,3},{8,12},{12,8},{9,1... | collective-permute-start | bytes 1572872 | tf_op jit(solution)/shard_map/ppermute | solution.py:1318
  640.9 35.6 %collective-permute-start.4 = (bf16[1024,384]{0,1:T(8,128)(2,1)S(1)}, bf16[1024,384]{0,1:T(8,128)(2,1)S(1)}, u32[]{:S(2)}, u32[]{:S(2)}) collective-permute-start(bf16[1024,384]{0,1:T(8,128)(2,1)S(1)} %get-tuple-element.242), channel_id=1, source_target_pairs={{0,4},{4,0},{1,5},{5,1},{2,6},{6,2},{3,7},{7,3},{8,12},{12,8},{9,1... | collective-permute-start | bytes 2359304 | tf_op jit(solution)/shard_map/ppermute | solution.py:1318
  688.1 29.8 %copy-start.14 = (bf16[320,1024]{1,0:T(8,128)(2,1)S(1)}, bf16[320,1024]{1,0:T(8,128)(2,1)}, u32[]{:S(2)}) copy-start(bf16[320,1024]{1,0:T(8,128)(2,1)} %src.1) | copy-start | bytes 1966084
  688.1 29.8 %copy-start.57 = (f32[1024]{0:T(1024)S(1)}, f32[1024]{0:T(1024)}, u32[]{:S(2)}) copy-start(f32[1024]{0:T(1024)} %dynamic_slice.105) | copy-start | bytes 12292
  688.1 29.8 %copy-start.58 = (f32[320]{0:T(512)S(1)}, f32[320]{0:T(512)}, u32[]{:S(2)}) copy-start(f32[320]{0:T(512)} %dynamic_slice.99) | copy-start | bytes 3844
  (65 other events, 322.0 us)
Sparse Core Ops, SparseCore 0:
  9.9 35.5 all-gather.5
  48.3 160.1 all-gather.7
  554.9 82.4 all-gather.9
  678.5 154.7 all-reduce.10

commit v4 on v3

--- a/solution.py
+++ b/solution.py
@@ -212,74 +212,102 @@
                     self.along(False, layer).wait_send()
 
 
-def gather_body(layers, by_rows, src, out, held, store_sem, *sems):
+def gather_body(layers, by_rows, *refs):
+    count = len(by_rows)
     me = Place(layers)
-    work = Gather(me, layers, by_rows, src.shape, held, sems)
-
-    def store(kind, layer, partner):
-        if partner:
-            pair = (work.partner_piece(held, kind, layer), work.partner_piece(out, kind, layer))
-        else:
-            pair = (work.piece(kind, layer), work.area(out, *work.owners[kind], layer))
-        return pltpu.make_async_copy(*pair, store_sem.at[1 if partner else 0, kind, layer])
-
-    own = pltpu.make_async_copy(src, work.piece(0, me.layer), store_sem.at[0, 0, me.layer])
-    own.start()
+    srcs, outs, refs = refs[:count], refs[count : 2 * count], refs[2 * count :]
+    works, stores = [], []
+    for i in range(count):
+        held, store_sem, *sems = refs[9 * i : 9 * i + 9]
+        works.append(Gather(me, layers, by_rows[i], srcs[i].shape, held, sems))
+
+        def store(kind, layer, partner, work=works[i], out=outs[i], store_sem=store_sem):
+            if partner:
+                pair = (
+                    work.partner_piece(work.held, kind, layer),
+                    work.partner_piece(out, kind, layer),
+                )
+            else:
+                pair = (work.piece(kind, layer), work.area(out, *work.owners[kind], layer))
+            return pltpu.make_async_copy(*pair, store_sem.at[1 if partner else 0, kind, layer])
+
+        stores.append(store)
+    own = [
+        pltpu.make_async_copy(src, work.piece(0, me.layer), refs[9 * i + 1].at[0, 0, me.layer])
+        for i, (src, work) in enumerate(zip(srcs, works))
+    ]
+    for copy in own:
+        copy.start()
     me.greet()
-    own.wait()
-    work.begin()
-    store(0, me.layer, False).start()
+    for copy, work, store in zip(own, works, stores):
+        copy.wait()
+        work.begin()
+        store(0, me.layer, False).start()
 
     def arrived(layer, upward):
-        work.arrived(layer, upward)
-        store(0, layer, False).start()
+        for work, store in zip(works, stores):
+            work.arrived(layer, upward)
+            store(0, layer, False).start()
 
     def second(layer, upward):
-        work.second(layer)
-        for kind in (1, 2):
-            store(kind, layer, False).start()
+        for work, store in zip(works, stores):
+            work.second(layer)
+            for kind in (1, 2):
+                store(kind, layer, False).start()
 
     def third(layer, upward):
-        work.third(layer)
-        store(3, layer, False).start()
-        for kind in range(4):
-            work.from_core(kind, layer).wait_recv()
-            store(kind, layer, True).start()
+        for work, store in zip(works, stores):
+            work.third(layer)
+            store(3, layer, False).start()
+            for kind in range(4):
+                work.from_core(kind, layer).wait_recv()
+                store(kind, layer, True).start()
 
     for step in range(1, layers + 2):
         if step < layers:
-            work.at_distance(step, arrived)
+            works[0].at_distance(step, arrived)
         if step - 1 < layers:
-            work.at_distance(step - 1, second)
+            works[0].at_distance(step - 1, second)
         if 0 <= step - 2 < layers:
-            work.at_distance(step - 2, third)
-    for layer in range(layers):
-        for kind in range(4):
-            store(kind, layer, False).wait()
-            store(kind, layer, True).wait()
-    work.finish()
+            works[0].at_distance(step - 2, third)
+    for work, store in zip(works, stores):
+        for layer in range(layers):
+            for kind in range(4):
+                store(kind, layer, False).wait()
+                store(kind, layer, True).wait()
+        work.finish()
 
 
 def gather(value, layers, collective_id, by_rows=False):
-    rows, width = value.shape
+    return gather_several((value,), layers, collective_id, (by_rows,))[0]
+
+
+def gather_several(values, layers, collective_id, by_rows):
     dma = pltpu.SemaphoreType.DMA
-    whole = (8 * rows, width) if by_rows else (4 * layers * rows, 2 * width)
+    shapes, scratch = [], []
+    for value, rows_only in zip(values, by_rows):
+        rows, width = value.shape
+        shapes.append((8 * rows, width) if rows_only else (4 * layers * rows, 2 * width))
+        scratch += [
+            pltpu.VMEM(shapes[-1], value.dtype),
+            dma((2, 4, layers)),
+            *Gather.semaphores(layers),
+        ]
+    in_hbm = pl.BlockSpec(memory_space=pl.ANY)
     return pl.pallas_call(
         functools.partial(gather_body, layers, by_rows),
-        out_shape=jax.ShapeDtypeStruct(whole, value.dtype),
-        in_specs=[pl.BlockSpec(memory_space=pl.ANY)],
-        out_specs=pl.BlockSpec(memory_space=pl.ANY),
-        scratch_shapes=[
-            pltpu.VMEM(whole, value.dtype),
-            dma((2, 4, layers)),
-            *Gather.semaphores(layers),
+        out_shape=[
+            jax.ShapeDtypeStruct(shape, value.dtype) for shape, value in zip(shapes, values)
         ],
+        in_specs=[in_hbm] * len(values),
+        out_specs=[in_hbm] * len(values),
+        scratch_shapes=scratch,
         compiler_params=pltpu.CompilerParams(
             collective_id=collective_id,
             has_side_effects=True,
             vmem_limit_bytes=56 * 1024 * 1024,
         ),
-    )(value)
+    )(*values)
 
 
 def scatter_body(
@@ -547,10 +575,14 @@
     )
 
 
-def made_scatter_body(layers, parts, *refs):
+def made_scatter_body(layers, parts, jobs, *refs):
     slots_hbm, refs = refs[:parts], refs[parts:]
     weights_hbm, refs = refs[:parts], refs[parts:]
-    spread_hbm, side_hbm, side_w_hbm, out, refs = *refs[:4], refs[4:]
+    spread_hbm, side_hbm, side_w_hbm, refs = *refs[:3], refs[3:]
+    job_a, job_b, refs = refs[:jobs], refs[jobs : 2 * jobs], refs[2 * jobs :]
+    out, job_out, refs = refs[0], refs[1 : 1 + jobs], refs[1 + jobs :]
+    if jobs:
+        job_acc, a_in, b_in, job_sem, flush_sem, refs = *refs[:5], refs[5:]
     slots_in, refs = refs[:parts], refs[parts:]
     weights, refs = refs[:parts], refs[parts:]
     spread_in, side_in, side_w, slot_rows, refs = *refs[:4], refs[4:]
@@ -677,8 +709,66 @@
 
         lax.fori_loop(0, size // lanes, step, 0)
 
+    turns = layers + 2
+    chunk = a_in.shape[1] if jobs else 0
+    chunks = job_a[0].shape[0] // chunk if jobs else 0
+
+    def job_loads(unit, job):
+        slot = lax.rem(unit, 2)
+        here = pl.ds(pl.multiple_of(lax.rem(unit, turns) * chunk, 16), chunk)
+        return [
+            pltpu.make_async_copy(src.at[here], dst.at[slot], job_sem.at[slot, i])
+            for i, (src, dst) in enumerate(((job_a[job], a_in), (job_b[job], b_in)))
+        ]
+
+    def start_job_loads(unit):
+        for job in range(jobs):
+
+            @pl.when((unit // turns == job) & (lax.rem(unit, turns) < chunks))
+            def _():
+                for copy in job_loads(unit, job):
+                    copy.start()
+
+    def flush(job):
+        return pltpu.make_async_copy(job_acc, job_out[job], flush_sem)
+
+    def job_turn(unit):
+        if not jobs:
+            return
+        at = lax.rem(unit, turns)
+        slot = lax.rem(unit, 2)
+
+        @pl.when(unit + 1 < jobs * turns)
+        def _():
+            start_job_loads(unit + 1)
+
+        @pl.when((at == 0) & (unit > 0))
+        def _():
+            flush(0).wait()
+
+        @pl.when(at == 0)
+        def _():
+            job_acc[...] = jnp.zeros_like(job_acc)
+
+        @pl.when(at < chunks)
+        def _():
+            for copy in job_loads(unit, 0):
+                copy.wait()
+            left = a_in[slot].T
+            for first in range(0, 2 * width, width // 2):
+                here = pl.ds(first, width // 2)
+                job_acc[:, here] += dot_nn(left, b_in[slot, :, here])
+
+        for job in range(jobs):
+
+            @pl.when((at == chunks - 1) & (unit // turns == job))
+            def _():
+                flush(job).start()
+
     for copy in (*weight_loads(), *loads(0)):
         copy.start()
+    if jobs:
+        start_job_loads(0)
     me.greet()
     for copy in weight_loads():
         copy.wait()
@@ -752,14 +842,19 @@
             produce(step)
             stage_a(step)
 
+        job_turn(3 * step)
+
         @pl.when((step >= 1) & (step <= layers))
         def _():
             stage_b(step - 1)
 
+        job_turn(3 * step + 1)
+
         @pl.when(step >= 2)
         def _():
             stage_c(step - 2)
 
+        job_turn(3 * step + 2)
         return carry
 
     lax.fori_loop(0, layers + 2, stages, 0)
@@ -785,6 +880,8 @@
     def _():
         add(acc.at[last, 0], [line_in.at[0, me.layer]], into=out)
 
+    if jobs:
+        flush(0).wait()
     for step in range(layers):
         if step >= layers - 2:
             for kind in range(4):
@@ -803,21 +900,34 @@
                 line(step, False).wait_send()
 
 
-def made_scatter(slots_in, weights, spread, side, side_w, layers, collective_id):
+def made_scatter(slots_in, weights, spread, side, side_w, job_a, job_b, layers, collective_id):
     block, width = side.shape[3], side_w.shape[1] // 2
-    bf16 = jnp.bfloat16
-    parts = len(weights)
+    bf16, f32 = jnp.bfloat16, jnp.float32
+    parts, jobs = len(weights), len(job_a)
     part = first_part(block)
     dma = pltpu.SemaphoreType.DMA
     buffer = lambda *lead: pltpu.VMEM((*lead, block, width), bf16)
     ahead = lambda value: pltpu.VMEM((2, 2, *value.shape[3:]), bf16)
     in_hbm = pl.BlockSpec(memory_space=pl.ANY)
+    job_shapes, job_scratch = [], []
+    if jobs:
+        rows, tall, wide = *job_a[0].shape, job_b[0].shape[1]
+        chunks = max(n for n in range(1, layers + 3) if rows % (16 * n) == 0)
+        job_shapes = [jax.ShapeDtypeStruct((tall, wide), f32)] * jobs
+        job_scratch = [
+            pltpu.VMEM((tall, wide), f32),
+            pltpu.VMEM((2, rows // chunks, tall), bf16),
+            pltpu.VMEM((2, rows // chunks, wide), bf16),
+            dma((2, 2)),
+            dma,
+        ]
     return pl.pallas_call(
-        functools.partial(made_scatter_body, layers, parts),
-        out_shape=jax.ShapeDtypeStruct((block, width), jnp.float32),
-        in_specs=[in_hbm] * (2 * parts + 3),
-        out_specs=pl.BlockSpec(memory_space=pltpu.VMEM),
+        functools.partial(made_scatter_body, layers, parts, jobs),
+        out_shape=[jax.ShapeDtypeStruct((block, width), f32), *job_shapes],
+        in_specs=[in_hbm] * (2 * parts + 3 + 2 * jobs),
+        out_specs=[pl.BlockSpec(memory_space=pltpu.VMEM), *[in_hbm] * jobs],
         scratch_shapes=[
+            *job_scratch,
             *(ahead(value) for value in slots_in),
             *(pltpu.VMEM(value.shape, bf16) for value in weights),
             ahead(spread),
@@ -847,7 +957,7 @@
             has_side_effects=True,
             vmem_limit_bytes=62 * 1024 * 1024,
         ),
-    )(*slots_in, *weights, spread, side, side_w)
+    )(*slots_in, *weights, spread, side, side_w, *job_a, *job_b)
 
 
 def small_sum_body(layers, src, out, core_in, mid, x_in, near, line_in, total, send, recv, line_send, line_recv):
@@ -1019,15 +1129,16 @@
 
         for turn in range(layers):
             at = nearest_first(layers, turn, me.layer)
+
+            @pl.when(which == (max(1, 2 * turn) if turn != 1 else 3))
+            def _():
+                work.third(at)
+
             if turn > 0:
 
-                @pl.when(which == 2 * turn - 1)
+                @pl.when(which == (2 * turn - 1 if turn != 1 else 2))
                 def _():
                     work.second(at)
-
-            @pl.when(which == max(1, 2 * turn))
-            def _():
-                work.third(at)
 
         layer = nearest_first(layers, which // 2, me.layer)
 
@@ -1055,8 +1166,6 @@
         work.begin()
         for copy in weight_loads:
             copy.wait()
-        work.second(me.layer)
-        prepare(step)
 
     rows = both_rows.at[lax.rem(step, 2)]
 
@@ -1078,6 +1187,12 @@
     d_side_hidden = sum(
         dot_nt(side_grads[c], side_down[:, c * half : (c + 1) * half]) for c in range(2)
     )
+
+    @pl.when(step == 0)
+    def _():
+        work.second(me.layer)
+        prepare(step)
+
     for core in range(2):
         load(step, core).wait()
 
@@ -1324,9 +1439,13 @@
     )
 
 
+def halves(value, split):
+    col = lax.axis_index("col")
+    return own_slice(value, col, split), own_slice(value, 1 - col, split)
+
+
 def trade(value, split, join):
-    col = lax.axis_index("col")
-    return col_pair(own_slice(value, col, split), own_slice(value, 1 - col, split), join)
+    return col_pair(*halves(value, split), join)
 
 
 def routed_and_shared(
@@ -1392,14 +1511,19 @@
     )
     spread = spread.reshape(2, 2, layers, -1, few, slots)
     gate_weight, up_weight, down_weight = expert_weights
-    d_normed = made_scatter(
-        (d_gate, d_up), (gate_weight, up_weight), spread, d_side, side_w, layers, 4
-    )
-    out_parts = ((hidden,), (down_weight,), spread, side_hidden, side_down)
-    flat = lambda value: value.reshape(-1, value.shape[-1])
-    grad_gate = dot_tn(flat(d_gate), flat(slot_rows))
-    grad_up = dot_tn(flat(d_up), flat(slot_rows))
-    grad_down = dot_tn(flat(hidden), flat(slot_grads))
+    (d_normed,) = made_scatter(
+        (d_gate, d_up), (gate_weight, up_weight), spread, d_side, side_w, (), (), layers, 4
+    )
+    flat = lambda *values: tuple(value.reshape(-1, value.shape[-1]) for value in values)
+    out_parts = (
+        (hidden,),
+        (down_weight,),
+        spread,
+        side_hidden,
+        side_down,
+        flat(d_gate, d_up, hidden),
+        flat(slot_rows, slot_rows, slot_grads),
+    )
     grad_shared = jnp.stack(
         [grad_side[:units], grad_side[lanes : lanes + units], grad_side_down[:units]]
     )
@@ -1444,7 +1568,7 @@
         precision=lax.Precision.HIGHEST,
         preferred_element_type=jnp.float32,
     )
-    return (d_normed, out_parts, (grad_gate, grad_up, grad_down, grad_shared, grad_router))
+    return (d_normed, out_parts, (grad_shared, grad_router))
 
 
 def per_device(
@@ -1487,27 +1611,17 @@
     query_rows = group // 2
     bf16 = jnp.bfloat16
 
-    w_query_own = trade(w_query, 1, 0)
-    w_latent_all = lax.all_gather(w_latent[0].T, ("col", "row"), axis=1, tiled=True)
+    query_halves, layer_input = lax.optimization_barrier((halves(w_query, 1), layer_input))
+    w_query_own = col_pair(*query_halves, 0)
     seq_ids, places = sequence_layout(lengths[0], group)
     cosine, sine = rotary_tables(places)
 
-    group_input = gather(layer_input, 1, 1)
-    group_input, w_out, shared_gate, shared_up, shared_down, cotangent = lax.optimization_barrier(
-        (group_input, w_out, shared_gate, shared_up, shared_down, cotangent)
-    )
+    group_input, w_latent_all = gather_several((layer_input, w_latent[0].T), 1, 10, (False, True))
+    latent_width, slab = w_latent.shape[2], w_latent.shape[1]
+    w_latent_all = w_latent_all.reshape(rows_n, cols_n, latent_width, slab)
+    w_latent_all = w_latent_all.transpose(2, 1, 0, 3).reshape(latent_width, width)
+    group_input, w_out, cotangent = lax.optimization_barrier((group_input, w_out, cotangent))
     w_out_own = trade(w_out, 0, 1)
-    units = shared_gate.shape[1] // (cols_n * exps_n)
-    shared_parts = jnp.stack(
-        [
-            lax.dynamic_index_in_dim(
-                part.reshape(cols_n, exps_n, units, half_width), exp_id, 1, keepdims=False
-            )
-            for part in (shared_gate.T, shared_up.T, shared_down)
-        ]
-    )
-    shared_own = trade(shared_parts, 1, 3)[:, 0]
-
     group_input = group_input.astype(jnp.float32)
     factor_group = lax.rsqrt(jnp.mean(group_input * group_input, axis=1) + epsilon)
     normed_group = (group_input * factor_group[:, None] * norm1_gain).astype(bf16)
@@ -1519,6 +1633,20 @@
         ],
         axis=2,
     ).astype(bf16)
+    queries, shared_gate, shared_up, shared_down = lax.optimization_barrier(
+        (queries, shared_gate, shared_up, shared_down)
+    )
+    units = shared_gate.shape[1] // (cols_n * exps_n)
+    shared_parts = jnp.stack(
+        [
+            lax.dynamic_index_in_dim(
+                part.reshape(cols_n, exps_n, units, half_width), exp_id, 1, keepdims=False
+            )
+            for part in (shared_gate.T, shared_up.T, shared_down)
+        ]
+    )
+    shared_own = trade(shared_parts, 1, 3)[:, 0]
+
     latent = dot_nt(normed_group, w_latent_all)
     compressed_raw = latent[:, :KV_RANK]
     kv_factor = lax.rsqrt(jnp.mean(compressed_raw * compressed_raw, axis=1) + epsilon)
@@ -1586,7 +1714,10 @@
 
         def one_piece(total, items):
             d_rows, out_parts, grads = feed(*items)
-            return (jax.tree.map(jnp.add, total, grads), (d_rows, made_scatter(*out_parts, exps_n, 9)))
+            *out_parts, job_a, job_b = out_parts
+            (branch_rows,) = made_scatter(*out_parts, (), (), exps_n, 9)
+            grads = (*grads, tuple(dot_tn(a, b) for a, b in zip(job_a, job_b)))
+            return (jax.tree.map(jnp.add, total, grads), (d_rows, branch_rows))
 
         split = lambda value: value.reshape(pieces, piece_rows, half_width)
         word_pieces = words_all.reshape(experts, pieces, piece_rows, words_n)
@@ -1595,11 +1726,15 @@
             split(cotangent),
             word_pieces.transpose(1, 0, 2, 3).reshape(pieces, -1, words_n),
         )
-        shapes = jax.eval_shape(lambda: feed(*(item[0] for item in items))[2])
-        start = jax.tree.map(lambda leaf: jnp.zeros(leaf.shape, leaf.dtype), shapes)
+        start = (
+            jnp.zeros((3, units, width), jnp.float32),
+            jnp.zeros((half_width, experts), jnp.float32),
+            (jnp.zeros(expert_gate.shape[:0:-1], jnp.float32),) * 3,
+        )
         weight_grads, (d_normed, branch) = lax.scan(one_piece, start, items)
         d_normed, branch = (v.reshape(block, half_width) for v in (d_normed, branch))
-    grad_gate, grad_up, grad_down, grad_shared, grad_router = weight_grads
+    grad_shared, grad_router = weight_grads[:2]
+    expert_grads = weight_grads[2] if pieces > 1 else None
     grad_shared = trade(grad_shared.astype(bf16)[:, None], 3, 1)
     d_normed, grad_shared = lax.optimization_barrier((d_normed, grad_shared))
     grad_shared = lax.all_gather(grad_shared, "exp", axis=2, tiled=False)
@@ -1702,7 +1837,7 @@
     input_grad = d_hidden_state + d_norm_one
     if pieces == 1:
         out_parts, input_grad = lax.optimization_barrier((out_parts, input_grad))
-        branch = made_scatter(*out_parts, exps_n, 9)
+        branch, *expert_grads = made_scatter(*out_parts, exps_n, 9)
     output = (hidden_state + branch).astype(bf16)
 
     small = jnp.concatenate(
@@ -1737,9 +1872,7 @@
         grad_shared[1].T,
         grad_shared[2],
         small[3 : 3 + experts].T,
-        grad_gate.T[None],
-        grad_up.T[None],
-        grad_down.T[None],
+        *(grad.T[None] for grad in expert_grads),
     )
 
 

time: 905 us -> 869 us (0.960)
  matrix products: 106 us -> 62.9 us
  local copies, waits for them, and re-layouts: 42.8 us -> 64.8 us
  Pallas kernels: 594 us -> 606 us
  starting transfers between devices: 21.8 us -> 10.2 us
  waiting for transfers between devices: 15.1 us -> 5.77 us
    dot_general x7 -> x4, matrix products: 54 us -> 11.5 us  [dot_tn(): lax.dot_general(left, right, (((0,), (0,)), ((), ())), preferred_element_...]
    pallas_call x5, Pallas kernels: 303 us -> 320 us  [the longest x2 231 us: made_scatter(): pl.pallas_call(functools.partial(made_scatter_body, layers, parts, jobs),...]
    ppermute x6, waiting for transfers between devices: 14.4 us -> 0.02 us  [col_pair(): received = lax.ppermute(sent, 'col', SWAP)]
    all_to_all x1, starting transfers between devices: 15.1 us -> 4.08 us  [routed_and_shared(): lax.all_to_all(d_gates_all.reshape(experts, block), ('row', 'exp'), split...]
    reshape x0 -> x2, local copies, waits for them, and re-layouts: none -> 10.3 us  [the longest x1 5.45 us: per_device(): w_latent_all.transpose(2, 1, 0, 3).reshape(latent_width, width)]
    unnamed x158 -> x163, local copies, waits for them, and re-layouts: 14.8 us -> 25 us
  transfers between devices with their start and end apart: 11 -> 10, of which waited for: 1 -> 1; matrix products, arithmetic and copies ran while one was open for 22% -> 19% of each run, Pallas kernels for 49% -> 48%
where the time goes in v4:
time: 869 us; the launch traced here: 860 us
  Pallas kernels  606 us (70%)
  other arithmetic  71.4 us (8%)
  local copies, waits for them, and re-layouts  64.8 us (7%)
  matrix products  62.9 us (7%)
  blocking collectives  23 us (3%)
  between operations  15.3 us (2%)
  starting transfers between devices  10.2 us (1%)
    pallas_call x2, Pallas kernels, made_scatter(): pl.pallas_call(functools.partial(made_scatter_body, layers, parts, jobs),...  231 us
    pallas_call x1, Pallas kernels, expert_pass(): pl.pallas_call(functools.partial(expert_body, layers, units, experts), gr...  159 us
    pallas_call x3, Pallas kernels, scatter(): pl.pallas_call(functools.partial(scatter_body, layers, by_rows), out_shap...  91.7 us
    pallas_call x3, Pallas kernels, gather_several(): pl.pallas_call(functools.partial(gather_body, layers, by_rows), out_shape...  88.1 us
    pallas_call x2, Pallas kernels, small_sum(): pl.pallas_call(functools.partial(small_sum_body, layers), out_shape=jax.S...  36.2 us
    unnamed x163, local copies, waits for them, and re-layouts  25 us
  transfers between devices with their start and end apart: 10, of which 1 were waited for; matrix products, arithmetic and copies ran while one was open for 19% of the time, Pallas kernels for 48%

profile of v4, /device:TPU:0, one launch (start us, length us, event | category | flops | bytes accessed | tf_op | source)
XLA Modules:
  0.0 859.7 jit_solution(9757034661417376358)
XLA Ops:
  10.1 38.3 %shard_map.307 = (bf16[1280,2048]{1,0:T(8,128)(2,1)}, bf16[4608,256]{1,0:T(8,128)(2,1)}) custom-call(bf16[320,1024]{1,0:T(8,128)(2,1)} %refs_0_, bf16[576,256]{1,0:T(8,128)(2,1)} %bitcast.211), custom_call_target="tpu_custom_call" | custom-call | tf_op jit(solution)/shard_map/pallas_call | solution.py:297
  52.5 4.9 copy.158
  57.4 5.5 reshape.634
  90.9 5.7 fusion.57
  109.4 5.4 convolution_convert_fusion.src
  114.8 47.6 %shard_map.308 = f32[320,1024]{1,0:T(8,128)} custom-call(bf16[1280,2048]{1,0:T(8,128)(2,1)} %convolution_convert_fusion.src), custom_call_target="tpu_custom_call" | custom-call | tf_op jit(solution)/shard_map/pallas_call | solution.py:532
  164.0 14.9 %shard_map.309 = f32[16,512]{1,0:T(8,128)S(1)} custom-call(f32[16,256]{1,0:T(8,128)S(1)} %broadcast_select_fusion.src), custom_call_target="tpu_custom_call" | custom-call | tf_op jit(solution)/shard_map/pallas_call | solution.py:1015
  179.3 4.9 psum.56
  199.1 5.7 all-gather.5.cloned.1.call-done
  204.8 158.8 %shard_map.310 = (bf16[5120,2048]{1,0:T(8,128)(2,1)}, bf16[2,2,4,192,2048]{4,3,2,1,0:T(8,128)(2,1)}, bf16[2,2,4,192,2048]{4,3,2,1,0:T(8,128)(2,1)}, bf16[2,2,4,1...) custom-call(bf16[320,1024]{1,0:T(8,128)(2,1)} %multiply_convert_fusi, ...), custom_call_target="tpu_custom_call" | custom-call | tf_op jit(solution)/shard_map/pallas_call | solution.py:1308
  376.9 105.0 %shard_map.311 = f32[320,1024]{1,0:T(8,128)} custom-call(bf16[2,2,4,192,704]{4,3,2,1,0:T(8,128)(2,1)} %get-tuple-element.141.refs_0_, bf16[2,2,4,192,704]{4,3,2,1,0:T(8,128)(2,1)} %get-tuple-element.142.refs_1_, bf16[704,2048]{1,0:T(8,128)(2,1)} %bitcast.181, bf16[704,2048]{1,0:T(8,128)(2,1)} %bitcast.183, ...), custom_call_target="tpu_custom_call" | custom-call | tf_op jit(solution)/shard_map/pallas_call | solution.py:924
  481.9 7.6 psum.57
  498.2 5.1 psum.58
  505.6 25.9 %shard_map.312 = bf16[1280,2048]{1,0:T(8,128)(2,1)} custom-call(bf16[320,1024]{1,0:T(8,128)(2,1)} %fusion.91.refs_0_), custom_call_target="tpu_custom_call" | custom-call | tf_op jit(solution)/shard_map/pallas_call | solution.py:297
  562.2 14.4 %shard_map.313 = f32[160,576]{1,0:T(8,128)} custom-call(bf16[1280,576]{1,0:T(8,128)(2,1)} %pad_maximum_fusion.src), custom_call_target="tpu_custom_call" | custom-call | tf_op jit(solution)/shard_map/pallas_call | solution.py:532
  588.1 23.9 %shard_map.314 = bf16[1280,576]{1,0:T(8,128)(2,1)} custom-call(bf16[160,576]{1,0:T(8,128)(2,1)} %pad_maximum_fusion.15.refs_0_), custom_call_target="tpu_custom_call" | custom-call | tf_op jit(solution)/shard_map/pallas_call | solution.py:297
  622.7 4.7 fusion.56
  631.3 29.8 %shard_map.315 = f32[320,1024]{1,0:T(8,128)} custom-call(bf16[1280,2048]{1,0:T(8,128)(2,1)} %convert_element_type.191.src), custom_call_target="tpu_custom_call" | custom-call | tf_op jit(solution)/shard_map/pallas_call | solution.py:532
  662.9 5.3 psum.59
  672.2 126.5 %shard_map.316 = (f32[320,1024]{1,0:T(8,128)}, f32[704,2048]{1,0:T(8,128)}, f32[704,2048]{1,0:T(8,128)}, f32[704,2048]{1,0:T(8,128)}) custom-call(bf16[2,2,4,192,704]{4,3,2,1,0:T(8,128)(2,1)} %get-tuple-element.151.refs_0_, bf16[704,2048]{1,0:T(8,128)(2,1)} %bitcast.185, bf16[2,2,4,2,160,96]{5,4,3,2,1,0:T(8,128)(2,1)} %fusion.11.spread_ref.refs_4_.refs_2_, ...), custom_call_target="tpu_custom_call" | custom-call | tf_op jit(solution)/shard_map/pallas_call | solution.py:924
  798.7 21.3 %shard_map.317 = f32[24,2048]{1,0:T(8,128)S(1)} custom-call(f32[24,1024]{1,0:T(8,128)S(1)} %select_maximum_fusion.src), custom_call_target="tpu_custom_call" | custom-call | tf_op jit(solution)/shard_map/pallas_call | solution.py:1015
  824.6 6.1 fusion.92
  838.4 6.0 copy.169
  844.4 6.0 copy.170
  (324 shorter events, 165.2 us)
Async XLA Ops:
  7.2 89.7 %copy-start = (bf16[1024,704]{0,1:T(8,128)(2,1)S(1)}, bf16[1024,704]{0,1:T(8,128)(2,1)}, u32[]{:S(2)}) copy-start(bf16[1024,704]{0,1:T(8,128)(2,1)} %param.40) | copy-start | bytes 4325380
  7.2 197.6 %all-gather.5.cloned.1.call-start = ((), (), s32[]{:S(2)}) async-start(), calls=%async_computation.1 | async-start | bytes 21626880 | tf_op jit(solution)/shard_map/all_gather | solution.py:1483
  7.3 42.3 %copy-start.46 = (bf16[512,1024]{1,0:T(8,128)(2,1)S(1)}, bf16[512,1024]{1,0:T(8,128)(2,1)}, u32[]{:S(2)}) copy-start(bf16[512,1024]{1,0:T(8,128)(2,1)} %param.38) | copy-start | bytes 3145732
  10.1 41.5 %copy-start.72 = (s32[1,3]{1,0:T(1,128)S(1)}, s32[1,3]{1,0:T(1,128)}, u32[]{:S(2)}) copy-start(s32[1,3]{1,0:T(1,128)} %param.31) | copy-start | bytes 40
  10.1 41.7 %copy-start.70 = (s32[1,160,6]{1,0,2:T(1,128)S(1)}, s32[1,160,6]{1,0,2:T(1,128)}, u32[]{:S(2)}) copy-start(s32[1,160,6]{1,0,2:T(1,128)} %param.32) | copy-start | bytes 11524
  10.1 41.8 %copy-start.71 = (f32[2048]{0:T(1024)S(1)}, f32[2048]{0:T(1024)}, u32[]{:S(2)}) copy-start(f32[2048]{0:T(1024)} %param.39) | copy-start | bytes 24580
  10.1 41.8 %copy-start.65 = (f32[2048]{0:T(1024)S(1)}, f32[2048]{0:T(1024)}, u32[]{:S(2)}) copy-start(f32[2048]{0:T(1024)} %param.33) | copy-start | bytes 24580
  48.5 42.4 %collective-permute-start = (bf16[1024,384]{1,0:T(8,128)(2,1)}, bf16[1024,384]{1,0:T(8,128)(2,1)}, u32[]{:S(2)}, u32[]{:S(2)}) collective-permute-start(bf16[1024,384]{1,0:T(8,128)(2,1)} %get-tuple-element.130), channel_id=1, source_target_pairs={{0,4},{4,0},{1,5},{5,1},{2,6},{6,2},{3,7},{7,3},{8,12},{12,8},{9,1... | collective-permute-start | bytes 2359304 | tf_op jit(solution)/shard_map/ppermute | solution.py:1433
  50.6 58.8 %collective-permute-start.1 = (bf16[256,1024]{1,0:T(8,128)(2,1)}, bf16[256,1024]{1,0:T(8,128)(2,1)}, u32[]{:S(2)}, u32[]{:S(2)}) collective-permute-start(bf16[256,1024]{1,0:T(8,128)(2,1)} %get-tuple-element.289), channel_id=1, source_target_pairs={{0,4},{4,0},{1,5},{5,1},{2,6},{6,2},{3,7},{7,3},{8,12},{12,8},{9,1... | collective-permute-start | bytes 1572872 | tf_op jit(solution)/shard_map/ppermute | solution.py:1433
  88.1 19.8 %copy-start.15 = (bf16[1280,512]{0,1:T(8,128)(2,1)}, bf16[1280,512]{0,1:T(8,128)(2,1)S(1)}, u32[]{:S(2)}) copy-start(bf16[1280,512]{0,1:T(8,128)(2,1)S(1)} %convolution_convert_fusion.2) | copy-start | bytes 3932164
  99.6 95.7 %collective-permute-start.2 = (bf16[3,1,88,1024]{3,2,1,0:T(8,128)(2,1)}, bf16[3,1,88,1024]{3,2,1,0:T(8,128)(2,1)}, u32[]{:S(2)}, u32[]{:S(2)}) collective-permute-start(bf16[3,1,88,1024]{3,2,1,0:T(8,128)(2,1)} %get-tuple-element.283), channel_id=1, source_target_pairs={{0,4},{4,0},{1,5},{5,1},{2,6},{6,2},{3,7},{7,3},{8,12},{12,8},{9,1... | collective-permute-start | bytes 1622024 | tf_op jit(solution)/shard_map/ppermute | solution.py:1433
  114.8 47.6 %copy-start.13 = (bf16[320,1024]{1,0:T(8,128)(2,1)S(1)}, bf16[320,1024]{1,0:T(8,128)(2,1)}, u32[]{:S(2)}) copy-start(bf16[320,1024]{1,0:T(8,128)(2,1)} %refs_0_) | copy-start | bytes 1966084
  163.9 505.1 %copy-start.3 = (f32[320,1024]{1,0:T(8,128)}, f32[320,1024]{1,0:T(8,128)S(1)}, u32[]{:S(2)}) copy-start(f32[320,1024]{1,0:T(8,128)S(1)} %convert_add_fusion) | copy-start | bytes 3932164
  366.8 115.0 %all-to-all-start = ((f32[16,1,320]{2,1,0:T(1,128)}), f32[16,1,320]{2,1,0:T(1,128)S(1)}, u32[]{:S(2)}, u32[]{:S(2)}) async-start(f32[16,1,320]{2,1,0:T(1,128)} %all_to_all.8), calls=%async_computation | async-start | bytes 49152 | tf_op jit(solution)/shard_map/all_to_all | solution.py:1532
  370.9 250.6 %all-gather.7.cloned.1.call-start = ((), (), s32[]{:S(2)}) async-start(), calls=%async_computation.2 | async-start | bytes 5406720 | tf_op jit(solution)/shard_map/all_gather | solution.py:1740
  375.9 119.4 %collective-permute-start.3 = (bf16[3,1,88,1024]{3,2,1,0:T(8,128)(2,1)}, bf16[3,1,88,1024]{3,2,1,0:T(8,128)(2,1)}, u32[]{:S(2)}, u32[]{:S(2)}) collective-permute-start(bf16[3,1,88,1024]{3,2,1,0:T(8,128)(2,1)} %get-tuple-element.278), channel_id=1, source_target_pairs={{0,4},{4,0},{1,5},{5,1},{2,6},{6,2},{3,7},{7,3},{8,12},{12,8},{9,1... | collective-permute-start | bytes 1622024 | tf_op jit(solution)/shard_map/ppermute | solution.py:1433
  497.8 332.9 %all-reduce.11.cloned.1.call-start = ((), (), s32[]{:S(2)}) async-start(), calls=%async_computation.3 | async-start | bytes 6881280 | tf_op jit(solution)/shard_map/psum | solution.py:1858
  505.6 25.9 %copy-start.48 = (bf16[1280,2,128]{0,2,1:T(8,128)(2,1)S(1)}, bf16[1280,2,128]{0,2,1:T(8,128)(2,1)}, u32[]{:S(2)}) copy-start(bf16[1280,2,128]{0,2,1:T(8,128)(2,1)} %copy-done.47) | copy-start | bytes 1966084
  540.0 77.1 %collective-permute-start.5 = (bf16[256,1024]{1,0:T(8,128)(2,1)}, bf16[256,1024]{1,0:T(8,128)(2,1)}, u32[]{:S(2)}, u32[]{:S(2)}) collective-permute-start(bf16[256,1024]{1,0:T(8,128)(2,1)} %get-tuple-element.285), channel_id=1, source_target_pairs={{0,4},{4,0},{1,5},{5,1},{2,6},{6,2},{3,7},{7,3},{8,12},{12,8},{9,1... | collective-permute-start | bytes 1572872 | tf_op jit(solution)/shard_map/ppermute | solution.py:1433
  584.0 35.7 %collective-permute-start.4 = (bf16[1024,384]{0,1:T(8,128)(2,1)S(1)}, bf16[1024,384]{0,1:T(8,128)(2,1)S(1)}, u32[]{:S(2)}, u32[]{:S(2)}) collective-permute-start(bf16[1024,384]{0,1:T(8,128)(2,1)S(1)} %get-tuple-element.274), channel_id=1, source_target_pairs={{0,4},{4,0},{1,5},{5,1},{2,6},{6,2},{3,7},{7,3},{8,12},{12,8},{9,1... | collective-permute-start | bytes 2359304 | tf_op jit(solution)/shard_map/ppermute | solution.py:1433
  631.3 29.8 %copy-start.14 = (bf16[320,1024]{1,0:T(8,128)(2,1)S(1)}, bf16[320,1024]{1,0:T(8,128)(2,1)}, u32[]{:S(2)}) copy-start(bf16[320,1024]{1,0:T(8,128)(2,1)} %refs_0_) | copy-start | bytes 1966084
  631.3 29.8 %copy-start.61 = (f32[1024]{0:T(1024)S(1)}, f32[1024]{0:T(1024)}, u32[]{:S(2)}) copy-start(f32[1024]{0:T(1024)} %dynamic_slice.105) | copy-start | bytes 12292
  631.3 29.8 %copy-start.62 = (f32[320]{0:T(512)S(1)}, f32[320]{0:T(512)}, u32[]{:S(2)}) copy-start(f32[320]{0:T(512)} %dynamic_slice.99) | copy-start | bytes 3844
  672.2 126.5 %copy-start.55 = (f32[16,1024]{1,0:T(8,128)S(1)}, f32[16,1024]{1,0:T(8,128)}, u32[]{:S(2)}) copy-start(f32[16,1024]{1,0:T(8,128)} %fusion.63) | copy-start | bytes 196612
  (65 other events, 294.4 us)
Sparse Core Ops, SparseCore 0:
  48.6 156.1 all-gather.4
  497.9 83.1 all-gather.6
  621.7 164.3 all-reduce.10

commit v5 on v4

--- a/solution.py
+++ b/solution.py
@@ -1037,6 +1037,15 @@
     )(value)
 
 
+class PairGather(Gather):
+    def area(self, where, row, col, layer, span=None):
+        rows, width = self.shape
+        start, size = (0, rows) if span is None else span
+        at = (row // 2 * self.layers + layer) * 2 + lax.rem(row, 2)
+        first = pl.multiple_of(at * rows + start, 16)
+        return where.at[pl.ds(first, size), pl.ds(pl.multiple_of(col * width, 128), width)]
+
+
 def nearest_first(layers, turn, layer):
     found = 0
     for here in range(layers):
@@ -1060,7 +1069,7 @@
     down_hbm,
     side_hbm,
     side_down_hbm,
-    rows_all,
+    own_rows_ref,
     slot_rows_ref,
     slot_grads_ref,
     hidden_ref,
@@ -1076,7 +1085,7 @@
     down_w,
     side_w,
     side_down,
-    both_rows,
+    held,
     side_hidden,
     d_side,
     weight_sem,
@@ -1085,7 +1094,7 @@
 ):
     bf16, f32 = jnp.bfloat16, jnp.float32
     me = Place(layers)
-    work = Gather(me, layers, False, src.shape, rows_all, sems)
+    work = PairGather(me, layers, False, src.shape, held, sems)
     own_expert = me.row * layers + me.layer
     block, half = src.shape
     width = 2 * half
@@ -1108,38 +1117,29 @@
         )
     ]
 
-    def load(which, core):
-        layer = nearest_first(layers, which // 2, me.layer)
-        far = lax.rem(which, 2)
-        x_place = me.row // 2 * (1 - far) + (1 - me.row // 2) * far
-        first = pl.multiple_of(((2 * x_place + core) * layers + layer) * block, 16)
-        slot = lax.rem(which, 2)
-        return pltpu.make_async_copy(
-            rows_all.at[pl.ds(first, block)],
-            both_rows.at[slot, pl.ds(core * block, block)],
-            rows_sem.at[slot, core],
-        )
-
-    def prepare(which):
-        for distance in range(1, layers):
-
-            @pl.when(which == distance - 1)
-            def _():
-                work.at_distance(distance, work.arrived)
-
+    def relay(early):
         for turn in range(layers):
             at = nearest_first(layers, turn, me.layer)
-
-            @pl.when(which == (max(1, 2 * turn) if turn != 1 else 3))
-            def _():
-                work.third(at)
-
-            if turn > 0:
-
-                @pl.when(which == (2 * turn - 1 if turn != 1 else 2))
+            if early and turn > 0:
+
+                @pl.when(step == max(1, 2 * turn - 2))
                 def _():
                     work.second(at)
 
+            if not early:
+
+                @pl.when(step == (0, 2)[turn] if turn < 2 else step == 2 * turn - 1)
+                def _():
+                    work.third(at)
+
+        for distance in range(2, layers):
+            if not early:
+
+                @pl.when(step == distance - 2)
+                def _():
+                    work.at_distance(distance, work.arrived)
+
+    def prepare(which):
         layer = nearest_first(layers, which // 2, me.layer)
 
         @pl.when(lax.rem(which, 2) == 0)
@@ -1152,12 +1152,9 @@
             work.from_core(1, layer).wait_recv()
             work.from_core(3, layer).wait_recv()
 
-        for core in range(2):
-            load(which, core).start()
-
     @pl.when(step == 0)
     def _():
-        own = pltpu.make_async_copy(src, work.piece(0, me.layer), rows_sem.at[0, 0])
+        own = pltpu.make_async_copy(src, work.piece(0, me.layer), rows_sem)
         own.start()
         for copy in weight_loads:
             copy.start()
@@ -1167,7 +1164,10 @@
         for copy in weight_loads:
             copy.wait()
 
-    rows = both_rows.at[lax.rem(step, 2)]
+    far = lax.rem(step, 2)
+    x_place = me.row // 2 * (1 - far) + (1 - me.row // 2) * far
+    pair = x_place * layers + nearest_first(layers, step // 2, me.layer)
+    rows = held.at[pl.ds(pl.multiple_of(pair * 2 * block, 16), 2 * block)]
 
     def spot(b):
         core, j = b // per_block, b % per_block
@@ -1188,13 +1188,15 @@
         dot_nt(side_grads[c], side_down[:, c * half : (c + 1) * half]) for c in range(2)
     )
 
+    relay(True)
+
     @pl.when(step == 0)
     def _():
         work.second(me.layer)
+        if layers > 1:
+            work.at_distance(1, work.arrived)
         prepare(step)
 
-    for core in range(2):
-        load(step, core).wait()
 
     side = dot_nt(rows[...], side_w[...])
     side_gate, side_up = side[:, :lanes], side[:, lanes:]
@@ -1250,6 +1252,8 @@
     d_gate = (d_hidden * up_pre * sigmoid * (1.0 + gate_pre * (1.0 - sigmoid))).astype(bf16)
     keep(d_gate_ref, d_gate)
 
+    relay(False)
+
     @pl.when(step + 1 < steps)
     def _():
         prepare(step + 1)
@@ -1282,7 +1286,12 @@
 
     @pl.when(step == steps - 1)
     def _():
+        at = (me.row // 2 * layers + me.layer) * 2 + me.core
+        mine = held.at[pl.ds(pl.multiple_of(at * block, 16), block)]
+        keep_rows = pltpu.make_async_copy(mine, own_rows_ref, rows_sem)
+        keep_rows.start()
         work.finish()
+        keep_rows.wait()
 
 
 def expert_pass(layers, few, slots, units, experts, rows_own, grads, pick, spread, words, weights, side_w, side_down):
@@ -1330,7 +1339,7 @@
             pl.BlockSpec((lanes, width), lambda i: (0, 0)),
         ],
         out_shape=[
-            jax.ShapeDtypeStruct((tokens, width), jnp.bfloat16),
+            jax.ShapeDtypeStruct((block, width), jnp.bfloat16),
             shape(each, width),
             shape(each, width),
             shape(each, hidden),
@@ -1344,11 +1353,11 @@
         ],
         scratch_shapes=[
             *(pltpu.VMEM(w.shape, jnp.bfloat16) for w in (*weights, side_w, side_down)),
-            pltpu.VMEM((2, 2 * block, width), jnp.bfloat16),
+            pltpu.VMEM((tokens, width), jnp.bfloat16),
             pltpu.VMEM((2 * block, lanes), jnp.bfloat16),
             pltpu.VMEM((2 * block, 2 * lanes), jnp.bfloat16),
             pltpu.SemaphoreType.DMA((5,)),
-            pltpu.SemaphoreType.DMA((2, 2)),
+            pltpu.SemaphoreType.DMA,
             *Gather.semaphores(layers),
         ],
         compiler_params=pltpu.CompilerParams(
@@ -1483,7 +1492,7 @@
     grads_all = lax.all_gather(grads_own, ("row", "exp", "col"), axis=0)
     grads_all = grads_all.reshape(experts, 2, block, half_width)
     (
-        normed_all,
+        own_normed,
         slot_rows,
         slot_grads,
         hidden,
@@ -1534,9 +1543,7 @@
         ),
         "col",
     ).T
-    own_probs = jax.nn.softmax(
-        dot_nn(lax.dynamic_slice_in_dim(normed_all, own_expert * block, block, 0), router), axis=1
-    )
+    own_probs = jax.nn.softmax(dot_nn(own_normed, router), axis=1)
     own_words = lax.dynamic_slice_in_dim(words, own_expert * block, block, 0)
     numbers = jnp.arange(experts, dtype=jnp.int32)
     picks = (

time: 869 us -> 850 us (0.978)
  Pallas kernels: 606 us -> 583 us
    pallas_call x1, Pallas kernels: 159 us -> 136 us  [expert_pass(): pl.pallas_call(functools.partial(expert_body, layers, units, experts), gr...]
    unnamed x163 -> x165, local copies, waits for them, and re-layouts: 25 us -> 24.9 us
  transfers between devices with their start and end apart: 10 -> 10, of which waited for: 1 -> 1; matrix products, arithmetic and copies ran while one was open for 19% -> 19% of each run, Pallas kernels for 48% -> 49%
where the time goes in v5:
time: 850 us; the launch traced here: 841 us
  Pallas kernels  583 us (69%)
  other arithmetic  71.7 us (8%)
  local copies, waits for them, and re-layouts  64.8 us (8%)
  matrix products  61.4 us (7%)
  blocking collectives  23 us (3%)
  between operations  15.3 us (2%)
  starting transfers between devices  15.2 us (2%)
    pallas_call x2, Pallas kernels, made_scatter(): pl.pallas_call(functools.partial(made_scatter_body, layers, parts, jobs),...  232 us
    pallas_call x1, Pallas kernels, expert_pass(): pl.pallas_call(functools.partial(expert_body, layers, units, experts), gr...  136 us
    pallas_call x3, Pallas kernels, scatter(): pl.pallas_call(functools.partial(scatter_body, layers, by_rows), out_shap...  91.4 us
    pallas_call x3, Pallas kernels, gather_several(): pl.pallas_call(functools.partial(gather_body, layers, by_rows), out_shape...  88 us
    pallas_call x2, Pallas kernels, small_sum(): pl.pallas_call(functools.partial(small_sum_body, layers), out_shape=jax.S...  35.3 us
    unnamed x165, local copies, waits for them, and re-layouts  24.9 us
  transfers between devices with their start and end apart: 10, of which 1 were waited for; matrix products, arithmetic and copies ran while one was open for 19% of the time, Pallas kernels for 49%

profile of v5, /device:TPU:0, one launch (start us, length us, event | category | flops | bytes accessed | tf_op | source)
XLA Modules:
  0.0 841.0 jit_solution(5170270570880126323)
XLA Ops:
  10.1 38.3 %shard_map.307 = (bf16[1280,2048]{1,0:T(8,128)(2,1)}, bf16[4608,256]{1,0:T(8,128)(2,1)}) custom-call(bf16[320,1024]{1,0:T(8,128)(2,1)} %refs_0_, bf16[576,256]{1,0:T(8,128)(2,1)} %bitcast.212), custom_call_target="tpu_custom_call" | custom-call | tf_op jit(solution)/shard_map/pallas_call | solution.py:297
  52.5 4.9 copy.158
  57.4 5.5 reshape.634
  90.9 5.6 fusion.55
  109.3 5.4 convolution_convert_fusion.src
  114.7 47.4 %shard_map.308 = f32[320,1024]{1,0:T(8,128)} custom-call(bf16[1280,2048]{1,0:T(8,128)(2,1)} %convolution_convert_fusion.src), custom_call_target="tpu_custom_call" | custom-call | tf_op jit(solution)/shard_map/pallas_call | solution.py:532
  163.7 14.2 %shard_map.309 = f32[16,512]{1,0:T(8,128)S(1)} custom-call(f32[16,256]{1,0:T(8,128)S(1)} %broadcast_select_fusion.src), custom_call_target="tpu_custom_call" | custom-call | tf_op jit(solution)/shard_map/pallas_call | solution.py:1015
  178.4 4.9 psum.56
  198.2 6.5 all-gather.5.cloned.1.call-done
  204.7 136.2 %shard_map.310 = (bf16[320,2048]{1,0:T(8,128)(2,1)}, bf16[2,2,4,192,2048]{4,3,2,1,0:T(8,128)(2,1)}, bf16[2,2,4,192,2048]{4,3,2,1,0:T(8,128)(2,1)}, bf16[2,2,4,19...) custom-call(bf16[320,1024]{1,0:T(8,128)(2,1)} %multiply_convert_fusi, ...), custom_call_target="tpu_custom_call" | custom-call | tf_op jit(solution)/shard_map/pallas_call | solution.py:1317
  344.3 9.4 %all-to-all-start = ((f32[16,1,320]{2,1,0:T(1,128)}), f32[16,1,320]{2,1,0:T(1,128)S(1)}, u32[]{:S(2)}, u32[]{:S(2)}) async-start(f32[16,1,320]{2,1,0:T(1,128)} %all_to_all.8), calls=%async_computation | async-start | bytes 49152 | tf_op jit(solution)/shard_map/all_to_all | solution.py:1541
  358.0 105.4 %shard_map.311 = f32[320,1024]{1,0:T(8,128)} custom-call(bf16[2,2,4,192,704]{4,3,2,1,0:T(8,128)(2,1)} %get-tuple-element.141.refs_0_, bf16[2,2,4,192,704]{4,3,2,1,0:T(8,128)(2,1)} %get-tuple-element.142.refs_1_, bf16[704,2048]{1,0:T(8,128)(2,1)} %bitcast.182, bf16[704,2048]{1,0:T(8,128)(2,1)} %bitcast.184, ...), custom_call_target="tpu_custom_call" | custom-call | tf_op jit(solution)/shard_map/pallas_call | solution.py:924
  463.4 7.7 psum.57
  479.8 5.1 psum.58
  487.2 25.8 %shard_map.312 = bf16[1280,2048]{1,0:T(8,128)(2,1)} custom-call(bf16[320,1024]{1,0:T(8,128)(2,1)} %fusion.88.refs_0_), custom_call_target="tpu_custom_call" | custom-call | tf_op jit(solution)/shard_map/pallas_call | solution.py:297
  543.9 14.2 %shard_map.313 = f32[160,576]{1,0:T(8,128)} custom-call(bf16[1280,576]{1,0:T(8,128)(2,1)} %pad_maximum_fusion.src), custom_call_target="tpu_custom_call" | custom-call | tf_op jit(solution)/shard_map/pallas_call | solution.py:532
  569.5 23.9 %shard_map.314 = bf16[1280,576]{1,0:T(8,128)(2,1)} custom-call(bf16[160,576]{1,0:T(8,128)(2,1)} %pad_maximum_fusion.15.refs_0_), custom_call_target="tpu_custom_call" | custom-call | tf_op jit(solution)/shard_map/pallas_call | solution.py:297
  612.8 29.7 %shard_map.315 = f32[320,1024]{1,0:T(8,128)} custom-call(bf16[1280,2048]{1,0:T(8,128)(2,1)} %convert_element_type.191.src), custom_call_target="tpu_custom_call" | custom-call | tf_op jit(solution)/shard_map/pallas_call | solution.py:532
  644.3 5.3 psum.59
  653.5 126.7 %shard_map.316 = (f32[320,1024]{1,0:T(8,128)}, f32[704,2048]{1,0:T(8,128)}, f32[704,2048]{1,0:T(8,128)}, f32[704,2048]{1,0:T(8,128)}) custom-call(bf16[2,2,4,192,704]{4,3,2,1,0:T(8,128)(2,1)} %get-tuple-element.151.refs_0_, bf16[704,2048]{1,0:T(8,128)(2,1)} %bitcast.186, bf16[2,2,4,2,160,96]{5,4,3,2,1,0:T(8,128)(2,1)} %fusion.11.spread_ref.refs_4_.refs_2_, ...), custom_call_target="tpu_custom_call" | custom-call | tf_op jit(solution)/shard_map/pallas_call | solution.py:924
  780.3 21.1 %shard_map.317 = f32[24,2048]{1,0:T(8,128)S(1)} custom-call(f32[24,1024]{1,0:T(8,128)S(1)} %select_maximum_fusion.src), custom_call_target="tpu_custom_call" | custom-call | tf_op jit(solution)/shard_map/pallas_call | solution.py:1015
  805.9 6.1 fusion.89
  819.7 6.0 copy.169
  825.8 6.0 copy.170
  (326 shorter events, 164.3 us)
Async XLA Ops:
  7.2 89.7 %copy-start = (bf16[1024,704]{0,1:T(8,128)(2,1)S(1)}, bf16[1024,704]{0,1:T(8,128)(2,1)}, u32[]{:S(2)}) copy-start(bf16[1024,704]{0,1:T(8,128)(2,1)} %param.40) | copy-start | bytes 4325380
  7.2 197.5 %all-gather.5.cloned.1.call-start = ((), (), s32[]{:S(2)}) async-start(), calls=%async_computation.1 | async-start | bytes 21626880 | tf_op jit(solution)/shard_map/all_gather | solution.py:1492
  7.3 42.4 %copy-start.47 = (bf16[512,1024]{1,0:T(8,128)(2,1)S(1)}, bf16[512,1024]{1,0:T(8,128)(2,1)}, u32[]{:S(2)}) copy-start(bf16[512,1024]{1,0:T(8,128)(2,1)} %param.38) | copy-start | bytes 3145732
  10.1 41.5 %copy-start.73 = (s32[1,3]{1,0:T(1,128)S(1)}, s32[1,3]{1,0:T(1,128)}, u32[]{:S(2)}) copy-start(s32[1,3]{1,0:T(1,128)} %param.31) | copy-start | bytes 40
  10.1 41.7 %copy-start.71 = (s32[1,160,6]{1,0,2:T(1,128)S(1)}, s32[1,160,6]{1,0,2:T(1,128)}, u32[]{:S(2)}) copy-start(s32[1,160,6]{1,0,2:T(1,128)} %param.32) | copy-start | bytes 11524
  10.1 41.8 %copy-start.72 = (f32[2048]{0:T(1024)S(1)}, f32[2048]{0:T(1024)}, u32[]{:S(2)}) copy-start(f32[2048]{0:T(1024)} %param.39) | copy-start | bytes 24580
  10.1 41.8 %copy-start.66 = (f32[2048]{0:T(1024)S(1)}, f32[2048]{0:T(1024)}, u32[]{:S(2)}) copy-start(f32[2048]{0:T(1024)} %param.33) | copy-start | bytes 24580
  48.5 42.4 %collective-permute-start = (bf16[1024,384]{1,0:T(8,128)(2,1)}, bf16[1024,384]{1,0:T(8,128)(2,1)}, u32[]{:S(2)}, u32[]{:S(2)}) collective-permute-start(bf16[1024,384]{1,0:T(8,128)(2,1)} %get-tuple-element.130), channel_id=1, source_target_pairs={{0,4},{4,0},{1,5},{5,1},{2,6},{6,2},{3,7},{7,3},{8,12},{12,8},{9,1... | collective-permute-start | bytes 2359304 | tf_op jit(solution)/shard_map/ppermute | solution.py:1442
  50.6 58.7 %collective-permute-start.1 = (bf16[256,1024]{1,0:T(8,128)(2,1)}, bf16[256,1024]{1,0:T(8,128)(2,1)}, u32[]{:S(2)}, u32[]{:S(2)}) collective-permute-start(bf16[256,1024]{1,0:T(8,128)(2,1)} %get-tuple-element.289), channel_id=1, source_target_pairs={{0,4},{4,0},{1,5},{5,1},{2,6},{6,2},{3,7},{7,3},{8,12},{12,8},{9,1... | collective-permute-start | bytes 1572872 | tf_op jit(solution)/shard_map/ppermute | solution.py:1442
  88.2 19.7 %copy-start.15 = (bf16[1280,512]{0,1:T(8,128)(2,1)}, bf16[1280,512]{0,1:T(8,128)(2,1)S(1)}, u32[]{:S(2)}) copy-start(bf16[1280,512]{0,1:T(8,128)(2,1)S(1)} %convolution_convert_fusion.2) | copy-start | bytes 3932164
  99.6 94.8 %collective-permute-start.2 = (bf16[3,1,88,1024]{3,2,1,0:T(8,128)(2,1)}, bf16[3,1,88,1024]{3,2,1,0:T(8,128)(2,1)}, u32[]{:S(2)}, u32[]{:S(2)}) collective-permute-start(bf16[3,1,88,1024]{3,2,1,0:T(8,128)(2,1)} %get-tuple-element.283), channel_id=1, source_target_pairs={{0,4},{4,0},{1,5},{5,1},{2,6},{6,2},{3,7},{7,3},{8,12},{12,8},{9,1... | collective-permute-start | bytes 1622024 | tf_op jit(solution)/shard_map/ppermute | solution.py:1442
  114.7 47.5 %copy-start.13 = (bf16[320,1024]{1,0:T(8,128)(2,1)S(1)}, bf16[320,1024]{1,0:T(8,128)(2,1)}, u32[]{:S(2)}) copy-start(bf16[320,1024]{1,0:T(8,128)(2,1)} %refs_0_) | copy-start | bytes 1966084
  163.7 486.7 %copy-start.3 = (f32[320,1024]{1,0:T(8,128)}, f32[320,1024]{1,0:T(8,128)S(1)}, u32[]{:S(2)}) copy-start(f32[320,1024]{1,0:T(8,128)S(1)} %convert_add_fusion) | copy-start | bytes 3932164
  344.3 119.1 %all-to-all-start = ((f32[16,1,320]{2,1,0:T(1,128)}), f32[16,1,320]{2,1,0:T(1,128)S(1)}, u32[]{:S(2)}, u32[]{:S(2)}) async-start(f32[16,1,320]{2,1,0:T(1,128)} %all_to_all.8), calls=%async_computation | async-start | bytes 49152 | tf_op jit(solution)/shard_map/all_to_all | solution.py:1541
  353.7 249.3 %all-gather.7.cloned.1.call-start = ((), (), s32[]{:S(2)}) async-start(), calls=%async_computation.2 | async-start | bytes 5406720 | tf_op jit(solution)/shard_map/all_gather | solution.py:1747
  357.0 120.0 %collective-permute-start.3 = (bf16[3,1,88,1024]{3,2,1,0:T(8,128)(2,1)}, bf16[3,1,88,1024]{3,2,1,0:T(8,128)(2,1)}, u32[]{:S(2)}, u32[]{:S(2)}) collective-permute-start(bf16[3,1,88,1024]{3,2,1,0:T(8,128)(2,1)} %get-tuple-element.278), channel_id=1, source_target_pairs={{0,4},{4,0},{1,5},{5,1},{2,6},{6,2},{3,7},{7,3},{8,12},{12,8},{9,1... | collective-permute-start | bytes 1622024 | tf_op jit(solution)/shard_map/ppermute | solution.py:1442
  479.4 332.6 %all-reduce.11.cloned.1.call-start = ((), (), s32[]{:S(2)}) async-start(), calls=%async_computation.3 | async-start | bytes 6881280 | tf_op jit(solution)/shard_map/psum | solution.py:1865
  487.2 25.8 %copy-start.49 = (bf16[1280,2,128]{0,2,1:T(8,128)(2,1)S(1)}, bf16[1280,2,128]{0,2,1:T(8,128)(2,1)}, u32[]{:S(2)}) copy-start(bf16[1280,2,128]{0,2,1:T(8,128)(2,1)} %copy-done.48) | copy-start | bytes 1966084
  521.5 77.1 %collective-permute-start.5 = (bf16[256,1024]{1,0:T(8,128)(2,1)}, bf16[256,1024]{1,0:T(8,128)(2,1)}, u32[]{:S(2)}, u32[]{:S(2)}) collective-permute-start(bf16[256,1024]{1,0:T(8,128)(2,1)} %get-tuple-element.285), channel_id=1, source_target_pairs={{0,4},{4,0},{1,5},{5,1},{2,6},{6,2},{3,7},{7,3},{8,12},{12,8},{9,1... | collective-permute-start | bytes 1572872 | tf_op jit(solution)/shard_map/ppermute | solution.py:1442
  565.5 35.7 %collective-permute-start.4 = (bf16[1024,384]{0,1:T(8,128)(2,1)S(1)}, bf16[1024,384]{0,1:T(8,128)(2,1)S(1)}, u32[]{:S(2)}, u32[]{:S(2)}) collective-permute-start(bf16[1024,384]{0,1:T(8,128)(2,1)S(1)} %get-tuple-element.274), channel_id=1, source_target_pairs={{0,4},{4,0},{1,5},{5,1},{2,6},{6,2},{3,7},{7,3},{8,12},{12,8},{9,1... | collective-permute-start | bytes 2359304 | tf_op jit(solution)/shard_map/ppermute | solution.py:1442
  612.8 29.7 %copy-start.14 = (bf16[320,1024]{1,0:T(8,128)(2,1)S(1)}, bf16[320,1024]{1,0:T(8,128)(2,1)}, u32[]{:S(2)}) copy-start(bf16[320,1024]{1,0:T(8,128)(2,1)} %refs_0_) | copy-start | bytes 1966084
  612.8 29.7 %copy-start.62 = (f32[1024]{0:T(1024)S(1)}, f32[1024]{0:T(1024)}, u32[]{:S(2)}) copy-start(f32[1024]{0:T(1024)} %dynamic_slice.101) | copy-start | bytes 12292
  612.8 29.7 %copy-start.63 = (f32[320]{0:T(512)S(1)}, f32[320]{0:T(512)}, u32[]{:S(2)}) copy-start(f32[320]{0:T(512)} %dynamic_slice.95) | copy-start | bytes 3844
  653.5 126.7 %copy-start.56 = (f32[16,1024]{1,0:T(8,128)S(1)}, f32[16,1024]{1,0:T(8,128)}, u32[]{:S(2)}) copy-start(f32[16,1024]{1,0:T(8,128)} %fusion.61) | copy-start | bytes 196612
  (66 other events, 305.7 us)
Sparse Core Ops, SparseCore 0:
  48.6 156.0 all-gather.4
  479.5 83.0 all-gather.6
  603.2 164.1 all-reduce.10

commit v6 on v5

--- a/solution.py
+++ b/solution.py
@@ -69,6 +69,9 @@
 def piece_of(where, layers, shape, by_rows, row, col, layer, span=None):
     rows, width = shape
     start, size = (0, rows) if span is None else span
+    if by_rows == "lanes":
+        first = pl.multiple_of((col * 4 + row) * width, 128)
+        return where.at[pl.ds(start, size), pl.ds(first, width)]
     if by_rows:
         first = pl.multiple_of((row * 2 + col) * rows + start, 16)
         return where.at[pl.ds(first, size)]
@@ -287,7 +290,10 @@
     shapes, scratch = [], []
     for value, rows_only in zip(values, by_rows):
         rows, width = value.shape
-        shapes.append((8 * rows, width) if rows_only else (4 * layers * rows, 2 * width))
+        if rows_only == "lanes":
+            shapes.append((rows, 8 * width))
+        else:
+            shapes.append((8 * rows, width) if rows_only else (4 * layers * rows, 2 * width))
         scratch += [
             pltpu.VMEM(shapes[-1], value.dtype),
             dma((2, 4, layers)),
@@ -1623,10 +1629,9 @@
     seq_ids, places = sequence_layout(lengths[0], group)
     cosine, sine = rotary_tables(places)
 
-    group_input, w_latent_all = gather_several((layer_input, w_latent[0].T), 1, 10, (False, True))
-    latent_width, slab = w_latent.shape[2], w_latent.shape[1]
-    w_latent_all = w_latent_all.reshape(rows_n, cols_n, latent_width, slab)
-    w_latent_all = w_latent_all.transpose(2, 1, 0, 3).reshape(latent_width, width)
+    group_input, w_latent_all = gather_several(
+        (layer_input, w_latent[0].T), 1, 10, (False, "lanes")
+    )
     group_input, w_out, cotangent = lax.optimization_barrier((group_input, w_out, cotangent))
     w_out_own = trade(w_out, 0, 1)
     group_input = group_input.astype(jnp.float32)

time: 850 us -> 838 us (0.986)
  waiting for transfers between devices: 6.58 us -> 17.7 us
  local copies, waits for them, and re-layouts: 64.8 us -> 54.9 us
  Pallas kernels: 583 us -> 574 us
    all_gather x1, waiting for transfers between devices: 6.51 us -> 17.7 us  [routed_and_shared(): grads_all = lax.all_gather(grads_own, ('row', 'exp', 'col'), axis=0)]
    reshape x2 -> x0, local copies, waits for them, and re-layouts: 10.3 us -> none  [the longest x1 5.45 us: per_device(): w_latent_all.transpose(2, 1, 0, 3).reshape(latent_width, width)]
    pallas_call x3, Pallas kernels: 91.4 us -> 81.5 us  [scatter(): pl.pallas_call(functools.partial(scatter_body, layers, by_rows), out_shap...]
    unnamed x165 -> x167, local copies, waits for them, and re-layouts: 24.9 us -> 25.4 us
  transfers between devices with their start and end apart: 10 -> 10, of which waited for: 1 -> 1; matrix products, arithmetic and copies ran while one was open for 19% -> 17% of each run, Pallas kernels for 49% -> 48%
where the time goes in v6:
time: 838 us; the launch traced here: 831 us
  Pallas kernels  574 us (68%)
  other arithmetic  68.7 us (8%)
  matrix products  61.4 us (7%)
  local copies, waits for them, and re-layouts  54.9 us (7%)
  blocking collectives  23.4 us (3%)
  waiting for transfers between devices  17.7 us (2%)
  starting transfers between devices  15.9 us (2%)
  between operations  15.3 us (2%)
    pallas_call x2, Pallas kernels, made_scatter(): pl.pallas_call(functools.partial(made_scatter_body, layers, parts, jobs),...  231 us
    pallas_call x1, Pallas kernels, expert_pass(): pl.pallas_call(functools.partial(expert_body, layers, units, experts), gr...  136 us
    pallas_call x3, Pallas kernels, gather_several(): pl.pallas_call(functools.partial(gather_body, layers, by_rows), out_shape...  87.9 us
    pallas_call x3, Pallas kernels, scatter(): pl.pallas_call(functools.partial(scatter_body, layers, by_rows), out_shap...  81.5 us
    pallas_call x2, Pallas kernels, small_sum(): pl.pallas_call(functools.partial(small_sum_body, layers), out_shape=jax.S...  36.8 us
    unnamed x167, local copies, waits for them, and re-layouts  25.4 us
    all_gather x1, waiting for transfers between devices, routed_and_shared(): grads_all = lax.all_gather(grads_own, ('row', 'exp', 'col'), axis=0)  17.7 us
  transfers between devices with their start and end apart: 10, of which 1 were waited for; matrix products, arithmetic and copies ran while one was open for 17% of the time, Pallas kernels for 48%

profile of v6, /device:TPU:0, one launch (start us, length us, event | category | flops | bytes accessed | tf_op | source)
XLA Modules:
  0.0 831.2 jit_solution(6799964789483383795)
XLA Ops:
  10.1 38.4 %shard_map.307 = (bf16[1280,2048]{1,0:T(8,128)(2,1)}, bf16[576,2048]{1,0:T(8,128)(2,1)}) custom-call(bf16[320,1024]{1,0:T(8,128)(2,1)} %refs_0_, bf16[576,256]{1,0:T(8,128)(2,1)} %bitcast.206), custom_call_target="tpu_custom_call" | custom-call | tf_op jit(solution)/shard_map/pallas_call | solution.py:303
  59.0 4.3 fusion.96
  78.2 5.6 fusion.55
  97.0 5.4 convolution_convert_fusion.src
  102.4 37.6 %shard_map.308 = f32[320,1024]{1,0:T(8,128)} custom-call(bf16[1280,2048]{1,0:T(8,128)(2,1)} %convolution_convert_fusion.src), custom_call_target="tpu_custom_call" | custom-call | tf_op jit(solution)/shard_map/pallas_call | solution.py:538
  141.6 15.2 %shard_map.309 = f32[16,512]{1,0:T(8,128)S(1)} custom-call(f32[16,256]{1,0:T(8,128)S(1)} %broadcast_select_fusion.src), custom_call_target="tpu_custom_call" | custom-call | tf_op jit(solution)/shard_map/pallas_call | solution.py:1021
  157.2 5.0 psum.56
  177.0 17.7 %all-gather.5.cloned.1.call-done = bf16[10240,1024]{1,0:T(8,128)(2,1)} async-done(((bf16[320,1024]{1,0:T(8,128)(2,1)}), bf16[10240,1024]{1,0:T(8,128)(2,1)}) %all-gather.5.cloned.1.call-update) | async-done | bytes 20971536 | tf_op jit(solution)/shard_map/all_gather | solution.py:1498
  194.7 136.5 %shard_map.310 = (bf16[320,2048]{1,0:T(8,128)(2,1)}, bf16[2,2,4,192,2048]{4,3,2,1,0:T(8,128)(2,1)}, bf16[2,2,4,192,2048]{4,3,2,1,0:T(8,128)(2,1)}, bf16[2,2,4,19...) custom-call(bf16[320,1024]{1,0:T(8,128)(2,1)} %multiply_convert_fusi, ...), custom_call_target="tpu_custom_call" | custom-call | tf_op jit(solution)/shard_map/pallas_call | solution.py:1323
  334.6 9.1 %all-to-all-start = ((f32[16,1,320]{2,1,0:T(1,128)}), f32[16,1,320]{2,1,0:T(1,128)S(1)}, u32[]{:S(2)}, u32[]{:S(2)}) async-start(f32[16,1,320]{2,1,0:T(1,128)} %all_to_all.8), calls=%async_computation | async-start | bytes 49152 | tf_op jit(solution)/shard_map/all_to_all | solution.py:1547
  348.2 105.2 %shard_map.311 = f32[320,1024]{1,0:T(8,128)} custom-call(bf16[2,2,4,192,704]{4,3,2,1,0:T(8,128)(2,1)} %get-tuple-element.141.refs_0_, bf16[2,2,4,192,704]{4,3,2,1,0:T(8,128)(2,1)} %get-tuple-element.142.refs_1_, bf16[704,2048]{1,0:T(8,128)(2,1)} %bitcast.178, bf16[704,2048]{1,0:T(8,128)(2,1)} %bitcast.180, ...), custom_call_target="tpu_custom_call" | custom-call | tf_op jit(solution)/shard_map/pallas_call | solution.py:930
  453.4 7.9 psum.57
  470.0 5.1 psum.58
  477.4 25.6 %shard_map.312 = bf16[1280,2048]{1,0:T(8,128)(2,1)} custom-call(bf16[320,1024]{1,0:T(8,128)(2,1)} %fusion.88.refs_0_), custom_call_target="tpu_custom_call" | custom-call | tf_op jit(solution)/shard_map/pallas_call | solution.py:303
  534.0 14.1 %shard_map.313 = f32[160,576]{1,0:T(8,128)} custom-call(bf16[1280,576]{1,0:T(8,128)(2,1)} %pad_maximum_fusion.src), custom_call_target="tpu_custom_call" | custom-call | tf_op jit(solution)/shard_map/pallas_call | solution.py:538
  559.6 23.9 %shard_map.314 = bf16[1280,576]{1,0:T(8,128)(2,1)} custom-call(bf16[160,576]{1,0:T(8,128)(2,1)} %pad_maximum_fusion.15.refs_0_), custom_call_target="tpu_custom_call" | custom-call | tf_op jit(solution)/shard_map/pallas_call | solution.py:303
  594.3 4.7 fusion.54
  603.0 29.8 %shard_map.315 = f32[320,1024]{1,0:T(8,128)} custom-call(bf16[1280,2048]{1,0:T(8,128)(2,1)} %convert_element_type.191.src), custom_call_target="tpu_custom_call" | custom-call | tf_op jit(solution)/shard_map/pallas_call | solution.py:538
  634.6 5.3 psum.59
  643.8 126.0 %shard_map.316 = (f32[320,1024]{1,0:T(8,128)}, f32[704,2048]{1,0:T(8,128)}, f32[704,2048]{1,0:T(8,128)}, f32[704,2048]{1,0:T(8,128)}) custom-call(bf16[2,2,4,192,704]{4,3,2,1,0:T(8,128)(2,1)} %get-tuple-element.151.refs_0_, bf16[704,2048]{1,0:T(8,128)(2,1)} %bitcast.182, bf16[2,2,4,2,160,96]{5,4,3,2,1,0:T(8,128)(2,1)} %fusion.11.spread_ref.refs_4_.refs_2_, ...), custom_call_target="tpu_custom_call" | custom-call | tf_op jit(solution)/shard_map/pallas_call | solution.py:930
  769.9 21.6 %shard_map.317 = f32[24,2048]{1,0:T(8,128)S(1)} custom-call(f32[24,1024]{1,0:T(8,128)S(1)} %select_maximum_fusion.src), custom_call_target="tpu_custom_call" | custom-call | tf_op jit(solution)/shard_map/pallas_call | solution.py:1021
  796.1 6.1 fusion.89
  809.9 6.0 copy.163
  815.9 6.0 copy.164
  (326 shorter events, 153.7 us)
Async XLA Ops:
  7.2 76.9 %copy-start = (bf16[1024,704]{0,1:T(8,128)(2,1)S(1)}, bf16[1024,704]{0,1:T(8,128)(2,1)}, u32[]{:S(2)}) copy-start(bf16[1024,704]{0,1:T(8,128)(2,1)} %param.40) | copy-start | bytes 4325380
  7.2 187.5 %all-gather.5.cloned.1.call-start = ((), (), s32[]{:S(2)}) async-start(), calls=%async_computation.1 | async-start | bytes 21626880 | tf_op jit(solution)/shard_map/all_gather | solution.py:1498
  7.3 42.4 %copy-start.47 = (bf16[512,1024]{1,0:T(8,128)(2,1)S(1)}, bf16[512,1024]{1,0:T(8,128)(2,1)}, u32[]{:S(2)}) copy-start(bf16[512,1024]{1,0:T(8,128)(2,1)} %param.38) | copy-start | bytes 3145732
  10.1 41.6 %copy-start.74 = (s32[1,3]{1,0:T(1,128)S(1)}, s32[1,3]{1,0:T(1,128)}, u32[]{:S(2)}) copy-start(s32[1,3]{1,0:T(1,128)} %param.31) | copy-start | bytes 40
  10.1 41.7 %copy-start.71 = (s32[1,160,6]{1,0,2:T(1,128)S(1)}, s32[1,160,6]{1,0,2:T(1,128)}, u32[]{:S(2)}) copy-start(s32[1,160,6]{1,0,2:T(1,128)} %param.32) | copy-start | bytes 11524
  10.1 41.8 %copy-start.72 = (f32[2048]{0:T(1024)S(1)}, f32[2048]{0:T(1024)}, u32[]{:S(2)}) copy-start(f32[2048]{0:T(1024)} %param.39) | copy-start | bytes 24580
  10.1 41.8 %copy-start.66 = (f32[2048]{0:T(1024)S(1)}, f32[2048]{0:T(1024)}, u32[]{:S(2)}) copy-start(f32[2048]{0:T(1024)} %param.33) | copy-start | bytes 24580
  48.6 29.7 %collective-permute-start = (bf16[1024,384]{1,0:T(8,128)(2,1)}, bf16[1024,384]{1,0:T(8,128)(2,1)}, u32[]{:S(2)}, u32[]{:S(2)}) collective-permute-start(bf16[1024,384]{1,0:T(8,128)(2,1)} %get-tuple-element.130), channel_id=1, source_target_pairs={{0,4},{4,0},{1,5},{5,1},{2,6},{6,2},{3,7},{7,3},{8,12},{12,8},{9,1... | collective-permute-start | bytes 2359304 | tf_op jit(solution)/shard_map/ppermute | solution.py:1448
  50.7 46.4 %collective-permute-start.1 = (bf16[256,1024]{1,0:T(8,128)(2,1)}, bf16[256,1024]{1,0:T(8,128)(2,1)}, u32[]{:S(2)}, u32[]{:S(2)}) collective-permute-start(bf16[256,1024]{1,0:T(8,128)(2,1)} %get-tuple-element.289), channel_id=1, source_target_pairs={{0,4},{4,0},{1,5},{5,1},{2,6},{6,2},{3,7},{7,3},{8,12},{12,8},{9,1... | collective-permute-start | bytes 1572872 | tf_op jit(solution)/shard_map/ppermute | solution.py:1448
  75.5 20.0 %copy-start.16 = (bf16[1280,512]{0,1:T(8,128)(2,1)}, bf16[1280,512]{0,1:T(8,128)(2,1)S(1)}, u32[]{:S(2)}) copy-start(bf16[1280,512]{0,1:T(8,128)(2,1)S(1)} %convolution_convert_fusion.2) | copy-start | bytes 3932164
  86.9 86.4 %collective-permute-start.2 = (bf16[3,1,88,1024]{3,2,1,0:T(8,128)(2,1)}, bf16[3,1,88,1024]{3,2,1,0:T(8,128)(2,1)}, u32[]{:S(2)}, u32[]{:S(2)}) collective-permute-start(bf16[3,1,88,1024]{3,2,1,0:T(8,128)(2,1)} %get-tuple-element.283), channel_id=1, source_target_pairs={{0,4},{4,0},{1,5},{5,1},{2,6},{6,2},{3,7},{7,3},{8,12},{12,8},{9,1... | collective-permute-start | bytes 1622024 | tf_op jit(solution)/shard_map/ppermute | solution.py:1448
  102.4 37.6 %copy-start.14 = (bf16[320,1024]{1,0:T(8,128)(2,1)S(1)}, bf16[320,1024]{1,0:T(8,128)(2,1)}, u32[]{:S(2)}) copy-start(bf16[320,1024]{1,0:T(8,128)(2,1)} %refs_0_) | copy-start | bytes 1966084
  141.6 499.1 %copy-start.3 = (f32[320,1024]{1,0:T(8,128)}, f32[320,1024]{1,0:T(8,128)S(1)}, u32[]{:S(2)}) copy-start(f32[320,1024]{1,0:T(8,128)S(1)} %convert_add_fusion) | copy-start | bytes 3932164
  334.6 118.8 %all-to-all-start = ((f32[16,1,320]{2,1,0:T(1,128)}), f32[16,1,320]{2,1,0:T(1,128)S(1)}, u32[]{:S(2)}, u32[]{:S(2)}) async-start(f32[16,1,320]{2,1,0:T(1,128)} %all_to_all.8), calls=%async_computation | async-start | bytes 49152 | tf_op jit(solution)/shard_map/all_to_all | solution.py:1547
  343.7 249.4 %all-gather.7.cloned.1.call-start = ((), (), s32[]{:S(2)}) async-start(), calls=%async_computation.2 | async-start | bytes 5406720 | tf_op jit(solution)/shard_map/all_gather | solution.py:1752
  347.0 120.2 %collective-permute-start.3 = (bf16[3,1,88,1024]{3,2,1,0:T(8,128)(2,1)}, bf16[3,1,88,1024]{3,2,1,0:T(8,128)(2,1)}, u32[]{:S(2)}, u32[]{:S(2)}) collective-permute-start(bf16[3,1,88,1024]{3,2,1,0:T(8,128)(2,1)} %get-tuple-element.278), channel_id=1, source_target_pairs={{0,4},{4,0},{1,5},{5,1},{2,6},{6,2},{3,7},{7,3},{8,12},{12,8},{9,1... | collective-permute-start | bytes 1622024 | tf_op jit(solution)/shard_map/ppermute | solution.py:1448
  469.6 332.6 %all-reduce.11.cloned.1.call-start = ((), (), s32[]{:S(2)}) async-start(), calls=%async_computation.3 | async-start | bytes 6881280 | tf_op jit(solution)/shard_map/psum | solution.py:1870
  477.4 25.6 %copy-start.49 = (bf16[1280,2,128]{0,2,1:T(8,128)(2,1)S(1)}, bf16[1280,2,128]{0,2,1:T(8,128)(2,1)}, u32[]{:S(2)}) copy-start(bf16[1280,2,128]{0,2,1:T(8,128)(2,1)} %copy-done.48) | copy-start | bytes 1966084
  511.5 77.2 %collective-permute-start.5 = (bf16[256,1024]{1,0:T(8,128)(2,1)}, bf16[256,1024]{1,0:T(8,128)(2,1)}, u32[]{:S(2)}, u32[]{:S(2)}) collective-permute-start(bf16[256,1024]{1,0:T(8,128)(2,1)} %get-tuple-element.285), channel_id=1, source_target_pairs={{0,4},{4,0},{1,5},{5,1},{2,6},{6,2},{3,7},{7,3},{8,12},{12,8},{9,1... | collective-permute-start | bytes 1572872 | tf_op jit(solution)/shard_map/ppermute | solution.py:1448
  555.5 35.9 %collective-permute-start.4 = (bf16[1024,384]{0,1:T(8,128)(2,1)S(1)}, bf16[1024,384]{0,1:T(8,128)(2,1)S(1)}, u32[]{:S(2)}, u32[]{:S(2)}) collective-permute-start(bf16[1024,384]{0,1:T(8,128)(2,1)S(1)} %get-tuple-element.274), channel_id=1, source_target_pairs={{0,4},{4,0},{1,5},{5,1},{2,6},{6,2},{3,7},{7,3},{8,12},{12,8},{9,1... | collective-permute-start | bytes 2359304 | tf_op jit(solution)/shard_map/ppermute | solution.py:1448
  603.0 29.8 %copy-start.15 = (bf16[320,1024]{1,0:T(8,128)(2,1)S(1)}, bf16[320,1024]{1,0:T(8,128)(2,1)}, u32[]{:S(2)}) copy-start(bf16[320,1024]{1,0:T(8,128)(2,1)} %refs_0_) | copy-start | bytes 1966084
  603.0 29.8 %copy-start.62 = (f32[1024]{0:T(1024)S(1)}, f32[1024]{0:T(1024)}, u32[]{:S(2)}) copy-start(f32[1024]{0:T(1024)} %dynamic_slice.101) | copy-start | bytes 12292
  603.0 29.9 %copy-start.63 = (f32[320]{0:T(512)S(1)}, f32[320]{0:T(512)}, u32[]{:S(2)}) copy-start(f32[320]{0:T(512)} %dynamic_slice.95) | copy-start | bytes 3844
  643.8 126.0 %copy-start.56 = (f32[16,1024]{1,0:T(8,128)S(1)}, f32[16,1024]{1,0:T(8,128)}, u32[]{:S(2)}) copy-start(f32[16,1024]{1,0:T(8,128)} %fusion.61) | copy-start | bytes 196612
  (67 other events, 305.2 us)
Sparse Core Ops, SparseCore 0:
  48.7 145.9 all-gather.4
  469.7 83.0 all-gather.6
  593.3 164.3 all-reduce.10
